TPU v7x, 128 devices: a whole 4x4x4 slice. The times are simulated.
128 devices in a mesh: seq: 16 (over z, x), kvh: 8 (over y, core).
Axes of the slice: x: 4, y: 4, z: 4, core: 2. Of those that a mesh axis runs over, the one named last changes fastest.
Arguments:
- queries: bfloat16 [2048, 8, 1024], P('seq', 'kvh'), may hold values from -140 to 140
- kv_cache: bfloat16 [8, 131072, 256], P('kvh', 'seq'), may hold values from -6 to 6
- block_list: int32 [32, 64], replicated, may hold values from 0 to 2047, as said below
- out_weight: bfloat16 [8, 1024, 8192], P('kvh'), may hold values from -0.09375 to 0.09375
Outputs:
- projected: float32 [2048, 8192], P('seq', 'kvh')
Inputs may be any that keep to these rules, and one draw needn't show every extreme that they name: `block_list`: each row names 64 different key blocks, none after its own query block's key block 2016 + row; it names that block and the 3 blocks before it; at most 16 of a row's blocks lie in one key group, and in every row exactly 16 lie in some key group other than the last.
All inputs are finite; a program needn't handle non-finite values.
Results may differ from a plain program's by a relative error of at most 0.0038.
Values may be sent and summed in bfloat16 or wider, within the bound.
No kernel may reach another device: no remote copies, remote signals or barrier semaphores. Data moves between devices by JAX's collectives and lax.ppermute only.
A program may use at most 128 MiB of HBM per device.

v0:
```python
import math

import jax
import jax.numpy as jnp
from jax import lax
from jax.sharding import PartitionSpec as P

BLK = 64
MOST = 16


def body(queries, kv_cache, block_list, out_weight):
    shard_count = lax.axis_size("seq")
    my_shard = lax.axis_index("seq")
    all_queries = lax.all_gather(queries, "seq", axis=0, tiled=True)
    head_dim = kv_cache.shape[2] // 2
    group_size = queries.shape[2] // head_dim
    query_total = all_queries.shape[0]
    local_len = kv_cache.shape[1]
    block_count = local_len // BLK
    qblock_count = query_total // BLK
    row_count = BLK * group_size
    first_pos = shard_count * local_len - query_total
    score_scale = 1.0 / math.sqrt(head_dim)
    cache_blocks = kv_cache[0].reshape(block_count, BLK, 2 * head_dim)
    owner_ids = block_list // block_count
    local_ids = block_list % block_count
    mine = owner_ids == my_shard
    ranks = jnp.cumsum(mine.astype(jnp.int32), axis=1) - 1
    slot_index = jnp.arange(MOST, dtype=jnp.int32)
    matched = mine[:, :, None] & (ranks[:, :, None] == slot_index[None, None, :])
    slot_ids = jnp.sum(jnp.where(matched, local_ids[:, :, None], 0), axis=1)
    slot_used = jnp.any(matched, axis=1)
    group_len = math.gcd(qblock_count, 8)
    group_total = qblock_count // group_len
    query_rows = all_queries.reshape(group_total, group_len, row_count, head_dim)
    slot_groups = slot_ids.reshape(group_total, group_len, MOST)
    used_groups = slot_used.reshape(group_total, group_len, MOST)
    block_numbers = jnp.arange(qblock_count, dtype=jnp.int32).reshape(group_total, group_len)

    def attend_group(inputs):
        rows_in, slots_in, used_in, numbers_in = inputs
        fetched = cache_blocks[slots_in].reshape(group_len, MOST * BLK, 2 * head_dim)
        key_part = fetched[:, :, :head_dim]
        value_part = fetched[:, :, head_dim:]
        scores = (
            jnp.einsum("grd,gkd->grk", rows_in, key_part, preferred_element_type=jnp.float32)
            * score_scale
        )
        query_pos = (
            first_pos
            + numbers_in[:, None] * BLK
            + jnp.arange(row_count, dtype=jnp.int32)[None, :] // group_size
        )
        key_pos = (my_shard * block_count + slots_in)[:, :, None] * BLK + jnp.arange(
            BLK, dtype=jnp.int32
        )[None, None, :]
        key_pos = key_pos.reshape(group_len, MOST * BLK)
        used_keys = jnp.repeat(used_in, BLK, axis=1)
        allowed = used_keys[:, None, :] & (key_pos[:, None, :] <= query_pos[:, :, None])
        masked = jnp.where(allowed, scores, -1e30)
        row_peak = jnp.max(masked, axis=2)
        weights = jnp.where(allowed, jnp.exp(masked - row_peak[:, :, None]), 0.0)
        totals = jnp.sum(weights, axis=2)
        partial_value = jnp.einsum(
            "grk,gkd->grd",
            weights.astype(jnp.bfloat16),
            value_part,
            preferred_element_type=jnp.float32,
        )
        return (partial_value, row_peak, totals)

    partial_value, row_peak, totals = lax.map(
        attend_group, (query_rows, slot_groups, used_groups, block_numbers)
    )
    numer_part = partial_value.reshape(query_total, group_size, head_dim)
    peak_part = row_peak.reshape(query_total, group_size)
    total_part = totals.reshape(query_total, group_size)
    own_rows = query_total // shard_count
    row_top = lax.pmax(peak_part, "seq")
    factors = jnp.exp(peak_part - row_top)
    scaled_numer = (numer_part * factors[:, :, None]).reshape(query_total, group_size * head_dim)
    scaled_total = total_part * factors
    own_numer, own_total = (
        lax.psum_scatter(scaled_numer, "seq", scatter_dimension=0, tiled=True),
        lax.psum_scatter(scaled_total, "seq", scatter_dimension=0, tiled=True),
    )
    own_numer = own_numer.reshape(own_rows, group_size, head_dim)
    attention = (
        (own_numer / own_total[:, :, None])
        .reshape(own_rows, group_size * head_dim)
        .astype(jnp.bfloat16)
    )
    head_terms = jnp.dot(attention, out_weight[0], preferred_element_type=jnp.float32)
    return lax.psum_scatter(head_terms, "kvh", scatter_dimension=1, tiled=True)


def solution(mesh):
    in_specs = (P("seq", "kvh", None), P("kvh", "seq", None), P(), P("kvh", None, None))
    out_specs = P("seq", "kvh")
    return jax.shard_map(body, mesh=mesh, in_specs=in_specs, out_specs=out_specs, check_vma=False)
```

profile of v0, /device:TPU:0, one launch (start us, length us, event | category | flops | bytes accessed | tf_op | source)
XLA Modules:
  0.0 481.3 jit_solution(2275992870258607145)
XLA Ops:
  6.5 0.7 all-gather.2.cloned.1.call-update
  7.3 0.7 fusion.33
  8.1 0.2 reduce_window_sum.11
  8.3 0.7 add_select_fusion.1
  9.0 0.6 fusion.28
  9.7 0.6 select_reduce_fusion
  10.3 53.4 %all-gather.2.cloned.1.call-done = bf16[2048,1,1024]{2,0,1:T(8,128)(2,1)} async-done(((bf16[128,1,1024]{2,0,1:T(8,128)(2,1)}), bf16[2048,1,1024]{2,0,1:T(8,128)(2,1)}) %all-gather.2.cloned.1.call-update) | async-done | bytes 4194320 | tf_op jit(solution)/shard_map/all_gather | solution.py:15
  63.7 7.3 %reshape.209 = bf16[4,8,512,128]{3,2,1,0:T(8,128)(2,1)} reshape(bf16[2048,1,1024]{2,0,1:T(8,128)(2,1)} %all-gather.2.cloned.1.call-done) | data formatting | bytes 8388608 | tf_op jit(solution)/shard_map/reshape | solution.py:36
  71.0 103.2 %while.16 = (s32[]{:T(128)}, f32[4,8,512,128]{3,2,1,0:T(8,128)}, f32[4,8,512]{2,1,0:T(8,128)S(1)}, f32[4,8,512]{2,1,0:T(8,128)S(1)}, pred[4,8,16]{2,1,0:T(8,128)...) while((s32[]{:T(128)}, f32[4,8,512,128]{3,2,1,0:T(8,128)}, ...), condition=%wide.region_6.7_spmd, body=%wide.region_3.6_spmd.sunk | while | flops 2227185152 | bytes 83376256 | solution.py:73
  71.1 0.1 add.160
  71.3 5.0 %gather_fusion = bf16[128,64,256]{2,1,0:T(8,128)(2,1)} fusion(bf16[128,64,256]{2,1,0:T(8,128)(2,1)} %get-tuple-element.268, s32[1024]{0:T(1024)S(1)} %pad_clamp_fusion.2), kind=kCustom, calls=%fused_computation.clone.1 | custom fusion | bytes 8389120 | tf_op jit(solution)/shard_map/while/body/eval_jaxpr/gather | solution.py:43
  76.4 0.1 and.118
  76.6 5.9 %fusion.43 = (f32[8,512]{1,0:T(8,128)S(1)}, f32[8,512,1024]{2,1,0:T(8,128)S(1)}) fusion(s32[8,512]{1,0:T(8,128)S(1)} %broadcast_add_fusion.5, s32[8,1024]{1,0:T(8,128)S(1)} %broadcast_add_fusion.6, pred[8,1024]{1,0:T(8,128)(4,1)S(1)} %and.118, bf16[8,1024,256]{2,1,0:T(8,128)(2,1)} %bitcast.58, bf16[4,8,512,128]{3,2,1,0:T(8,128)(2,1)} %get-tuple-element.267, ...), kind=kOutput, calls=%fused_computation.4.clone.1 | convolution fusion | flops 1094709248 | bytes 19997184 | tf_op jit(solution)/shard_map/while/body/eval_jaxpr/grd,gkd->grk/dot_general | solution.py:47
  82.6 6.6 %fusion.44 = f32[8,512]{1,0:T(8,128)S(1)} fusion(f32[8,512]{1,0:T(8,128)S(1)} %get-tuple-element.233, f32[8,512,1024]{2,1,0:T(8,128)S(1)} %get-tuple-element.234, s32[8,512]{1,0:T(8,128)S(1)} %broadcast_add_fusion.5, s32[8,1024]{1,0:T(8,128)S(1)} %broadcast_add_fusion.6, pred[8,1024]{1,0:T(8,128)(4,1)S(1)} %and.118), kind=kLoop, calls=%fused_computation.7.clone.1 | loop fusion | flops 29356032 | bytes 16867328 | tf_op jit(solution)/shard_map/while/body/eval_jaxpr/reduce_sum | solution.py:64
  89.2 7.5 %bitcast_dynamic-update-slice_fusion.5 = f32[4,8,512,128]{3,2,1,0:T(8,128)} fusion(f32[4,8,512,128]{3,2,1,0:T(8,128)} %get-tuple-element.249, s32[]{:T(128)} %get-tuple-element.248, bf16[8,1024,256]{2,1,0:T(8,128)(2,1)S(1)} %bitcast.59, f32[8,512]{1,0:T(8,128)S(1)} %get-tuple-element.233, f32[8,512,1024]{2,1,0:T(8,128)S(1)} %get-tuple-element.234, ...), kind=kOutput, calls=%fused_computation.11.clone.1 | convolution fusion | flops 1103101952 | bytes 21045760 | tf_op jit(solution)/shard_map/while/body/eval_jaxpr/grk,gkd->grd/dot_general | solution.py:65
  96.8 0.1 add.160
  97.1 5.0 %gather_fusion = bf16[128,64,256]{2,1,0:T(8,128)(2,1)} fusion(bf16[128,64,256]{2,1,0:T(8,128)(2,1)} %get-tuple-element.268, s32[1024]{0:T(1024)S(1)} %pad_clamp_fusion.2), kind=kCustom, calls=%fused_computation.clone.1 | custom fusion | bytes 8389120 | tf_op jit(solution)/shard_map/while/body/eval_jaxpr/gather | solution.py:43
  102.1 0.1 broadcast_in_dim.100
  102.2 0.1 and.118
  102.4 5.9 %fusion.43 = (f32[8,512]{1,0:T(8,128)S(1)}, f32[8,512,1024]{2,1,0:T(8,128)S(1)}) fusion(s32[8,512]{1,0:T(8,128)S(1)} %broadcast_add_fusion.5, s32[8,1024]{1,0:T(8,128)S(1)} %broadcast_add_fusion.6, pred[8,1024]{1,0:T(8,128)(4,1)S(1)} %and.118, bf16[8,1024,256]{2,1,0:T(8,128)(2,1)} %bitcast.58, bf16[4,8,512,128]{3,2,1,0:T(8,128)(2,1)} %get-tuple-element.267, ...), kind=kOutput, calls=%fused_computation.4.clone.1 | convolution fusion | flops 1094709248 | bytes 19997184 | tf_op jit(solution)/shard_map/while/body/eval_jaxpr/grd,gkd->grk/dot_general | solution.py:47
  108.3 6.6 %fusion.44 = f32[8,512]{1,0:T(8,128)S(1)} fusion(f32[8,512]{1,0:T(8,128)S(1)} %get-tuple-element.233, f32[8,512,1024]{2,1,0:T(8,128)S(1)} %get-tuple-element.234, s32[8,512]{1,0:T(8,128)S(1)} %broadcast_add_fusion.5, s32[8,1024]{1,0:T(8,128)S(1)} %broadcast_add_fusion.6, pred[8,1024]{1,0:T(8,128)(4,1)S(1)} %and.118), kind=kLoop, calls=%fused_computation.7.clone.1 | loop fusion | flops 29356032 | bytes 16867328 | tf_op jit(solution)/shard_map/while/body/eval_jaxpr/reduce_sum | solution.py:64
  115.0 7.5 %bitcast_dynamic-update-slice_fusion.5 = f32[4,8,512,128]{3,2,1,0:T(8,128)} fusion(f32[4,8,512,128]{3,2,1,0:T(8,128)} %get-tuple-element.249, s32[]{:T(128)} %get-tuple-element.248, bf16[8,1024,256]{2,1,0:T(8,128)(2,1)S(1)} %bitcast.59, f32[8,512]{1,0:T(8,128)S(1)} %get-tuple-element.233, f32[8,512,1024]{2,1,0:T(8,128)S(1)} %get-tuple-element.234, ...), kind=kOutput, calls=%fused_computation.11.clone.1 | convolution fusion | flops 1103101952 | bytes 21045760 | tf_op jit(solution)/shard_map/while/body/eval_jaxpr/grk,gkd->grd/dot_general | solution.py:65
  122.6 0.1 add.160
  122.9 5.0 %gather_fusion = bf16[128,64,256]{2,1,0:T(8,128)(2,1)} fusion(bf16[128,64,256]{2,1,0:T(8,128)(2,1)} %get-tuple-element.268, s32[1024]{0:T(1024)S(1)} %pad_clamp_fusion.2), kind=kCustom, calls=%fused_computation.clone.1 | custom fusion | bytes 8389120 | tf_op jit(solution)/shard_map/while/body/eval_jaxpr/gather | solution.py:43
  127.9 0.1 broadcast_in_dim.100
  128.0 0.1 and.118
  128.2 5.9 %fusion.43 = (f32[8,512]{1,0:T(8,128)S(1)}, f32[8,512,1024]{2,1,0:T(8,128)S(1)}) fusion(s32[8,512]{1,0:T(8,128)S(1)} %broadcast_add_fusion.5, s32[8,1024]{1,0:T(8,128)S(1)} %broadcast_add_fusion.6, pred[8,1024]{1,0:T(8,128)(4,1)S(1)} %and.118, bf16[8,1024,256]{2,1,0:T(8,128)(2,1)} %bitcast.58, bf16[4,8,512,128]{3,2,1,0:T(8,128)(2,1)} %get-tuple-element.267, ...), kind=kOutput, calls=%fused_computation.4.clone.1 | convolution fusion | flops 1094709248 | bytes 19997184 | tf_op jit(solution)/shard_map/while/body/eval_jaxpr/grd,gkd->grk/dot_general | solution.py:47
  134.1 6.6 %fusion.44 = f32[8,512]{1,0:T(8,128)S(1)} fusion(f32[8,512]{1,0:T(8,128)S(1)} %get-tuple-element.233, f32[8,512,1024]{2,1,0:T(8,128)S(1)} %get-tuple-element.234, s32[8,512]{1,0:T(8,128)S(1)} %broadcast_add_fusion.5, s32[8,1024]{1,0:T(8,128)S(1)} %broadcast_add_fusion.6, pred[8,1024]{1,0:T(8,128)(4,1)S(1)} %and.118), kind=kLoop, calls=%fused_computation.7.clone.1 | loop fusion | flops 29356032 | bytes 16867328 | tf_op jit(solution)/shard_map/while/body/eval_jaxpr/reduce_sum | solution.py:64
  140.8 7.5 %bitcast_dynamic-update-slice_fusion.5 = f32[4,8,512,128]{3,2,1,0:T(8,128)} fusion(f32[4,8,512,128]{3,2,1,0:T(8,128)} %get-tuple-element.249, s32[]{:T(128)} %get-tuple-element.248, bf16[8,1024,256]{2,1,0:T(8,128)(2,1)S(1)} %bitcast.59, f32[8,512]{1,0:T(8,128)S(1)} %get-tuple-element.233, f32[8,512,1024]{2,1,0:T(8,128)S(1)} %get-tuple-element.234, ...), kind=kOutput, calls=%fused_computation.11.clone.1 | convolution fusion | flops 1103101952 | bytes 21045760 | tf_op jit(solution)/shard_map/while/body/eval_jaxpr/grk,gkd->grd/dot_general | solution.py:65
  148.4 0.1 add.160
  148.7 5.0 %gather_fusion = bf16[128,64,256]{2,1,0:T(8,128)(2,1)} fusion(bf16[128,64,256]{2,1,0:T(8,128)(2,1)} %get-tuple-element.268, s32[1024]{0:T(1024)S(1)} %pad_clamp_fusion.2), kind=kCustom, calls=%fused_computation.clone.1 | custom fusion | bytes 8389120 | tf_op jit(solution)/shard_map/while/body/eval_jaxpr/gather | solution.py:43
  153.8 0.1 and.118
  154.0 5.9 %fusion.43 = (f32[8,512]{1,0:T(8,128)S(1)}, f32[8,512,1024]{2,1,0:T(8,128)S(1)}) fusion(s32[8,512]{1,0:T(8,128)S(1)} %broadcast_add_fusion.5, s32[8,1024]{1,0:T(8,128)S(1)} %broadcast_add_fusion.6, pred[8,1024]{1,0:T(8,128)(4,1)S(1)} %and.118, bf16[8,1024,256]{2,1,0:T(8,128)(2,1)} %bitcast.58, bf16[4,8,512,128]{3,2,1,0:T(8,128)(2,1)} %get-tuple-element.267, ...), kind=kOutput, calls=%fused_computation.4.clone.1 | convolution fusion | flops 1094709248 | bytes 19997184 | tf_op jit(solution)/shard_map/while/body/eval_jaxpr/grd,gkd->grk/dot_general | solution.py:47
  159.9 6.6 %fusion.44 = f32[8,512]{1,0:T(8,128)S(1)} fusion(f32[8,512]{1,0:T(8,128)S(1)} %get-tuple-element.233, f32[8,512,1024]{2,1,0:T(8,128)S(1)} %get-tuple-element.234, s32[8,512]{1,0:T(8,128)S(1)} %broadcast_add_fusion.5, s32[8,1024]{1,0:T(8,128)S(1)} %broadcast_add_fusion.6, pred[8,1024]{1,0:T(8,128)(4,1)S(1)} %and.118), kind=kLoop, calls=%fused_computation.7.clone.1 | loop fusion | flops 29356032 | bytes 16867328 | tf_op jit(solution)/shard_map/while/body/eval_jaxpr/reduce_sum | solution.py:64
  166.6 7.5 %bitcast_dynamic-update-slice_fusion.5 = f32[4,8,512,128]{3,2,1,0:T(8,128)} fusion(f32[4,8,512,128]{3,2,1,0:T(8,128)} %get-tuple-element.249, s32[]{:T(128)} %get-tuple-element.248, bf16[8,1024,256]{2,1,0:T(8,128)(2,1)S(1)} %bitcast.59, f32[8,512]{1,0:T(8,128)S(1)} %get-tuple-element.233, f32[8,512,1024]{2,1,0:T(8,128)S(1)} %get-tuple-element.234, ...), kind=kOutput, calls=%fused_computation.11.clone.1 | convolution fusion | flops 1103101952 | bytes 21045760 | tf_op jit(solution)/shard_map/while/body/eval_jaxpr/grk,gkd->grd/dot_general | solution.py:65
  174.1 1.6 reshape.211
  175.8 0.6 reshape.212
  176.4 9.4 %reshape.210 = f32[2048,1024]{1,0:T(8,128)} reshape(f32[4,8,512,128]{3,2,1,0:T(8,128)} %get-tuple-element.135) | data formatting | bytes 16777216 | tf_op jit(solution)/shard_map/reshape | solution.py:76
  185.8 76.9 %all-reduce.2.cloned.1.call-done = f32[2048,8]{1,0:T(8,128)} async-done(((f32[2048,8]{1,0:T(8,128)}), f32[2048,8]{1,0:T(8,128)}) %all-reduce.2.cloned.1.call-update) | async-done | bytes 65552 | tf_op jit(solution)/shard_map/pmax | solution.py:80
  262.7 2.4 fusion.32
  265.1 0.2 reduce-scatter.4.cloned.1.call-start
  265.3 6.6 %mul.52 = f32[2048,8,128]{2,1,0:T(8,128)} broadcast(f32[2048,8]{1,0:T(8,128)S(1)} %get-tuple-element.159), dimensions={0,1} | broadcast | bytes 8454144 | tf_op jit(solution)/shard_map/mul | solution.py:82
  271.9 12.2 %bitcast_multiply_fusion = f32[2048,1024]{1,0:T(8,128)} fusion(f32[2048,1024]{1,0:T(8,128)} %reshape.210, f32[256,8,8,128]{3,2,1,0:T(8,128)} %bitcast.60), kind=kLoop, calls=%fused_computation.39 | loop fusion | flops 2097152 | bytes 25165824 | tf_op jit(solution)/shard_map/mul | solution.py:82
  284.1 53.9 %reduce-scatter.6.cloned.1.call-done = f32[128,8]{1,0:T(8,128)} async-done(((f32[2048,8]{1,0:T(8,128)}), f32[128,8]{1,0:T(8,128)}) %reduce-scatter.6.cloned.1.call-update) | async-done | bytes 4112 | tf_op jit(solution)/shard_map/reduce_scatter | solution.py:86
  338.0 88.2 %reduce-scatter.4.cloned.1.call-done = f32[128,1024]{1,0:T(8,128)} async-done(((f32[2048,1024]{1,0:T(8,128)}), f32[128,1024]{1,0:T(8,128)}) %reduce-scatter.4.cloned.1.call-update) | async-done | bytes 524304 | tf_op jit(solution)/shard_map/reduce_scatter | solution.py:85
  426.2 1.0 div.35
  427.2 10.3 %fusion.23 = f32[128,8192]{1,0:T(8,128)} fusion(bf16[1,1024,8192]{2,1,0:T(8,128)(2,1)} %param.9, f32[128,1024]{1,0:T(8,128)} %reduce-scatter.4.cloned.1.call-done, f32[16,8,8,128]{3,2,1,0:T(8,128)S(1)} %bitcast.61), kind=kOutput, calls=%fused_computation.37 | convolution fusion | flops 2147745792 | bytes 22020096 | tf_op jit(solution)/shard_map/dot_general | solution.py:94
  437.6 37.3 %reduce-scatter.8.cloned.1.call-done = f32[128,1024]{1,0:T(8,128)} async-done(((f32[128,8192]{1,0:T(8,128)}), f32[128,1024]{1,0:T(8,128)}) %reduce-scatter.8.cloned.1.call-update) | async-done | bytes 524304 | tf_op jit(solution)/shard_map/reduce_scatter | solution.py:95
  (76 shorter events, 1.8 us)
Async XLA Ops:
  6.5 57.1 %all-gather.2.cloned.1.call-start = ((), (), s32[]{:S(2)}) async-start(), calls=%async_computation.3 | async-start | bytes 4456448 | tf_op jit(solution)/shard_map/all_gather | solution.py:15
  7.3 255.4 %all-reduce.2.cloned.1.call-start = ((), (), s32[]{:S(2)}) async-start(), calls=%async_computation.4 | async-start | bytes 2097152 | tf_op jit(solution)/shard_map/pmax | solution.py:80
  82.6 6.7 %copy-start = (bf16[128,64,256]{2,1,0:T(8,128)(2,1)S(1)}, bf16[128,64,256]{2,1,0:T(8,128)(2,1)}, u32[]{:S(2)}) copy-start(bf16[128,64,256]{2,1,0:T(8,128)(2,1)} %gather_fusion) | copy-start | bytes 12582916 | tf_op jit(solution)/shard_map/while
  108.3 6.7 %copy-start = (bf16[128,64,256]{2,1,0:T(8,128)(2,1)S(1)}, bf16[128,64,256]{2,1,0:T(8,128)(2,1)}, u32[]{:S(2)}) copy-start(bf16[128,64,256]{2,1,0:T(8,128)(2,1)} %gather_fusion) | copy-start | bytes 12582916 | tf_op jit(solution)/shard_map/while
  134.1 6.7 %copy-start = (bf16[128,64,256]{2,1,0:T(8,128)(2,1)S(1)}, bf16[128,64,256]{2,1,0:T(8,128)(2,1)}, u32[]{:S(2)}) copy-start(bf16[128,64,256]{2,1,0:T(8,128)(2,1)} %gather_fusion) | copy-start | bytes 12582916 | tf_op jit(solution)/shard_map/while
  159.9 6.7 %copy-start = (bf16[128,64,256]{2,1,0:T(8,128)(2,1)S(1)}, bf16[128,64,256]{2,1,0:T(8,128)(2,1)}, u32[]{:S(2)}) copy-start(bf16[128,64,256]{2,1,0:T(8,128)(2,1)} %gather_fusion) | copy-start | bytes 12582916 | tf_op jit(solution)/shard_map/while
  175.7 162.3 %reduce-scatter.6.cloned.1.call-start = ((), (), s32[]{:S(2)}) async-start(), calls=%async_computation.6 | async-start | bytes 1114112 | tf_op jit(solution)/shard_map/reduce_scatter | solution.py:86
  176.4 86.3 %copy-start.1 = (f32[2048,8]{1,0:T(8,128)S(1)}, f32[2048,8]{1,0:T(8,128)}, u32[]{:S(2)}) copy-start(f32[2048,8]{1,0:T(8,128)} %reshape.211) | copy-start | bytes 196612
  265.1 161.1 %reduce-scatter.4.cloned.1.call-start = ((), (), s32[]{:S(2)}) async-start(), calls=%async_computation.5 | async-start | bytes 8912896 | tf_op jit(solution)/shard_map/reduce_scatter | solution.py:85
  284.1 190.7 %reduce-scatter.8.cloned.1.call-start = ((), (), s32[]{:S(2)}) async-start(), calls=%async_computation.7 | async-start | bytes 4718592 | tf_op jit(solution)/shard_map/reduce_scatter | solution.py:95
Sparse Core Ops, SparseCore 0:
  9.5 54.1 all-gather.1
  175.9 86.7 all-reduce.1
  265.9 72.1 reduce-scatter.5
  341.7 84.4 reduce-scatter.3
  437.7 37.0 reduce-scatter.7
where the time goes:
time: 482 us; the launch traced here: 481 us
  waiting for transfers between devices  310 us (64%)
  matrix products  64.2 us (13%)
  local copies, waits for them, and re-layouts  48.4 us (10%)
  other arithmetic  44.5 us (9%)
  between operations  13.2 us (3%)
    reduce_scatter x1, waiting for transfers between devices, body(): lax.psum_scatter(scaled_numer, 'seq', scatter_dimension=0, tiled=True)  88.2 us
    pmax x1, waiting for transfers between devices, body(): row_top = lax.pmax(peak_part, 'seq')  76.9 us
    reduce_scatter x1, waiting for transfers between devices, body(): lax.psum_scatter(scaled_total, 'seq', scatter_dimension=0, tiled=True)  53.9 us
    all_gather x1, waiting for transfers between devices, body(): all_queries = lax.all_gather(queries, 'seq', axis=0, tiled=True)  53.4 us
    reduce_scatter x1, waiting for transfers between devices, body(): return lax.psum_scatter(head_terms, 'kvh', scatter_dimension=1, tiled=True)  37.3 us
    dot_general x4, matrix products, attend_group(): jnp.einsum('grk,gkd->grd', weights.astype(jnp.bfloat16), value_part, pref...  30.2 us
    reduce_sum x4, other arithmetic, attend_group(): totals = jnp.sum(weights, axis=2)  26.5 us
    dot_general x4, matrix products, attend_group(): jnp.einsum('grd,gkd->grk', rows_in, key_part, preferred_element_type=jnp....  23.8 us
  transfers between devices with their start and end apart: 5, of which 5 were waited for; matrix products, arithmetic and copies ran while one was open for 7% of the time, Pallas kernels for 0%

commit v1 on v0

v1 whole, which is shorter than its diff:
```python
import functools
import math

import jax
import jax.numpy as jnp
from jax import lax
from jax.experimental import pallas as pl
from jax.experimental.pallas import tpu as pltpu
from jax.sharding import PartitionSpec as P

BLK = 64
MOST = 16
HD = 128
GROUP = 8
ROWS = BLK * GROUP
CHUNK = 4
PAY = HD + 16
NEG = -1e30
SCALE = 1.0 / math.sqrt(HD)
LOG2E = math.log2(math.e)
BF = jnp.bfloat16
F32 = jnp.float32


def seq_shift(dz, dx):
    return [(z * 4 + x, ((z + dz) % 4) * 4 + (x + dx) % 4) for z in range(4) for x in range(4)]


def kvh_shift(dy, dc):
    return [(y * 2 + c, ((y + dy) % 4) * 2 + (c + dc) % 2) for y in range(4) for c in range(2)]


def pack(numer, peak, total):
    high = total.astype(BF).astype(F32)
    low = total - high
    row = lax.broadcasted_iota(jnp.int32, (16, ROWS), 0)
    tail = jnp.where(row == 0, peak, jnp.where(row == 1, high, jnp.where(row == 2, low, 0.0)))
    return numer, tail


def attend_kernel(meta_ref, count_ref, ids_ref, kv_ref, *refs, parts, per):
    q_refs, out_refs = refs[:parts], refs[parts : 2 * parts]
    q_scr, o_scr, s_scr, acc = refs[2 * parts :]
    for i, q_ref in enumerate(q_refs):
        q_scr[i * per : (i + 1) * per] = q_ref[...]
    diag_here = meta_ref[parts * per]

    def one(t, carry):
        qb = meta_ref[t]
        n = count_ref[qb]
        chunks = (n + (CHUNK - 1)) // CHUNK
        q = jnp.concatenate([q_scr[t, :, g * HD : (g + 1) * HD] for g in range(GROUP)], axis=0)

        def fetch(c, lo):
            return jnp.concatenate(
                [
                    kv_ref[pl.ds(pl.multiple_of(ids_ref[qb * MOST + c * CHUNK + u] * BLK, BLK), BLK), lo : lo + HD]
                    for u in range(CHUNK)
                ],
                axis=0,
            )

        def first(c, peak):
            base = pl.multiple_of(c * CHUNK * BLK, CHUNK * BLK)
            s_scr[pl.ds(base, CHUNK * BLK), :] = lax.dot_general(
                fetch(c, 0), q, (((1,), (1,)), ((), ())), preferred_element_type=F32
            )

            @pl.when((c == 0) & (diag_here == 1))
            def _():
                off = lax.broadcasted_iota(jnp.int32, (BLK, ROWS), 0)
                tok = lax.broadcasted_iota(jnp.int32, (BLK, ROWS), 1) % BLK
                s_scr[0:BLK, :] = jnp.where(off <= tok, s_scr[0:BLK, :], NEG)

            for u in range(1, CHUNK):

                @pl.when(c * CHUNK + u >= n)
                def _(u=u):
                    s_scr[pl.ds(base + u * BLK, BLK), :] = jnp.full((BLK, ROWS), NEG, F32)

            s = s_scr[pl.ds(base, CHUNK * BLK), :]
            return jnp.maximum(peak, jnp.max(s.reshape(CHUNK * BLK // 8, 8, ROWS), axis=0))

        peak = lax.fori_loop(0, chunks, first, jnp.full((8, ROWS), NEG, F32))
        peak = jnp.max(peak, axis=0, keepdims=True)
        acc[...] = jnp.zeros_like(acc)

        def second(c, total):
            base = pl.multiple_of(c * CHUNK * BLK, CHUNK * BLK)
            s = s_scr[pl.ds(base, CHUNK * BLK), :]
            w = jnp.exp2((s - peak) * (SCALE * LOG2E))
            acc[...] += lax.dot_general(
                fetch(c, HD), w.astype(BF), (((0,), (0,)), ((), ())), preferred_element_type=F32
            )
            return total + jnp.sum(w.reshape(CHUNK * BLK // 8, 8, ROWS), axis=0)

        total = lax.fori_loop(0, chunks, second, jnp.zeros((8, ROWS), F32))
        total = jnp.sum(total, axis=0, keepdims=True)
        scaled = peak * SCALE
        near = scaled.astype(BF).astype(F32)
        gain = jnp.exp2(jnp.where(n > 0, scaled - near, 0.0) * LOG2E)
        numer, tail = pack(acc[...] * gain, near, total * gain)
        o_scr[t, :HD] = numer.astype(o_scr.dtype)
        o_scr[t, HD:] = tail.astype(o_scr.dtype)
        return carry

    lax.fori_loop(0, parts * per, one, 0)
    for i, out_ref in enumerate(out_refs):
        out_ref[...] = o_scr[i * per : (i + 1) * per]


VM = pl.BlockSpec(memory_space=pltpu.VMEM)
SM = pl.BlockSpec(memory_space=pltpu.SMEM)


def attend(qbs, diag_here, counts, ids, kv, arrays, dtype):
    parts, per = len(arrays), arrays[0].shape[0]
    meta = jnp.stack(qbs + [diag_here]).astype(jnp.int32)
    total = parts * per
    return pl.pallas_call(
        functools.partial(attend_kernel, parts=parts, per=per),
        out_shape=[jax.ShapeDtypeStruct((per, PAY, ROWS), dtype)] * parts,
        in_specs=[SM, SM, SM, VM] + [VM] * parts,
        out_specs=[VM] * parts,
        scratch_shapes=[
            pltpu.VMEM((total, BLK, GROUP * HD), BF),
            pltpu.VMEM((total, PAY, ROWS), dtype),
            pltpu.VMEM((MOST * BLK, ROWS), F32),
            pltpu.VMEM((HD, ROWS), F32),
        ],
        compiler_params=pltpu.CompilerParams(vmem_limit_bytes=40 * 2**20),
        cost_estimate=pl.CostEstimate(flops=total * 8 * 16777216, bytes_accessed=8 * 2**20, transcendentals=total * 8 * 32768),
        name="attend",
    )(meta, counts, ids, kv, *arrays)


def merge(blocks):
    tails = [b[HD:].astype(F32) for b in blocks]
    peaks = [t[0:1] for t in tails]
    top = functools.reduce(jnp.maximum, peaks)
    gains = [jnp.exp2((p - top) * LOG2E) for p in peaks]
    numer = sum(b[:HD].astype(F32) * g for b, g in zip(blocks, gains))
    total = sum((t[1:2] + t[2:3]) * g for t, g in zip(tails, gains))
    return numer, top, total


def stage_kernel(*refs):
    ins, outs = refs[:16], refs[16:]
    for half in range(2):
        for pair in range(2):
            srcs = ins[(half * 2 + pair) * 4 : (half * 2 + pair) * 4 + 4]
            for u in range(2):
                slot = pair * 2 + u
                numer, tail = pack(*merge([r[u] for r in srcs]))
                out = outs[half * 4 + slot]
                out[:HD] = numer.astype(out.dtype)
                out[HD:] = tail.astype(out.dtype)


def final_kernel(*refs):
    ins, out = refs[:8], refs[8]
    for half in range(2):
        numer, _, total = merge([r[...] for r in ins[half * 4 : half * 4 + 4]])
        att = numer / total
        for g in range(0, GROUP, 2):
            turned = att[:, g * BLK : (g + 2) * BLK].T.astype(BF)
            out[half * BLK : (half + 1) * BLK, g * HD : (g + 1) * HD] = turned[:BLK]
            out[half * BLK : (half + 1) * BLK, (g + 1) * HD : (g + 2) * HD] = turned[BLK:]


def local_call(kernel, out_shape, args, name):
    return pl.pallas_call(
        kernel,
        out_shape=out_shape,
        in_specs=[VM] * len(args),
        out_specs=jax.tree.map(lambda _: VM, out_shape),
        compiler_params=pltpu.CompilerParams(vmem_limit_bytes=40 * 2**20),
        cost_estimate=pl.CostEstimate(flops=10**7, bytes_accessed=6 * 2**20, transcendentals=0),
        name=name,
    )(*args)


COLS = 512


def project_kernel(idx_ref, att_ref, other_ref, w_ref, wo_ref, out_ref):
    out_ref[...] = (
        jnp.dot(att_ref[...], w_ref[...], preferred_element_type=F32)
        + jnp.dot(other_ref[...], wo_ref[...], preferred_element_type=F32)
    ).astype(out_ref.dtype)


def project(att, other, w, wo, mine, theirs, dtype):
    rows, depth = att.shape
    steps = 1024 // COLS
    idx = jnp.stack([mine, theirs]).astype(jnp.int32)
    return pl.pallas_call(
        project_kernel,
        out_shape=jax.ShapeDtypeStruct((rows, 1024), dtype),
        grid_spec=pltpu.PrefetchScalarGridSpec(
            num_scalar_prefetch=1,
            grid=(steps,),
            in_specs=[
                pl.BlockSpec((rows, depth), lambda i, idx: (0, 0)),
                pl.BlockSpec((rows, depth), lambda i, idx: (0, 0)),
                pl.BlockSpec((depth, COLS), lambda i, idx: (0, idx[0] * steps + i)),
                pl.BlockSpec((depth, COLS), lambda i, idx: (0, idx[1] * steps + i)),
            ],
            out_specs=pl.BlockSpec((rows, COLS), lambda i, idx: (0, i)),
        ),
        compiler_params=pltpu.CompilerParams(vmem_limit_bytes=40 * 2**20),
        cost_estimate=pl.CostEstimate(flops=2 * rows * 2 * depth * 1024, bytes_accessed=5 * 2**20, transcendentals=0),
        name="project",
    )(idx, att, other, w, wo)


def body(queries, kv_cache, block_list, out_weight):
    s = lax.axis_index("seq")
    z, x = s // 4, s % 4
    k = lax.axis_index("kvh")
    y, core = k // 2, k % 2
    kv = kv_cache[0]
    w = out_weight[0]
    block_count = kv.shape[0] // BLK
    qb_count = block_list.shape[0]

    def zx(v, dz, dx):
        return lax.ppermute(v, "seq", seq_shift(dz % 4, dx % 4))

    def yc(v, dy, dc):
        return lax.ppermute(v, "kvh", kvh_shift(dy % 4, dc))

    q = queries[:, 0, :].reshape(2, BLK, GROUP * HD)
    a0, b0 = q[0:1], q[1:2]
    a1, a3, a2 = zx(a0, 0, 1), zx(a0, 0, -1), zx(a0, 0, 2)
    b1, b3, b2 = zx(b0, 1, 0), zx(b0, -1, 0), zx(b0, 2, 0)

    w_split = w.reshape(w.shape[0], 4, 2, 1024)
    w_send = lax.dynamic_index_in_dim(w_split, 1 - core, axis=2, keepdims=False).reshape(w.shape[0], 4096)
    w_other = yc(w_send, 0, 1)

    last = lax.axis_size("seq") - 1
    own_ids = (last + 1) * block_count - qb_count + jnp.arange(qb_count, dtype=jnp.int32)
    diag_here = (s == last).astype(jnp.int32)
    mine = (block_list // block_count == s) & (block_list != own_ids[:, None])
    rank = jnp.cumsum(mine.astype(jnp.int32), axis=1) - 1 + diag_here
    counts = jnp.sum(mine.astype(jnp.int32), axis=1) + diag_here
    slots = jnp.arange(MOST, dtype=jnp.int32)
    hit = mine[:, :, None] & (rank[:, :, None] == slots[None, None, :])
    ids = jnp.sum(jnp.where(hit, (block_list % block_count)[:, :, None], 0), axis=1)
    ids = jnp.where((slots[None, :] == 0) & (diag_here == 1), (own_ids % block_count)[:, None], ids)
    ids = ids.reshape(-1)

    def qb_a(i, j):
        return 2 * (((z - i) % 4) * 4 + (x - j) % 4)

    def qb_b(i, j):
        return 2 * (((z - i) % 4) * 4 + (x - j) % 4) + 1

    a01, a23 = jnp.concatenate([a0, a1]), jnp.concatenate([a2, a3])
    b01, b23 = jnp.concatenate([b0, b1]), jnp.concatenate([b2, b3])
    au01, ad23 = zx(a01, 1, 0), zx(a23, -1, 0)
    bu01, bd23 = zx(b01, 0, 1), zx(b23, 0, -1)
    af01, af23 = zx(au01, 1, 0), zx(ad23, -1, 0)
    bf01, bf23 = zx(bu01, 0, 1), zx(bd23, 0, -1)
    au23, ad01 = zx(a23, 1, 0), zx(a01, -1, 0)
    bu23, bd01 = zx(b23, 0, 1), zx(b01, 0, -1)

    def run(arrays, steps, dtype):
        qbs = []
        for n, (far, pair) in enumerate(steps):
            for near in pair:
                qbs.append(qb_a(far, near) if n < 2 else qb_b(near, far))
        return attend(qbs, diag_here, counts, ids, kv, arrays, dtype)

    lo, hi = (0, 1), (2, 3)
    ao01, ao23, bo01, bo23 = run([a01, a23, b01, b23], [(0, lo), (0, hi)] * 2, F32)
    ra1_01, ra3_23, rb1_01, rb3_23 = run([au01, ad23, bu01, bd23], [(1, lo), (3, hi)] * 2, BF)
    ra2_01, ra2_23, rb2_01, rb2_23 = run([af01, af23, bf01, bf23], [(2, lo), (2, hi)] * 2, BF)
    ra1_23, ra3_01, rb1_23, rb3_01 = run([au23, ad01, bu23, bd01], [(1, hi), (3, lo)] * 2, BF)

    stage_in = [
        ao01, zx(ra1_01, -1, 0), zx(ra2_01, 2, 0), zx(ra3_01, 1, 0),
        ao23, zx(ra1_23, -1, 0), zx(zx(ra2_23, -1, 0), -1, 0), zx(ra3_23, 1, 0),
        bo01, zx(rb1_01, 0, -1), zx(rb2_01, 0, 2), zx(rb3_01, 0, 1),
        bo23, zx(rb1_23, 0, -1), zx(zx(rb2_23, 0, -1), 0, -1), zx(rb3_23, 0, 1),
    ]
    f_shape = jax.ShapeDtypeStruct((PAY, ROWS), F32)
    b_shape = jax.ShapeDtypeStruct((PAY, ROWS), BF)
    m = local_call(stage_kernel, [f_shape, b_shape, b_shape, b_shape] * 2, stage_in, "stage")
    final_in = [
        m[0], zx(m[1], 0, -1), zx(m[2], 0, 2), zx(m[3], 0, 1),
        m[4], zx(m[5], -1, 0), zx(m[6], 2, 0), zx(m[7], 1, 0),
    ]
    att = local_call(final_kernel, jax.ShapeDtypeStruct((2 * BLK, GROUP * HD), BF), final_in, "final")

    other = yc(att, 0, 1)

    def chunk(d, dtype):
        to = (y + d) % 4
        return project(att, other, w, w_other, 2 * to + core, to, dtype)

    r2 = yc(chunk(2, BF), 2, 0)
    r1 = yc(chunk(1, BF), 1, 0)
    r3 = yc(chunk(3, BF), 3, 0)
    return chunk(0, F32) + r1.astype(F32) + r2.astype(F32) + r3.astype(F32)


def solution(mesh):
    in_specs = (P("seq", "kvh", None), P("kvh", "seq", None), P(), P("kvh", None, None))
    out_specs = P("seq", "kvh")
    return jax.shard_map(body, mesh=mesh, in_specs=in_specs, out_specs=out_specs, check_vma=False)
```

time: 482 us -> 258 us (0.54)
  waiting for transfers between devices: 310 us -> 32.2 us
  matrix products: 64.2 us -> 0 us
  local copies, waits for them, and re-layouts: 48.4 us -> 110 us
  Pallas kernels: 0 us -> 58.5 us
  starting transfers between devices: 0.35 us -> 54.2 us
  other arithmetic: 44.5 us -> 2.41 us
  between operations: 13.2 us -> 0.39 us
    reduce_scatter x3 -> x0, waiting for transfers between devices: 179 us -> none  [the longest x1 88.2 us: body(): lax.psum_scatter(scaled_numer, 'seq', scatter_dimension=0, tiled=True)]
    pmax x1 -> x0, waiting for transfers between devices: 76.9 us -> none  [body(): row_top = lax.pmax(peak_part, 'seq')]
    dot_general x9 -> x0, matrix products: 64.2 us -> none  [the longest x4 30.2 us: attend_group(): jnp.einsum('grk,gkd->grd', weights.astype(jnp.bfloat16), value_part, pref...]
    pallas_call x0 -> x10, Pallas kernels: none -> 58.5 us  [the longest x4 42.4 us: attend(): pl.pallas_call(functools.partial(attend_kernel, parts=parts, per=per), ou...]
    dynamic_slice x0 -> x1, local copies, waits for them, and re-layouts: none -> 57.6 us  [body(): lax.dynamic_index_in_dim(w_split, 1 - core, axis=2, keepdims=False)]
    ppermute x0 -> x43, starting transfers between devices: none -> 54.2 us  [the longest x38 48.1 us: zx(): return lax.ppermute(v, 'seq', seq_shift(dz % 4, dx % 4))]
    all_gather x1 -> x0, waiting for transfers between devices: 53.4 us -> none  [body(): all_queries = lax.all_gather(queries, 'seq', axis=0, tiled=True)]
    ppermute x0 -> x43, waiting for transfers between devices: none -> 32.2 us  [the longest x38 27.5 us: zx(): return lax.ppermute(v, 'seq', seq_shift(dz % 4, dx % 4))]
  transfers between devices with their start and end apart: 5 -> 43, of which waited for: 5 -> 15; matrix products, arithmetic and copies ran while one was open for 7% -> 1% of each run, Pallas kernels for 0% -> 21%
where the time goes in v1:
time: 258 us
  local copies, waits for them, and re-layouts  110 us (43%)
  Pallas kernels  58.5 us (23%)
  starting transfers between devices  54.2 us (21%)
  waiting for transfers between devices  32.2 us (12%)
    dynamic_slice x1, local copies, waits for them, and re-layouts, body(): lax.dynamic_index_in_dim(w_split, 1 - core, axis=2, keepdims=False)  57.6 us
    ppermute x38, starting transfers between devices, zx(): return lax.ppermute(v, 'seq', seq_shift(dz % 4, dx % 4))  48.1 us
    pallas_call x4, Pallas kernels, attend(): pl.pallas_call(functools.partial(attend_kernel, parts=parts, per=per), ou...  42.4 us
    another operation x1, local copies, waits for them, and re-layouts, body(): w_split = w.reshape(w.shape[0], 4, 2, 1024)  27.7 us
    ppermute x38, waiting for transfers between devices, zx(): return lax.ppermute(v, 'seq', seq_shift(dz % 4, dx % 4))  27.5 us
    unnamed x31, local copies, waits for them, and re-layouts  24.4 us
    pallas_call x4, Pallas kernels, project(): pl.pallas_call(project_kernel, out_shape=jax.ShapeDtypeStruct((rows, 1024...  13 us
    ppermute x5, starting transfers between devices, yc(): return lax.ppermute(v, 'kvh', kvh_shift(dy % 4, dc))  6.11 us
  transfers between devices with their start and end apart: 43, of which 15 were waited for; matrix products, arithmetic and copies ran while one was open for 1% of the time, Pallas kernels for 21%

profile of v1, /device:TPU:0, one launch (start us, length us, event | category | flops | bytes accessed | tf_op | source)
XLA Modules:
  0.0 257.8 jit_solution(216542034336842053)
XLA Ops:
  0.0 27.7 %reshape_squeeze.4 = bf16[1024,4,2,1024]{3,2,1,0:T(2,128)(2,1)} reshape(bf16[1,1024,8192]{2,1,0:T(8,128)(2,1)} %param.7) | data formatting | bytes 33554432 | tf_op jit(solution)/shard_map/reshape;squeeze | solution.py:238
  27.7 57.6 %dynamic-slice_reduce_fusion = bf16[1024,4,1024]{2,1,0:T(4,128)(2,1)} fusion(bf16[1024,4,2,1024]{3,2,1,0:T(2,128)(2,1)} %reshape_squeeze.4, s32[]{:T(128)S(6)} %select_n.234), kind=kLoop, calls=%fused_computation | loop fusion | bytes 16777220 | tf_op jit(solution)/shard_map/jit(dynamic_index_in_dim)/dynamic_slice | solution.py:239
  85.3 12.2 %copy.9 = bf16[128,8,4,1024]{3,1,2,0:T(8,128)(2,1)} copy(bf16[128,8,4,1024]{3,2,1,0:T(4,128)(2,1)} %bitcast.57) | data formatting | bytes 16777216
  97.5 3.2 %collective-permute-start.1 = (bf16[1,64,1024]{2,1,0:T(8,128)(2,1)S(1)}, bf16[1,64,1024]{2,1,0:T(8,128)(2,1)S(1)}, u32[]{:S(2)}, u32[]{:S(2)}) collective-permute-start(bf16[1,64,1024]{2,1,0:T(8,128)(2,1)S(1)} %get-tuple-element.56), channel_id=1, source_target_pairs={{0,16},{8,24},{16,0},{24,8},{32,48},{40,56},{48,32},{56,40},{64,80... | collective-permute-start | bytes 393224 | tf_op jit(solution)/shard_map/ppermute | solution.py:228
  101.8 3.9 %collective-permute-start.4 = (bf16[1,64,1024]{2,1,0:T(8,128)(2,1)S(1)}, bf16[1,64,1024]{2,1,0:T(8,128)(2,1)S(1)}, u32[]{:S(2)}, u32[]{:S(2)}) collective-permute-start(bf16[1,64,1024]{2,1,0:T(8,128)(2,1)S(1)} %get-tuple-element.55), channel_id=1, source_target_pairs={{0,64},{8,72},{16,80},{24,88},{32,96},{40,104},{48,112},{56,120},{... | collective-permute-start | bytes 393224 | tf_op jit(solution)/shard_map/ppermute | solution.py:228
  107.4 1.4 collective-permute-start.3
  109.8 4.0 %collective-permute-start.7 = (bf16[2,64,1024]{2,1,0:T(8,128)(2,1)S(1)}, bf16[2,64,1024]{2,1,0:T(8,128)(2,1)S(1)}, u32[]{:S(2)}, u32[]{:S(2)}) collective-permute-start(bf16[2,64,1024]{2,1,0:T(8,128)(2,1)S(1)} %constant_dynamic-update-slice_fusion.refs_1_), channel_id=1, source_target_pairs={{0,96},{8,104},{16,112},{24,120},{32,0},{40,8},{48,16},{56,24},{64... | collective-permute-start | bytes 786440 | tf_op jit(solution)/shard_map/ppermute | solution.py:228
  113.8 1.9 collective-permute-start.9
  116.1 3.1 %collective-permute-done.7.refs_1_ = bf16[2,64,1024]{2,1,0:T(8,128)(2,1)S(1)} collective-permute-done((bf16[2,64,1024]{2,1,0:T(8,128)(2,1)S(1)}, bf16[2,64,1024]{2,1,0:T(8,128)(2,1)S(1)}, u32[]{:S(2)}, u32[]{:S(2)}) %collective-permute-start.7) | collective-permute-done | bytes 262176 | tf_op jit(solution)/shard_map/ppermute | solution.py:228
  119.2 1.6 collective-permute-start.19
  120.8 1.5 collective-permute-done.9.refs_3_
  122.3 2.1 collective-permute-start.17
  125.7 1.4 collective-permute-done.19.refs_3_
  127.1 2.8 %collective-permute-start.12 = (bf16[2,64,1024]{2,1,0:T(8,128)(2,1)S(1)}, bf16[2,64,1024]{2,1,0:T(8,128)(2,1)S(1)}, u32[]{:S(2)}, u32[]{:S(2)}) collective-permute-start(bf16[2,64,1024]{2,1,0:T(8,128)(2,1)S(1)} %collective-permute-done.7.refs_1_), channel_id=1, source_target_pairs={{0,96},{8,104},{16,112},{24,120},{32,0},{40,8},{48,16},{56,24},{64... | collective-permute-start | bytes 786440 | tf_op jit(solution)/shard_map/ppermute | solution.py:228
  130.0 2.4 collective-permute-start.14
  132.4 2.2 copy-done
  134.6 10.3 %attend.7 = (bf16[2,144,512]{2,1,0:T(8,128)(2,1)}, bf16[2,144,512]{2,1,0:T(8,128)(2,1)}, bf16[2,144,512]{2,1,0:T(8,128)(2,1)S(1)}, bf16[2,144,512]{2,1,0:T(8,128)(2,1)S(1)}) custom-call(s32[9]{0:T(128)S(1)} %stack.189.meta_ref, s32[32]{0:T(128)S(1)} %broadcast_add_fusion.count_ref, s32[512]{0:T(512)S(1)} %select_n.233.ids_ref, ...), custom_call_target="tpu_custom_call" | custom-call | flops 1073741824 | bytes 8388608 | tf_op jit(solution)/shard_map/attend/pallas_call | solution.py:120
  145.0 3.2 %collective-permute-start.21 = (bf16[2,144,512]{2,1,0:T(8,128)(2,1)}, bf16[2,144,512]{2,1,0:T(8,128)(2,1)S(1)}, u32[]{:S(2)}, u32[]{:S(2)}) collective-permute-start(bf16[2,144,512]{2,1,0:T(8,128)(2,1)} %get-tuple-element.34), channel_id=1, source_target_pairs={{0,96},{8,104},{16,112},{24,120},{32,0},{40,8},{48,16},{56,24},{64... | collective-permute-start | bytes 884744 | tf_op jit(solution)/shard_map/ppermute | solution.py:228
  148.5 2.2 copy-done.1
  150.7 7.2 %attend.5 = (bf16[2,144,512]{2,1,0:T(8,128)(2,1)}, bf16[2,144,512]{2,1,0:T(8,128)(2,1)}, bf16[2,144,512]{2,1,0:T(8,128)(2,1)S(1)}, bf16[2,144,512]{2,1,0:T(8,128)(2,1)S(1)}) custom-call(s32[9]{0:T(128)S(1)} %stack.171.meta_ref, s32[32]{0:T(128)S(1)} %broadcast_add_fusion.count_ref, s32[512]{0:T(512)S(1)} %select_n.233.ids_ref, ...), custom_call_target="tpu_custom_call" | custom-call | flops 1073741824 | bytes 8388608 | tf_op jit(solution)/shard_map/attend/pallas_call | solution.py:120
  159.4 3.2 %collective-permute-start.28 = (bf16[2,144,512]{2,1,0:T(8,128)(2,1)}, bf16[2,144,512]{2,1,0:T(8,128)(2,1)S(1)}, u32[]{:S(2)}, u32[]{:S(2)}) collective-permute-start(bf16[2,144,512]{2,1,0:T(8,128)(2,1)} %copy-done.8), channel_id=1, source_target_pairs={{0,24},{8,0},{16,8},{24,16},{32,56},{40,32},{48,40},{56,48},{64,88... | collective-permute-start | bytes 884744 | tf_op jit(solution)/shard_map/ppermute | solution.py:228
  162.6 3.7 %collective-permute-start.10 = (bf16[2,144,512]{2,1,0:T(8,128)(2,1)}, bf16[2,144,512]{2,1,0:T(8,128)(2,1)S(1)}, u32[]{:S(2)}, u32[]{:S(2)}) collective-permute-start(bf16[2,144,512]{2,1,0:T(8,128)(2,1)} %get-tuple-element.30), channel_id=1, source_target_pairs={{0,96},{8,104},{16,112},{24,120},{32,0},{40,8},{48,16},{56,24},{64... | collective-permute-start | bytes 884744 | tf_op jit(solution)/shard_map/ppermute | solution.py:228
  166.5 2.2 copy-done.2
  170.6 13.3 %attend.6 = (bf16[2,144,512]{2,1,0:T(8,128)(2,1)}, bf16[2,144,512]{2,1,0:T(8,128)(2,1)S(1)}, bf16[2,144,512]{2,1,0:T(8,128)(2,1)}, bf16[2,144,512]{2,1,0:T(8,128)(2,1)S(1)}) custom-call(s32[9]{0:T(128)S(1)} %stack.180.meta_ref, s32[32]{0:T(128)S(1)} %broadcast_add_fusion.count_ref, s32[512]{0:T(512)S(1)} %select_n.233.ids_ref, ...), custom_call_target="tpu_custom_call" | custom-call | flops 1073741824 | bytes 8388608 | tf_op jit(solution)/shard_map/attend/pallas_call | solution.py:120
  184.0 2.0 collective-permute-start.31
  186.0 1.4 collective-permute-start.29
  187.4 6.8 %collective-permute-done.25.refs_9_ = bf16[2,144,512]{2,1,0:T(8,128)(2,1)S(1)} collective-permute-done((bf16[2,144,512]{2,1,0:T(8,128)(2,1)}, bf16[2,144,512]{2,1,0:T(8,128)(2,1)S(1)}, u32[]{:S(2)}, u32[]{:S(2)}) %collective-permute-start.25) | collective-permute-done | bytes 294944 | tf_op jit(solution)/shard_map/ppermute | solution.py:228
  195.8 3.1 %collective-permute-start.23 = (bf16[2,144,512]{2,1,0:T(8,128)(2,1)}, bf16[2,144,512]{2,1,0:T(8,128)(2,1)}, u32[]{:S(2)}, u32[]{:S(2)}) collective-permute-start(bf16[2,144,512]{2,1,0:T(8,128)(2,1)} %collective-permute-done.22), channel_id=1, source_target_pairs={{0,96},{8,104},{16,112},{24,120},{32,0},{40,8},{48,16},{56,24},{64... | collective-permute-start | bytes 884744 | tf_op jit(solution)/shard_map/ppermute | solution.py:228
  199.0 1.6 collective-permute-done.29
  200.6 1.8 collective-permute-start.30
  202.4 2.2 copy-done.3
  204.6 11.6 %attend.4 = (f32[2,144,512]{2,1,0:T(8,128)S(1)}, f32[2,144,512]{2,1,0:T(8,128)S(1)}, f32[2,144,512]{2,1,0:T(8,128)S(1)}, f32[2,144,512]{2,1,0:T(8,128)S(1)}) custom-call(s32[9]{0:T(128)S(1)} %stack.162.meta_ref, s32[32]{0:T(128)S(1)} %broadcast_add_fusion.count_ref, s32[512]{0:T(512)S(1)} %select_n.233.ids_ref, bf16[8192,256]{1,0:T(8,128)(2,1)S(1)} %bitcast.52, ...), custom_call_target="tpu_custom_call" | custom-call | flops 1073741824 | bytes 8388608 | tf_op jit(solution)/shard_map/attend/pallas_call | solution.py:120
  216.3 2.8 %stage.1 = (f32[144,512]{1,0:T(8,128)S(1)}, bf16[144,512]{1,0:T(8,128)(2,1)S(1)}, bf16[144,512]{1,0:T(8,128)(2,1)S(1)}, bf16[144,512]{1,0:T(8,128)(2,1)}, f32[14...) custom-call(f32[2,144,512]{2,1,0:T(8,128)S(1)} %get-tuple-element.29.r, ...), custom_call_target="tpu_custom_call" | custom-call | flops 10000000 | bytes 6291456 | tf_op jit(solution)/shard_map/stage/pallas_call | solution.py:172
  219.1 2.0 collective-permute-start.34
  221.1 3.1 %collective-permute-done.32.refs_1_ = bf16[144,512]{1,0:T(8,128)(2,1)S(1)} collective-permute-done((bf16[144,512]{1,0:T(8,128)(2,1)S(1)}, bf16[144,512]{1,0:T(8,128)(2,1)S(1)}, u32[]{:S(2)}, u32[]{:S(2)}) %collective-permute-start.32) | collective-permute-done | bytes 147488 | tf_op jit(solution)/shard_map/ppermute | solution.py:228
  224.2 1.5 collective-permute-done.33.refs_2_
  225.7 1.6 collective-permute-done.34.refs_3_
  227.3 3.6 %collective-permute-done.36.refs_6_ = bf16[144,512]{1,0:T(8,128)(2,1)S(1)} collective-permute-done((bf16[144,512]{1,0:T(8,128)(2,1)S(1)}, bf16[144,512]{1,0:T(8,128)(2,1)S(1)}, u32[]{:S(2)}, u32[]{:S(2)}) %collective-permute-start.36) | collective-permute-done | bytes 147488 | tf_op jit(solution)/shard_map/ppermute | solution.py:228
  230.9 1.5 collective-permute-done.37.refs_7_
  233.1 1.3 collective-permute-done.38.other_ref
  234.4 3.2 %project.5 = bf16[128,1024]{1,0:T(8,128)(2,1)S(1)} custom-call(s32[2]{0:T(128)S(1)} %pad_add_fusion.1.idx_ref, bf16[128,1024]{1,0:T(8,128)(2,1)S(1)} %final.1.att_ref, bf16[128,1024]{1,0:T(8,128)(2,1)S(1)} %collective-permute-done.38.other_ref, bf16[1024,8192]{1,0:T(8,128)(2,1)} %bitcast.53, bf16[1024,4096]{1,0:T(8,128)(2,1)} %collective-permute-done.39.wo_ref), custom_call_target="tpu_custom_call" | custom-call | flops 536870912 | bytes 5242880 | tf_op jit(solution)/shard_map/project/pallas_call | solution.py:197
  237.6 1.6 collective-permute-start.40
  239.2 3.2 %project.6 = bf16[128,1024]{1,0:T(8,128)(2,1)S(1)} custom-call(s32[2]{0:T(128)S(1)} %pad_add_fusion.2.idx_ref, bf16[128,1024]{1,0:T(8,128)(2,1)S(1)} %final.1.att_ref, bf16[128,1024]{1,0:T(8,128)(2,1)S(1)} %collective-permute-done.38.other_ref, bf16[1024,8192]{1,0:T(8,128)(2,1)} %bitcast.54, bf16[1024,4096]{1,0:T(8,128)(2,1)} %collective-permute-done.39.wo_ref), custom_call_target="tpu_custom_call" | custom-call | flops 536870912 | bytes 5242880 | tf_op jit(solution)/shard_map/project/pallas_call | solution.py:197
  242.5 3.0 %collective-permute-start.41 = (bf16[128,1024]{1,0:T(8,128)(2,1)S(1)}, bf16[128,1024]{1,0:T(8,128)(2,1)S(1)}, u32[]{:S(2)}, u32[]{:S(2)}) collective-permute-start(bf16[128,1024]{1,0:T(8,128)(2,1)S(1)} %project.6), channel_id=1, source_target_pairs={{0,4},{1,5},{2,6},{3,7},{4,0},{5,1},{6,2},{7,3},{8,12},{9,13},{10,... | collective-permute-start | bytes 786440 | tf_op jit(solution)/shard_map/ppermute | solution.py:231
  245.5 3.2 %project.7 = bf16[128,1024]{1,0:T(8,128)(2,1)S(1)} custom-call(s32[2]{0:T(128)S(1)} %pad_add_fusion.3.idx_ref, bf16[128,1024]{1,0:T(8,128)(2,1)S(1)} %final.1.att_ref, bf16[128,1024]{1,0:T(8,128)(2,1)S(1)} %collective-permute-done.38.other_ref, bf16[1024,8192]{1,0:T(8,128)(2,1)} %bitcast.55, bf16[1024,4096]{1,0:T(8,128)(2,1)} %collective-permute-done.39.wo_ref), custom_call_target="tpu_custom_call" | custom-call | flops 536870912 | bytes 5242880 | tf_op jit(solution)/shard_map/project/pallas_call | solution.py:197
  248.7 1.4 collective-permute-start.42
  250.2 3.3 %project.4 = f32[128,1024]{1,0:T(8,128)S(1)} custom-call(s32[2]{0:T(128)S(1)} %pad_add_fusion.idx_ref, bf16[128,1024]{1,0:T(8,128)(2,1)S(1)} %final.1.att_ref, bf16[128,1024]{1,0:T(8,128)(2,1)S(1)} %collective-permute-done.38.other_ref, bf16[1024,8192]{1,0:T(8,128)(2,1)} %bitcast.56, bf16[1024,4096]{1,0:T(8,128)(2,1)} %collective-permute-done.39.wo_ref), custom_call_target="tpu_custom_call" | custom-call | flops 536870912 | bytes 5242880 | tf_op jit(solution)/shard_map/project/pallas_call | solution.py:197
  254.1 2.8 %collective-permute-done.42 = bf16[128,1024]{1,0:T(8,128)(2,1)S(1)} collective-permute-done((bf16[128,1024]{1,0:T(8,128)(2,1)S(1)}, bf16[128,1024]{1,0:T(8,128)(2,1)S(1)}, u32[]{:S(2)}, u32[]{:S(2)}) %collective-permute-start.42) | collective-permute-done | bytes 262176 | tf_op jit(solution)/shard_map/ppermute | solution.py:231
  (106 shorter events, 13.3 us)
Async XLA Ops:
  85.3 12.2 %copy-start.12 = (bf16[128,1,1024]{2,0,1:T(8,128)(2,1)S(1)}, bf16[128,1,1024]{2,0,1:T(8,128)(2,1)}, u32[]{:S(2)}) copy-start(bf16[128,1,1024]{2,0,1:T(8,128)(2,1)} %param.4) | copy-start | bytes 786436
  85.3 21.2 %copy-start.13 = (s32[32,64]{1,0:T(8,128)S(1)}, s32[32,64]{1,0:T(8,128)}, u32[]{:S(2)}) copy-start(s32[32,64]{1,0:T(8,128)} %param.6) | copy-start | bytes 24580
  97.5 136.9 %collective-permute-start.39 = (bf16[1024,4096]{1,0:T(8,128)(2,1)}, bf16[1024,4096]{1,0:T(8,128)(2,1)}, u32[]{:S(2)}, u32[]{:S(2)}) collective-permute-start(bf16[1024,4096]{1,0:T(8,128)(2,1)} %bitcast.58), channel_id=1, source_target_pairs={{0,1},{1,0},{2,3},{3,2},{4,5},{5,4},{6,7},{7,6},{8,9},{9,8},{10,11... | collective-permute-start | bytes 25165832 | tf_op jit(solution)/shard_map/ppermute | solution.py:231
  97.5 9.9 %collective-permute-start.1 = (bf16[1,64,1024]{2,1,0:T(8,128)(2,1)S(1)}, bf16[1,64,1024]{2,1,0:T(8,128)(2,1)S(1)}, u32[]{:S(2)}, u32[]{:S(2)}) collective-permute-start(bf16[1,64,1024]{2,1,0:T(8,128)(2,1)S(1)} %get-tuple-element.56), channel_id=1, source_target_pairs={{0,16},{8,24},{16,0},{24,8},{32,48},{40,56},{48,32},{56,40},{64,80... | collective-permute-start | bytes 393224 | tf_op jit(solution)/shard_map/ppermute | solution.py:228
  100.7 8.1 %collective-permute-start.2 = (bf16[1,64,1024]{2,1,0:T(8,128)(2,1)S(1)}, bf16[1,64,1024]{2,1,0:T(8,128)(2,1)S(1)}, u32[]{:S(2)}, u32[]{:S(2)}) collective-permute-start(bf16[1,64,1024]{2,1,0:T(8,128)(2,1)S(1)} %get-tuple-element.56), channel_id=1, source_target_pairs={{0,24},{8,0},{16,8},{24,16},{32,56},{40,32},{48,40},{56,48},{64,88... | collective-permute-start | bytes 393224 | tf_op jit(solution)/shard_map/ppermute | solution.py:228
  101.8 7.9 %collective-permute-start.4 = (bf16[1,64,1024]{2,1,0:T(8,128)(2,1)S(1)}, bf16[1,64,1024]{2,1,0:T(8,128)(2,1)S(1)}, u32[]{:S(2)}, u32[]{:S(2)}) collective-permute-start(bf16[1,64,1024]{2,1,0:T(8,128)(2,1)S(1)} %get-tuple-element.55), channel_id=1, source_target_pairs={{0,64},{8,72},{16,80},{24,88},{32,96},{40,104},{48,112},{56,120},{... | collective-permute-start | bytes 393224 | tf_op jit(solution)/shard_map/ppermute | solution.py:228
  105.7 8.1 %collective-permute-start.5 = (bf16[1,64,1024]{2,1,0:T(8,128)(2,1)S(1)}, bf16[1,64,1024]{2,1,0:T(8,128)(2,1)S(1)}, u32[]{:S(2)}, u32[]{:S(2)}) collective-permute-start(bf16[1,64,1024]{2,1,0:T(8,128)(2,1)S(1)} %get-tuple-element.55), channel_id=1, source_target_pairs={{0,96},{8,104},{16,112},{24,120},{32,0},{40,8},{48,16},{56,24},{64... | collective-permute-start | bytes 393224 | tf_op jit(solution)/shard_map/ppermute | solution.py:228
  107.4 8.3 %collective-permute-start.3 = (bf16[1,64,1024]{2,1,0:T(8,128)(2,1)S(1)}, bf16[1,64,1024]{2,1,0:T(8,128)(2,1)S(1)}, u32[]{:S(2)}, u32[]{:S(2)}) collective-permute-start(bf16[1,64,1024]{2,1,0:T(8,128)(2,1)S(1)} %get-tuple-element.55), channel_id=1, source_target_pairs={{0,32},{8,40},{16,48},{24,56},{32,64},{40,72},{48,80},{56,88},{64,... | collective-permute-start | bytes 393224 | tf_op jit(solution)/shard_map/ppermute | solution.py:228
  108.8 7.0 %collective-permute-start = (bf16[1,64,1024]{2,1,0:T(8,128)(2,1)S(1)}, bf16[1,64,1024]{2,1,0:T(8,128)(2,1)S(1)}, u32[]{:S(2)}, u32[]{:S(2)}) collective-permute-start(bf16[1,64,1024]{2,1,0:T(8,128)(2,1)S(1)} %get-tuple-element.56), channel_id=1, source_target_pairs={{0,8},{8,16},{16,24},{24,0},{32,40},{40,48},{48,56},{56,32},{64,72... | collective-permute-start | bytes 393224 | tf_op jit(solution)/shard_map/ppermute | solution.py:228
  109.8 9.5 %collective-permute-start.7 = (bf16[2,64,1024]{2,1,0:T(8,128)(2,1)S(1)}, bf16[2,64,1024]{2,1,0:T(8,128)(2,1)S(1)}, u32[]{:S(2)}, u32[]{:S(2)}) collective-permute-start(bf16[2,64,1024]{2,1,0:T(8,128)(2,1)S(1)} %constant_dynamic-update-slice_fusion.refs_1_), channel_id=1, source_target_pairs={{0,96},{8,104},{16,112},{24,120},{32,0},{40,8},{48,16},{56,24},{64... | collective-permute-start | bytes 786440 | tf_op jit(solution)/shard_map/ppermute | solution.py:228
  113.8 8.5 %collective-permute-start.9 = (bf16[2,64,1024]{2,1,0:T(8,128)(2,1)S(1)}, bf16[2,64,1024]{2,1,0:T(8,128)(2,1)S(1)}, u32[]{:S(2)}, u32[]{:S(2)}) collective-permute-start(bf16[2,64,1024]{2,1,0:T(8,128)(2,1)S(1)} %constant_dynamic-update-slice_fusion.2.refs_3_), channel_id=1, source_target_pairs={{0,24},{8,0},{16,8},{24,16},{32,56},{40,32},{48,40},{56,48},{64,88... | collective-permute-start | bytes 786440 | tf_op jit(solution)/shard_map/ppermute | solution.py:228
  115.7 9.1 %collective-permute-start.16 = (bf16[2,64,1024]{2,1,0:T(8,128)(2,1)S(1)}, bf16[2,64,1024]{2,1,0:T(8,128)(2,1)S(1)}, u32[]{:S(2)}, u32[]{:S(2)}) collective-permute-start(bf16[2,64,1024]{2,1,0:T(8,128)(2,1)S(1)} %constant_dynamic-update-slice_fusion.refs_1_), channel_id=1, source_target_pairs={{0,32},{8,40},{16,48},{24,56},{32,64},{40,72},{48,80},{56,88},{64,... | collective-permute-start | bytes 786440 | tf_op jit(solution)/shard_map/ppermute | solution.py:228
  115.8 9.6 %collective-permute-start.18 = (bf16[2,64,1024]{2,1,0:T(8,128)(2,1)S(1)}, bf16[2,64,1024]{2,1,0:T(8,128)(2,1)S(1)}, u32[]{:S(2)}, u32[]{:S(2)}) collective-permute-start(bf16[2,64,1024]{2,1,0:T(8,128)(2,1)S(1)} %constant_dynamic-update-slice_fusion.2.refs_3_), channel_id=1, source_target_pairs={{0,8},{8,16},{16,24},{24,0},{32,40},{40,48},{48,56},{56,32},{64,72... | collective-permute-start | bytes 786440 | tf_op jit(solution)/shard_map/ppermute | solution.py:228
  119.2 7.9 %collective-permute-start.19 = (bf16[2,64,1024]{2,1,0:T(8,128)(2,1)S(1)}, bf16[2,64,1024]{2,1,0:T(8,128)(2,1)S(1)}, u32[]{:S(2)}, u32[]{:S(2)}) collective-permute-start(bf16[2,64,1024]{2,1,0:T(8,128)(2,1)S(1)} %pad_maximum_fusion.1.refs_2_), channel_id=1, source_target_pairs={{0,24},{8,0},{16,8},{24,16},{32,56},{40,32},{48,40},{56,48},{64,88... | collective-permute-start | bytes 786440 | tf_op jit(solution)/shard_map/ppermute | solution.py:228
  122.3 7.7 %collective-permute-start.17 = (bf16[2,64,1024]{2,1,0:T(8,128)(2,1)S(1)}, bf16[2,64,1024]{2,1,0:T(8,128)(2,1)S(1)}, u32[]{:S(2)}, u32[]{:S(2)}) collective-permute-start(bf16[2,64,1024]{2,1,0:T(8,128)(2,1)S(1)} %pad_maximum_fusion.refs_0_), channel_id=1, source_target_pairs={{0,96},{8,104},{16,112},{24,120},{32,0},{40,8},{48,16},{56,24},{64... | collective-permute-start | bytes 786440 | tf_op jit(solution)/shard_map/ppermute | solution.py:228
  124.8 20.1 %collective-permute-start.8 = (bf16[2,64,1024]{2,1,0:T(8,128)(2,1)S(1)}, bf16[2,64,1024]{2,1,0:T(8,128)(2,1)}, u32[]{:S(2)}, u32[]{:S(2)}) collective-permute-start(bf16[2,64,1024]{2,1,0:T(8,128)(2,1)S(1)} %pad_maximum_fusion.1.refs_2_), channel_id=1, source_target_pairs={{0,8},{8,16},{16,24},{24,0},{32,40},{40,48},{48,56},{56,32},{64,72... | collective-permute-start | bytes 786440 | tf_op jit(solution)/shard_map/ppermute | solution.py:228
  125.4 19.7 %collective-permute-start.6 = (bf16[2,64,1024]{2,1,0:T(8,128)(2,1)S(1)}, bf16[2,64,1024]{2,1,0:T(8,128)(2,1)}, u32[]{:S(2)}, u32[]{:S(2)}) collective-permute-start(bf16[2,64,1024]{2,1,0:T(8,128)(2,1)S(1)} %pad_maximum_fusion.refs_0_), channel_id=1, source_target_pairs={{0,32},{8,40},{16,48},{24,56},{32,64},{40,72},{48,80},{56,88},{64,... | collective-permute-start | bytes 786440 | tf_op jit(solution)/shard_map/ppermute | solution.py:228
  127.1 21.1 %collective-permute-start.12 = (bf16[2,64,1024]{2,1,0:T(8,128)(2,1)S(1)}, bf16[2,64,1024]{2,1,0:T(8,128)(2,1)S(1)}, u32[]{:S(2)}, u32[]{:S(2)}) collective-permute-start(bf16[2,64,1024]{2,1,0:T(8,128)(2,1)S(1)} %collective-permute-done.7.refs_1_), channel_id=1, source_target_pairs={{0,96},{8,104},{16,112},{24,120},{32,0},{40,8},{48,16},{56,24},{64... | collective-permute-start | bytes 786440 | tf_op jit(solution)/shard_map/ppermute | solution.py:228
  130.0 18.3 %collective-permute-start.14 = (bf16[2,64,1024]{2,1,0:T(8,128)(2,1)S(1)}, bf16[2,64,1024]{2,1,0:T(8,128)(2,1)S(1)}, u32[]{:S(2)}, u32[]{:S(2)}) collective-permute-start(bf16[2,64,1024]{2,1,0:T(8,128)(2,1)S(1)} %collective-permute-done.9.refs_3_), channel_id=1, source_target_pairs={{0,24},{8,0},{16,8},{24,16},{32,56},{40,32},{48,40},{56,48},{64,88... | collective-permute-start | bytes 786440 | tf_op jit(solution)/shard_map/ppermute | solution.py:228
  144.9 3.3 %copy-start.9 = (bf16[2,144,512]{2,1,0:T(8,128)(2,1)}, bf16[2,144,512]{2,1,0:T(8,128)(2,1)S(1)}, u32[]{:S(2)}) copy-start(bf16[2,144,512]{2,1,0:T(8,128)(2,1)S(1)} %get-tuple-element.40) | copy-start | bytes 884740
  145.0 17.7 %collective-permute-start.20 = (bf16[2,144,512]{2,1,0:T(8,128)(2,1)}, bf16[2,144,512]{2,1,0:T(8,128)(2,1)S(1)}, u32[]{:S(2)}, u32[]{:S(2)}) collective-permute-start(bf16[2,144,512]{2,1,0:T(8,128)(2,1)} %get-tuple-element.32), channel_id=1, source_target_pairs={{0,32},{8,40},{16,48},{24,56},{32,64},{40,72},{48,80},{56,88},{64,... | collective-permute-start | bytes 884744 | tf_op jit(solution)/shard_map/ppermute | solution.py:228
  145.0 21.3 %collective-permute-start.21 = (bf16[2,144,512]{2,1,0:T(8,128)(2,1)}, bf16[2,144,512]{2,1,0:T(8,128)(2,1)S(1)}, u32[]{:S(2)}, u32[]{:S(2)}) collective-permute-start(bf16[2,144,512]{2,1,0:T(8,128)(2,1)} %get-tuple-element.34), channel_id=1, source_target_pairs={{0,96},{8,104},{16,112},{24,120},{32,0},{40,8},{48,16},{56,24},{64... | collective-permute-start | bytes 884744 | tf_op jit(solution)/shard_map/ppermute | solution.py:228
  148.3 9.6 %collective-permute-start.13 = (bf16[2,64,1024]{2,1,0:T(8,128)(2,1)}, bf16[2,64,1024]{2,1,0:T(8,128)(2,1)S(1)}, u32[]{:S(2)}, u32[]{:S(2)}) collective-permute-start(bf16[2,64,1024]{2,1,0:T(8,128)(2,1)} %collective-permute-done.8.refs_2_), channel_id=1, source_target_pairs={{0,8},{8,16},{16,24},{24,0},{32,40},{40,48},{48,56},{56,32},{64,72... | collective-permute-start | bytes 786440 | tf_op jit(solution)/shard_map/ppermute | solution.py:228
  148.3 10.4 %collective-permute-start.11 = (bf16[2,64,1024]{2,1,0:T(8,128)(2,1)}, bf16[2,64,1024]{2,1,0:T(8,128)(2,1)S(1)}, u32[]{:S(2)}, u32[]{:S(2)}) collective-permute-start(bf16[2,64,1024]{2,1,0:T(8,128)(2,1)} %collective-permute-done.6.refs_0_), channel_id=1, source_target_pairs={{0,32},{8,40},{16,48},{24,56},{32,64},{40,72},{48,80},{56,88},{64,... | collective-permute-start | bytes 786440 | tf_op jit(solution)/shard_map/ppermute | solution.py:228
  157.9 8.4 %copy-start.10 = (bf16[2,144,512]{2,1,0:T(8,128)(2,1)}, bf16[2,144,512]{2,1,0:T(8,128)(2,1)S(1)}, u32[]{:S(2)}) copy-start(bf16[2,144,512]{2,1,0:T(8,128)(2,1)S(1)} %get-tuple-element.44) | copy-start | bytes 884740
  157.9 8.4 %copy-start.11 = (bf16[2,144,512]{2,1,0:T(8,128)(2,1)}, bf16[2,144,512]{2,1,0:T(8,128)(2,1)S(1)}, u32[]{:S(2)}) copy-start(bf16[2,144,512]{2,1,0:T(8,128)(2,1)S(1)} %get-tuple-element.38) | copy-start | bytes 884740
  158.7 25.3 %collective-permute-start.27 = (bf16[2,144,512]{2,1,0:T(8,128)(2,1)}, bf16[2,144,512]{2,1,0:T(8,128)(2,1)S(1)}, u32[]{:S(2)}, u32[]{:S(2)}) collective-permute-start(bf16[2,144,512]{2,1,0:T(8,128)(2,1)} %copy-done.9), channel_id=1, source_target_pairs={{0,8},{8,16},{16,24},{24,0},{32,40},{40,48},{48,56},{56,32},{64,72... | collective-permute-start | bytes 884744 | tf_op jit(solution)/shard_map/ppermute | solution.py:228
  159.4 24.6 %collective-permute-start.28 = (bf16[2,144,512]{2,1,0:T(8,128)(2,1)}, bf16[2,144,512]{2,1,0:T(8,128)(2,1)S(1)}, u32[]{:S(2)}, u32[]{:S(2)}) collective-permute-start(bf16[2,144,512]{2,1,0:T(8,128)(2,1)} %copy-done.8), channel_id=1, source_target_pairs={{0,24},{8,0},{16,8},{24,16},{32,56},{40,32},{48,40},{56,48},{64,88... | collective-permute-start | bytes 884744 | tf_op jit(solution)/shard_map/ppermute | solution.py:228
  162.6 23.4 %collective-permute-start.10 = (bf16[2,144,512]{2,1,0:T(8,128)(2,1)}, bf16[2,144,512]{2,1,0:T(8,128)(2,1)S(1)}, u32[]{:S(2)}, u32[]{:S(2)}) collective-permute-start(bf16[2,144,512]{2,1,0:T(8,128)(2,1)} %get-tuple-element.30), channel_id=1, source_target_pairs={{0,96},{8,104},{16,112},{24,120},{32,0},{40,8},{48,16},{56,24},{64... | collective-permute-start | bytes 884744 | tf_op jit(solution)/shard_map/ppermute | solution.py:228
  166.3 19.7 %collective-permute-start.24 = (bf16[2,144,512]{2,1,0:T(8,128)(2,1)}, bf16[2,144,512]{2,1,0:T(8,128)(2,1)S(1)}, u32[]{:S(2)}, u32[]{:S(2)}) collective-permute-start(bf16[2,144,512]{2,1,0:T(8,128)(2,1)} %get-tuple-element.36), channel_id=1, source_target_pairs={{0,32},{8,40},{16,48},{24,56},{32,64},{40,72},{48,80},{56,88},{64,... | collective-permute-start | bytes 884744 | tf_op jit(solution)/shard_map/ppermute | solution.py:228
  184.0 10.2 %collective-permute-start.25 = (bf16[2,144,512]{2,1,0:T(8,128)(2,1)}, bf16[2,144,512]{2,1,0:T(8,128)(2,1)S(1)}, u32[]{:S(2)}, u32[]{:S(2)}) collective-permute-start(bf16[2,144,512]{2,1,0:T(8,128)(2,1)} %copy-done.11), channel_id=1, source_target_pairs={{0,24},{8,0},{16,8},{24,16},{32,56},{40,32},{48,40},{56,48},{64,88... | collective-permute-start | bytes 884744 | tf_op jit(solution)/shard_map/ppermute | solution.py:228
  184.0 11.4 %collective-permute-start.31 = (bf16[2,144,512]{2,1,0:T(8,128)(2,1)}, bf16[2,144,512]{2,1,0:T(8,128)(2,1)S(1)}, u32[]{:S(2)}, u32[]{:S(2)}) collective-permute-start(bf16[2,144,512]{2,1,0:T(8,128)(2,1)} %copy-done.10), channel_id=1, source_target_pairs={{0,8},{8,16},{16,24},{24,0},{32,40},{40,48},{48,56},{56,32},{64,72... | collective-permute-start | bytes 884744 | tf_op jit(solution)/shard_map/ppermute | solution.py:228
  186.0 9.8 %collective-permute-start.22 = (bf16[2,144,512]{2,1,0:T(8,128)(2,1)S(1)}, bf16[2,144,512]{2,1,0:T(8,128)(2,1)}, u32[]{:S(2)}, u32[]{:S(2)}) collective-permute-start(bf16[2,144,512]{2,1,0:T(8,128)(2,1)S(1)} %get-tuple-element.35), channel_id=1, source_target_pairs={{0,96},{8,104},{16,112},{24,120},{32,0},{40,8},{48,16},{56,24},{64... | collective-permute-start | bytes 884744 | tf_op jit(solution)/shard_map/ppermute | solution.py:228
  186.0 14.5 %collective-permute-start.29 = (bf16[2,144,512]{2,1,0:T(8,128)(2,1)S(1)}, bf16[2,144,512]{2,1,0:T(8,128)(2,1)}, u32[]{:S(2)}, u32[]{:S(2)}) collective-permute-start(bf16[2,144,512]{2,1,0:T(8,128)(2,1)S(1)} %get-tuple-element.43), channel_id=1, source_target_pairs={{0,24},{8,0},{16,8},{24,16},{32,56},{40,32},{48,40},{56,48},{64,88... | collective-permute-start | bytes 884744 | tf_op jit(solution)/shard_map/ppermute | solution.py:228
  194.1 22.1 %collective-permute-start.15 = (bf16[2,144,512]{2,1,0:T(8,128)(2,1)}, bf16[2,144,512]{2,1,0:T(8,128)(2,1)}, u32[]{:S(2)}, u32[]{:S(2)}) collective-permute-start(bf16[2,144,512]{2,1,0:T(8,128)(2,1)} %get-tuple-element.31), channel_id=1, source_target_pairs={{0,64},{8,72},{16,80},{24,88},{32,96},{40,104},{48,112},{56,120},{... | collective-permute-start | bytes 884744 | tf_op jit(solution)/shard_map/ppermute | solution.py:228
  195.4 20.9 %collective-permute-start.26 = (bf16[2,144,512]{2,1,0:T(8,128)(2,1)}, bf16[2,144,512]{2,1,0:T(8,128)(2,1)}, u32[]{:S(2)}, u32[]{:S(2)}) collective-permute-start(bf16[2,144,512]{2,1,0:T(8,128)(2,1)} %get-tuple-element.39), channel_id=1, source_target_pairs={{0,16},{8,24},{16,0},{24,8},{32,48},{40,56},{48,32},{56,40},{64,80... | collective-permute-start | bytes 884744 | tf_op jit(solution)/shard_map/ppermute | solution.py:228
  195.8 20.4 %collective-permute-start.23 = (bf16[2,144,512]{2,1,0:T(8,128)(2,1)}, bf16[2,144,512]{2,1,0:T(8,128)(2,1)}, u32[]{:S(2)}, u32[]{:S(2)}) collective-permute-start(bf16[2,144,512]{2,1,0:T(8,128)(2,1)} %collective-permute-done.22), channel_id=1, source_target_pairs={{0,96},{8,104},{16,112},{24,120},{32,0},{40,8},{48,16},{56,24},{64... | collective-permute-start | bytes 884744 | tf_op jit(solution)/shard_map/ppermute | solution.py:228
  200.6 15.7 %collective-permute-start.30 = (bf16[2,144,512]{2,1,0:T(8,128)(2,1)}, bf16[2,144,512]{2,1,0:T(8,128)(2,1)}, u32[]{:S(2)}, u32[]{:S(2)}) collective-permute-start(bf16[2,144,512]{2,1,0:T(8,128)(2,1)} %collective-permute-done.29), channel_id=1, source_target_pairs={{0,24},{8,0},{16,8},{24,16},{32,56},{40,32},{48,40},{56,48},{64,88... | collective-permute-start | bytes 884744 | tf_op jit(solution)/shard_map/ppermute | solution.py:228
  219.1 5.1 %collective-permute-start.32 = (bf16[144,512]{1,0:T(8,128)(2,1)S(1)}, bf16[144,512]{1,0:T(8,128)(2,1)S(1)}, u32[]{:S(2)}, u32[]{:S(2)}) collective-permute-start(bf16[144,512]{1,0:T(8,128)(2,1)S(1)} %get-tuple-element.46), channel_id=1, source_target_pairs={{0,24},{8,0},{16,8},{24,16},{32,56},{40,32},{48,40},{56,48},{64,88... | collective-permute-start | bytes 442376 | tf_op jit(solution)/shard_map/ppermute | solution.py:228
  219.1 6.7 %collective-permute-start.33 = (bf16[144,512]{1,0:T(8,128)(2,1)S(1)}, bf16[144,512]{1,0:T(8,128)(2,1)S(1)}, u32[]{:S(2)}, u32[]{:S(2)}) collective-permute-start(bf16[144,512]{1,0:T(8,128)(2,1)S(1)} %get-tuple-element.47), channel_id=1, source_target_pairs={{0,16},{8,24},{16,0},{24,8},{32,48},{40,56},{48,32},{56,40},{64,80... | collective-permute-start | bytes 442376 | tf_op jit(solution)/shard_map/ppermute | solution.py:228
  219.1 8.2 %collective-permute-start.34 = (bf16[144,512]{1,0:T(8,128)(2,1)}, bf16[144,512]{1,0:T(8,128)(2,1)S(1)}, u32[]{:S(2)}, u32[]{:S(2)}) collective-permute-start(bf16[144,512]{1,0:T(8,128)(2,1)} %get-tuple-element.48), channel_id=1, source_target_pairs={{0,8},{8,16},{16,24},{24,0},{32,40},{40,48},{48,56},{56,32},{64,72... | collective-permute-start | bytes 442376 | tf_op jit(solution)/shard_map/ppermute | solution.py:228
  221.1 6.2 %collective-permute-start.35 = (bf16[144,512]{1,0:T(8,128)(2,1)}, bf16[144,512]{1,0:T(8,128)(2,1)S(1)}, u32[]{:S(2)}, u32[]{:S(2)}) collective-permute-start(bf16[144,512]{1,0:T(8,128)(2,1)} %get-tuple-element.50), channel_id=1, source_target_pairs={{0,96},{8,104},{16,112},{24,120},{32,0},{40,8},{48,16},{56,24},{64... | collective-permute-start | bytes 442376 | tf_op jit(solution)/shard_map/ppermute | solution.py:228
  224.2 6.7 %collective-permute-start.36 = (bf16[144,512]{1,0:T(8,128)(2,1)S(1)}, bf16[144,512]{1,0:T(8,128)(2,1)S(1)}, u32[]{:S(2)}, u32[]{:S(2)}) collective-permute-start(bf16[144,512]{1,0:T(8,128)(2,1)S(1)} %get-tuple-element.51), channel_id=1, source_target_pairs={{0,64},{8,72},{16,80},{24,88},{32,96},{40,104},{48,112},{56,120},{... | collective-permute-start | bytes 442376 | tf_op jit(solution)/shard_map/ppermute | solution.py:228
  225.7 6.7 %collective-permute-start.37 = (bf16[144,512]{1,0:T(8,128)(2,1)S(1)}, bf16[144,512]{1,0:T(8,128)(2,1)S(1)}, u32[]{:S(2)}, u32[]{:S(2)}) collective-permute-start(bf16[144,512]{1,0:T(8,128)(2,1)S(1)} %get-tuple-element.52), channel_id=1, source_target_pairs={{0,32},{8,40},{16,48},{24,56},{32,64},{40,72},{48,80},{56,88},{64,... | collective-permute-start | bytes 442376 | tf_op jit(solution)/shard_map/ppermute | solution.py:228
  232.7 1.6 collective-permute-start.38
  237.6 15.9 %collective-permute-start.40 = (bf16[128,1024]{1,0:T(8,128)(2,1)S(1)}, bf16[128,1024]{1,0:T(8,128)(2,1)S(1)}, u32[]{:S(2)}, u32[]{:S(2)}) collective-permute-start(bf16[128,1024]{1,0:T(8,128)(2,1)S(1)} %project.5), channel_id=1, source_target_pairs={{0,2},{1,3},{2,4},{3,5},{4,6},{5,7},{6,0},{7,1},{8,10},{9,11},{10,... | collective-permute-start | bytes 786440 | tf_op jit(solution)/shard_map/ppermute | solution.py:231
  242.5 11.6 %collective-permute-start.41 = (bf16[128,1024]{1,0:T(8,128)(2,1)S(1)}, bf16[128,1024]{1,0:T(8,128)(2,1)S(1)}, u32[]{:S(2)}, u32[]{:S(2)}) collective-permute-start(bf16[128,1024]{1,0:T(8,128)(2,1)S(1)} %project.6), channel_id=1, source_target_pairs={{0,4},{1,5},{2,6},{3,7},{4,0},{5,1},{6,2},{7,3},{8,12},{9,13},{10,... | collective-permute-start | bytes 786440 | tf_op jit(solution)/shard_map/ppermute | solution.py:231
  248.7 8.1 %collective-permute-start.42 = (bf16[128,1024]{1,0:T(8,128)(2,1)S(1)}, bf16[128,1024]{1,0:T(8,128)(2,1)S(1)}, u32[]{:S(2)}, u32[]{:S(2)}) collective-permute-start(bf16[128,1024]{1,0:T(8,128)(2,1)S(1)} %project.7), channel_id=1, source_target_pairs={{0,6},{1,7},{2,0},{3,1},{4,2},{5,3},{6,4},{7,5},{8,14},{9,15},{10,... | collective-permute-start | bytes 786440 | tf_op jit(solution)/shard_map/ppermute | solution.py:231
  (9 other events, 15.5 us)

commit v2 on v1

v2 whole, which is shorter than its diff:
```python
import functools
import math

import jax
import jax.numpy as jnp
from jax import lax
from jax.experimental import pallas as pl
from jax.experimental.pallas import tpu as pltpu
from jax.sharding import PartitionSpec as P

BLK = 64
MOST = 16
HD = 128
GROUP = 8
ROWS = BLK * GROUP
CHUNK = 4
FLIPS = (0, 1, 3, 2)
PAY = HD + 16
NEG = -1e30
SCALE = 1.0 / math.sqrt(HD)
LOG2E = math.log2(math.e)
BF = jnp.bfloat16
F32 = jnp.float32
COST = 8 * 10**9
VMEM_SOME = 20 * 2**20


def seq_shift(dz, dx):
    return [(z * 4 + x, ((z + dz) % 4) * 4 + (x + dx) % 4) for z in range(4) for x in range(4)]


def seq_flip(fz, fx):
    return [(z * 4 + x, (z ^ fz) * 4 + (x ^ fx)) for z in range(4) for x in range(4)]


def kvh_shift(dy, dc):
    return [(y * 2 + c, ((y + dy) % 4) * 2 + (c + dc) % 2) for y in range(4) for c in range(2)]


def pack(numer, peak, total):
    high = total.astype(BF).astype(F32)
    low = total - high
    row = lax.broadcasted_iota(jnp.int32, (16, ROWS), 0)
    tail = jnp.where(row == 0, peak, jnp.where(row == 1, high, jnp.where(row == 2, low, 0.0)))
    return numer, tail


def attend_kernel(place_ref, count_ref, ids_ref, kv_ref, *refs, far):
    parts, per = 2, 4
    q_refs, refs = refs[:parts], refs[parts:]
    out_refs, refs = refs[:parts], refs[parts:]
    q_scr, o_scr, s_scr, kv_scr, diag_scr, sems = refs
    total = parts * per
    pairs = total // 2
    step = CHUNK * BLK

    place = place_ref[0]
    z, x = place // 4, place % 4

    def qb_of(t):
        j = t % per
        f = j ^ (j // 2)
        qa = 2 * (((z + 4 - far) % 4) * 4 + (x ^ f))
        qb = 2 * ((z ^ f) * 4 + (x + 4 - far) % 4) + 1
        return jnp.where(t < per, qa, qb)

    def size(p):
        most = jnp.maximum(count_ref[qb_of(2 * p)], count_ref[qb_of(2 * p + 1)])
        return jnp.where(most <= CHUNK, 1, jnp.where(most <= 2 * CHUNK, 2, MOST // CHUNK))

    def start(p, slot):
        blocks = size(p) * CHUNK
        for u in range(2):
            base = qb_of(2 * p + u) * MOST

            def issue(v, carry, u=u, base=base):
                pltpu.make_async_copy(
                    kv_ref.at[pl.ds(pl.multiple_of(ids_ref[base + v] * BLK, BLK), BLK), :],
                    kv_scr.at[slot, u, pl.ds(pl.multiple_of(v * BLK, BLK), BLK), :],
                    sems.at[slot, u],
                ).start()
                return carry

            lax.fori_loop(0, blocks, issue, 0)

    start(0, 0)
    off = lax.broadcasted_iota(jnp.int32, (BLK, ROWS), 0)
    tok = lax.broadcasted_iota(jnp.int32, (BLK, ROWS), 1) % BLK
    diag_scr[...] = jnp.where((off > tok) & (place_ref[2] == 1), NEG, 0.0)
    for i, q_ref in enumerate(q_refs):
        q_scr[i * per : (i + 1) * per] = q_ref[...]

    def work(p, slot, chunks):
        counts = [count_ref[qb_of(2 * p + u)] for u in range(2)]
        for u in range(2):
            pltpu.make_async_copy(
                kv_ref.at[0 : chunks * step, :], kv_scr.at[slot, u, 0 : chunks * step, :], sems.at[slot, u]
            ).wait()
        peaks = []
        for u in range(2):
            q = jnp.concatenate([q_scr[2 * p + u, :, g * HD : (g + 1) * HD] for g in range(GROUP)], axis=0)
            peak = None
            for c in range(chunks):
                s = lax.dot_general(
                    kv_scr[slot, u, c * step : (c + 1) * step, :HD],
                    q,
                    (((1,), (1,)), ((), ())),
                    preferred_element_type=F32,
                )
                for v in range(CHUNK):
                    at = c * CHUNK + v
                    part = s[v * BLK : (v + 1) * BLK]
                    if at == 0:
                        part = part + diag_scr[...]
                    else:
                        part = part + jnp.where(at < counts[u], 0.0, NEG)
                    s_scr[u, at * BLK : (at + 1) * BLK, :] = part
                    part = jnp.max(part.reshape(BLK // 8, 8, ROWS), axis=0)
                    peak = part if peak is None else jnp.maximum(peak, part)
            peaks.append(jnp.max(peak, axis=0, keepdims=True))
        for u in range(2):
            peak = peaks[u]
            numer, mass = None, None
            for c in range(chunks):
                w = jnp.exp2((s_scr[u, c * step : (c + 1) * step, :] - peak) * (SCALE * LOG2E))
                part = lax.dot_general(
                    kv_scr[slot, u, c * step : (c + 1) * step, HD:],
                    w.astype(BF),
                    (((0,), (0,)), ((), ())),
                    preferred_element_type=F32,
                )
                numer = part if numer is None else numer + part
                part = jnp.sum(w.reshape(step // 8, 8, ROWS), axis=0)
                mass = part if mass is None else mass + part
            mass = jnp.sum(mass, axis=0, keepdims=True)
            used = counts[u] > 0
            scaled = peak * SCALE
            near = scaled.astype(BF).astype(F32)
            gain = jnp.where(used, jnp.exp2((scaled - near) * LOG2E), 0.0)
            near = jnp.where(used, near, NEG)
            numer, mass = numer * gain, mass * gain
            numer, tail = pack(numer, near, mass)
            o_scr[2 * p + u, :HD] = numer.astype(o_scr.dtype)
            o_scr[2 * p + u, HD:] = tail.astype(o_scr.dtype)

    def one(p, carry):
        slot = lax.rem(p, 2)

        @pl.when(p + 1 < pairs)
        def _():
            start(p + 1, 1 - slot)

        have = size(p)
        for chunks in (1, 2, MOST // CHUNK):

            @pl.when(have == chunks)
            def _(chunks=chunks):
                work(p, slot, chunks)

        return carry

    lax.fori_loop(0, pairs, one, 0)
    for i, out_ref in enumerate(out_refs):
        out_ref[...] = o_scr[i * per : (i + 1) * per]


VM = pl.BlockSpec(memory_space=pltpu.VMEM)
SM = pl.BlockSpec(memory_space=pltpu.SMEM)


HB = pl.BlockSpec(memory_space=pltpu.HBM)
WIDE = 1024


def attend(place, counts, ids, kv, arrays, far, dtype):
    parts, per = 2, 4
    total = parts * per
    return pl.pallas_call(
        functools.partial(attend_kernel, far=far),
        out_shape=[jax.ShapeDtypeStruct((per, PAY, ROWS), dtype)] * parts,
        in_specs=[SM, SM, SM, HB] + [VM] * parts,
        out_specs=[VM] * parts,
        scratch_shapes=[
            pltpu.VMEM((total, BLK, GROUP * HD), BF),
            pltpu.VMEM((total, PAY, ROWS), dtype),
            pltpu.VMEM((2, MOST * BLK, ROWS), F32),
            pltpu.VMEM((2, 2, MOST * BLK, 2 * HD), BF),
            pltpu.VMEM((BLK, ROWS), F32),
            pltpu.SemaphoreType.DMA((2, 2)),
        ],
        compiler_params=pltpu.CompilerParams(vmem_limit_bytes=VMEM_SOME),
        cost_estimate=pl.CostEstimate(flops=COST, bytes_accessed=2**20, transcendentals=0),
        name="attend",
    )(place, counts, ids, kv, *arrays)


def merge(blocks):
    tails = [b[HD:].astype(F32) for b in blocks]
    peaks = [t[0:1] for t in tails]
    top = functools.reduce(jnp.maximum, peaks)
    gains = [jnp.exp2((p - top) * LOG2E) for p in peaks]
    numer = sum(b[:HD].astype(F32) * g for b, g in zip(blocks, gains))
    total = sum((t[1:2] + t[2:3]) * g for t, g in zip(tails, gains))
    return numer, top, total


def store(out, at, numer, peak, total):
    numer, tail = pack(numer, peak, total)
    out[at, :HD] = numer.astype(out.dtype)
    out[at, HD:] = tail.astype(out.dtype)


def join_kernel(a_near, a_far, b_near, b_far, a_out, b_out):
    for near, far, out in ((a_near, a_far, a_out), (b_near, b_far, b_out)):
        for slot in range(4):
            store(out, slot, *merge([near[slot], far[slot]]))


def stage_kernel(*refs):
    ins, outs = refs[:6], refs[6:]
    for half in range(2):
        for slot in range(4):
            store(outs[half * 2 + slot // 2], slot % 2, *merge([r[slot] for r in ins[half * 3 : half * 3 + 3]]))


def step_kernel(*refs):
    ins, outs = refs[:4], refs[4:]
    for half in range(2):
        for slot in range(2):
            store(outs[half * 2 + slot], 0, *merge([r[slot] for r in ins[half * 2 : half * 2 + 2]]))


def final_kernel(*refs):
    ins, out = refs[:4], refs[4]
    for half in range(2):
        numer, _, total = merge([r[0] for r in ins[half * 2 : half * 2 + 2]])
        att = numer / total
        for g in range(0, GROUP, 2):
            turned = att[:, g * BLK : (g + 2) * BLK].T.astype(BF)
            out[half * BLK : (half + 1) * BLK, g * HD : (g + 1) * HD] = turned[:BLK]
            out[half * BLK : (half + 1) * BLK, (g + 1) * HD : (g + 2) * HD] = turned[BLK:]


def local_call(kernel, out_shape, args, name):
    return pl.pallas_call(
        kernel,
        out_shape=out_shape,
        in_specs=[VM] * len(args),
        out_specs=jax.tree.map(lambda _: VM, out_shape),
        compiler_params=pltpu.CompilerParams(vmem_limit_bytes=VMEM_SOME),
        cost_estimate=pl.CostEstimate(flops=10**7, bytes_accessed=2 * 2**20, transcendentals=0),
        name=name,
    )(*args)


def take_kernel(place_ref, w_ref, out_ref):
    out_ref[...] = w_ref[...]


def take_chunks(w, place):
    depth = w.shape[0]
    return pl.pallas_call(
        take_kernel,
        out_shape=jax.ShapeDtypeStruct((depth, 4 * WIDE), w.dtype),
        grid_spec=pltpu.PrefetchScalarGridSpec(
            num_scalar_prefetch=1,
            grid=(4,),
            in_specs=[pl.BlockSpec((depth, WIDE), lambda i, place: (0, i * 2 + 1 - place[1] % 2))],
            out_specs=pl.BlockSpec((depth, WIDE), lambda i, place: (0, i)),
        ),
        compiler_params=pltpu.CompilerParams(vmem_limit_bytes=52 * 2**20),
        cost_estimate=pl.CostEstimate(flops=0, bytes_accessed=16 * 2**20, transcendentals=0),
        name="take_chunks",
    )(place, w)


PIECE = 256


def project_kernel(place_ref, att_ref, other_ref, w_ref, wo_ref, out_ref, w_scr, acc, sems, *, far):
    k = place_ref[1]
    to = (k // 2 + far) % 4
    pieces = att_ref.shape[1] // PIECE
    copies = []
    for n, (ref, chunk) in enumerate([(w_ref, 2 * to + k % 2), (wo_ref, to)]):
        for r in range(pieces):
            copies.append(
                pltpu.make_async_copy(
                    ref.at[r * PIECE : (r + 1) * PIECE, pl.ds(pl.multiple_of(chunk * WIDE, WIDE), WIDE)],
                    w_scr.at[n * pieces + r],
                    sems.at[n * pieces + r],
                )
            )
    for c in copies:
        c.start()
    for n, ref in enumerate([att_ref, other_ref]):
        for r in range(pieces):
            at = n * pieces + r
            copies[at].wait()
            part = jnp.dot(ref[:, r * PIECE : (r + 1) * PIECE], w_scr[at], preferred_element_type=F32)
            if at == 0:
                acc[...] = part
            elif at < 2 * pieces - 1:
                acc[...] += part
            else:
                out_ref[...] = (acc[...] + part).astype(out_ref.dtype)


def project(place, att, other, w, wo, far, dtype):
    rows, depth = att.shape
    return pl.pallas_call(
        functools.partial(project_kernel, far=far),
        out_shape=jax.ShapeDtypeStruct((rows, WIDE), dtype),
        in_specs=[SM, VM, VM, HB, HB],
        out_specs=VM,
        scratch_shapes=[
            pltpu.VMEM((2 * depth // PIECE, PIECE, WIDE), BF),
            pltpu.VMEM((rows, WIDE), F32),
            pltpu.SemaphoreType.DMA((2 * depth // PIECE,)),
        ],
        compiler_params=pltpu.CompilerParams(vmem_limit_bytes=52 * 2**20),
        cost_estimate=pl.CostEstimate(flops=4 * rows * depth * WIDE, bytes_accessed=5 * 2**20, transcendentals=0),
        name="project",
    )(place, att, other, w, wo)


def body(queries, kv_cache, block_list, out_weight):
    s = lax.axis_index("seq")
    k = lax.axis_index("kvh")
    last = lax.axis_size("seq") - 1
    place = jnp.stack([s, k, jnp.where(s == last, 1, 0)]).astype(jnp.int32)
    kv = kv_cache[0]
    w = out_weight[0]
    block_count = kv.shape[0] // BLK
    qb_count = block_list.shape[0]

    def zx(v, dz, dx):
        return lax.ppermute(v, "seq", seq_shift(dz % 4, dx % 4))

    def flip(v, fz, fx):
        return lax.ppermute(v, "seq", seq_flip(fz, fx))

    def yc(v, dy, dc):
        return lax.ppermute(v, "kvh", kvh_shift(dy % 4, dc))

    q = queries[:, 0, :].reshape(2, BLK, GROUP * HD)
    a, b = q[0:1], q[1:2]
    a, b = lax.optimization_barrier((jnp.concatenate([a, flip(a, 0, 1)]), jnp.concatenate([b, flip(b, 1, 0)])))
    a, b = lax.optimization_barrier((jnp.concatenate([a, flip(a, 0, 3)]), jnp.concatenate([b, flip(b, 3, 0)])))
    w_send = take_chunks(lax.optimization_barrier((w, a, b))[0], place)
    w_other = yc(w_send, 0, 1)
    au, bu, ad, bd = lax.optimization_barrier((zx(a, 1, 0), zx(b, 0, 1), zx(a, -1, 0), zx(b, 0, -1)))
    af, bf = zx(au, 1, 0), zx(bu, 0, 1)

    own_ids = (last + 1) * block_count - qb_count + jnp.arange(qb_count, dtype=jnp.int32)
    diag_here = (s == last).astype(jnp.int32)
    mine = (block_list // block_count == s) & (block_list != own_ids[:, None])
    rank = jnp.cumsum(mine.astype(jnp.int32), axis=1) - 1 + diag_here
    counts = jnp.sum(mine.astype(jnp.int32), axis=1) + diag_here
    slots = jnp.arange(MOST, dtype=jnp.int32)
    hit = mine[:, :, None] & (rank[:, :, None] == slots[None, None, :])
    ids = jnp.sum(jnp.where(hit, (block_list % block_count)[:, :, None], 0), axis=1)
    ids = jnp.where((slots[None, :] == 0) & (diag_here == 1), (own_ids % block_count)[:, None], ids)
    ids = ids.reshape(-1)

    def run(pair, far, dtype):
        return attend(place, counts, ids, kv, pair, far, dtype)

    ra3, rb3 = run([ad, bd], 3, BF)
    ra3, rb3 = zx(ra3, 1, 0), zx(rb3, 0, 1)
    ra1, rb1 = run([au, bu], 1, F32)
    ra2, rb2 = run([af, bf], 2, BF)
    ra2, rb2 = zx(ra2, -1, 0), zx(rb2, 0, -1)
    ao, bo = run([a, b], 0, F32)
    b_four, b_two = (jax.ShapeDtypeStruct((n, PAY, ROWS), BF) for n in (4, 2))
    f_two = jax.ShapeDtypeStruct((2, PAY, ROWS), F32)
    b_one, f_one = (jax.ShapeDtypeStruct((1, PAY, ROWS), t) for t in (BF, F32))
    ra1, rb1 = local_call(join_kernel, [b_four] * 2, [ra1, ra2, rb1, rb2], "join")
    ra1, rb1 = zx(ra1, -1, 0), zx(rb1, 0, -1)
    a_stay, a_go, b_stay, b_go = local_call(
        stage_kernel, [f_two, b_two] * 2, [ao, ra3, ra1, bo, rb3, rb1], "stage"
    )
    a_go, b_go = flip(a_go, 0, 3), flip(b_go, 3, 0)
    a_stay, a_go, b_stay, b_go = local_call(step_kernel, [f_one, b_one] * 2, [a_stay, a_go, b_stay, b_go], "step")
    a_go, b_go = flip(a_go, 0, 1), flip(b_go, 1, 0)
    att = local_call(
        final_kernel, jax.ShapeDtypeStruct((2 * BLK, GROUP * HD), BF), [a_stay, a_go, b_stay, b_go], "final"
    )

    other = yc(att, 0, 1)

    def chunk(far, dtype):
        return project(place, att, other, w, w_other, far, dtype)

    r2 = yc(chunk(2, BF), 2, 0)
    r1 = yc(chunk(1, BF), 1, 0)
    r3 = yc(chunk(3, BF), 3, 0)
    return chunk(0, F32) + r1.astype(F32) + r2.astype(F32) + r3.astype(F32)


def solution(mesh):
    in_specs = (P("seq", "kvh", None), P("kvh", "seq", None), P(), P("kvh", None, None))
    out_specs = P("seq", "kvh")
    return jax.shard_map(body, mesh=mesh, in_specs=in_specs, out_specs=out_specs, check_vma=False)
```

time: 258 us -> 142 us (0.55)
  local copies, waits for them, and re-layouts: 110 us -> 3.27 us
  starting transfers between devices: 54.2 us -> 33.3 us
  waiting for transfers between devices: 32.2 us -> 48 us
  Pallas kernels: 58.5 us -> 53.5 us
    dynamic_slice x1 -> x0, local copies, waits for them, and re-layouts: 57.6 us -> none  [body(): lax.dynamic_index_in_dim(w_split, 1 - core, axis=2, keepdims=False)]
    ppermute x38 -> x12, starting transfers between devices: 48.1 us -> 13.7 us  [zx(): return lax.ppermute(v, 'seq', seq_shift(dz % 4, dx % 4))]
    another operation x5 -> x0, local copies, waits for them, and re-layouts: 28 us -> none  [the longest x1 27.7 us: body(): w_split = w.reshape(w.shape[0], 4, 2, 1024)]
    unnamed x31 -> x6, local copies, waits for them, and re-layouts: 24.4 us -> 2.2 us
    ppermute x0 -> x8, waiting for transfers between devices: none -> 21 us  [flip(): return lax.ppermute(v, 'seq', seq_flip(fz, fx))]
    ppermute x0 -> x8, starting transfers between devices: none -> 13.4 us  [flip(): return lax.ppermute(v, 'seq', seq_flip(fz, fx))]
    ppermute x38 -> x12, waiting for transfers between devices: 27.5 us -> 21.6 us  [zx(): return lax.ppermute(v, 'seq', seq_shift(dz % 4, dx % 4))]
    pallas_call x8 -> x9, Pallas kernels: 55.4 us -> 52 us  [the longest x4 32.2 us: attend(): pl.pallas_call(functools.partial(attend_kernel, far=far), out_shape=[jax....]
  transfers between devices with their start and end apart: 43 -> 25, of which waited for: 15 -> 18; matrix products, arithmetic and copies ran while one was open for 1% -> 1% of each run, Pallas kernels for 21% -> 30%
where the time goes in v2:
time: 142 us; the launch traced here: 141 us
  Pallas kernels  53.5 us (38%)
  waiting for transfers between devices  48 us (34%)
  starting transfers between devices  33.3 us (23%)
  local copies, waits for them, and re-layouts  3.27 us (2%)
  other arithmetic  2.28 us (2%)
    pallas_call x4, Pallas kernels, attend(): pl.pallas_call(functools.partial(attend_kernel, far=far), out_shape=[jax....  32.2 us
    ppermute x12, waiting for transfers between devices, zx(): return lax.ppermute(v, 'seq', seq_shift(dz % 4, dx % 4))  21.6 us
    ppermute x8, waiting for transfers between devices, flip(): return lax.ppermute(v, 'seq', seq_flip(fz, fx))  21 us
    ppermute x12, starting transfers between devices, zx(): return lax.ppermute(v, 'seq', seq_shift(dz % 4, dx % 4))  13.7 us
    ppermute x8, starting transfers between devices, flip(): return lax.ppermute(v, 'seq', seq_flip(fz, fx))  13.4 us
    pallas_call x4, Pallas kernels, project(): pl.pallas_call(functools.partial(project_kernel, far=far), out_shape=jax....  12.1 us
    pallas_call x1, Pallas kernels, take_chunks(): pl.pallas_call(take_kernel, out_shape=jax.ShapeDtypeStruct((depth, 4 * WI...  7.71 us
    ppermute x5, starting transfers between devices, yc(): return lax.ppermute(v, 'kvh', kvh_shift(dy % 4, dc))  6.15 us
  transfers between devices with their start and end apart: 25, of which 18 were waited for; matrix products, arithmetic and copies ran while one was open for 1% of the time, Pallas kernels for 30%

profile of v2, /device:TPU:0, one launch (start us, length us, event | category | flops | bytes accessed | tf_op | source)
XLA Modules:
  0.0 140.6 jit_solution(3544224361793284145)
XLA Ops:
  0.0 1.0 slice_bitcast_fusion
  1.0 2.1 %collective-permute-start.1 = (bf16[1,64,1024]{2,1,0:T(8,128)(2,1)S(1)}, bf16[1,64,1024]{2,1,0:T(8,128)(2,1)S(1)}, u32[]{:S(2)}, u32[]{:S(2)}) collective-permute-start(bf16[1,64,1024]{2,1,0:T(8,128)(2,1)S(1)} %get-tuple-element.61), channel_id=1, source_target_pairs={{0,32},{8,40},{16,48},{24,56},{32,0},{40,8},{48,16},{56,24},{64,96... | collective-permute-start | bytes 393224 | tf_op jit(solution)/shard_map/ppermute | solution.py:341
  3.1 1.5 %collective-permute-start = (bf16[1,64,1024]{2,1,0:T(8,128)(2,1)S(1)}, bf16[1,64,1024]{2,1,0:T(8,128)(2,1)S(1)}, u32[]{:S(2)}, u32[]{:S(2)}) collective-permute-start(bf16[1,64,1024]{2,1,0:T(8,128)(2,1)S(1)} %get-tuple-element.62), channel_id=1, source_target_pairs={{0,8},{8,0},{16,24},{24,16},{32,40},{40,32},{48,56},{56,48},{64,72... | collective-permute-start | bytes 393224 | tf_op jit(solution)/shard_map/ppermute | solution.py:341
  4.6 2.0 %collective-permute-done.1 = bf16[1,64,1024]{2,1,0:T(8,128)(2,1)S(1)} collective-permute-done((bf16[1,64,1024]{2,1,0:T(8,128)(2,1)S(1)}, bf16[1,64,1024]{2,1,0:T(8,128)(2,1)S(1)}, u32[]{:S(2)}, u32[]{:S(2)}) %collective-permute-start.1) | collective-permute-done | bytes 131104 | tf_op jit(solution)/shard_map/ppermute | solution.py:341
  6.6 1.4 %collective-permute-done = bf16[1,64,1024]{2,1,0:T(8,128)(2,1)S(1)} collective-permute-done((bf16[1,64,1024]{2,1,0:T(8,128)(2,1)S(1)}, bf16[1,64,1024]{2,1,0:T(8,128)(2,1)S(1)}, u32[]{:S(2)}, u32[]{:S(2)}) %collective-permute-start) | collective-permute-done | bytes 131104 | tf_op jit(solution)/shard_map/ppermute | solution.py:341
  8.1 2.8 %collective-permute-start.2 = (bf16[2,64,1024]{2,1,0:T(8,128)(2,1)S(1)}, bf16[2,64,1024]{2,1,0:T(8,128)(2,1)S(1)}, u32[]{:S(2)}, u32[]{:S(2)}) collective-permute-start(bf16[2,64,1024]{2,1,0:T(8,128)(2,1)S(1)} %pad_maximum_fusion.2), channel_id=1, source_target_pairs={{0,24},{8,16},{16,8},{24,0},{32,56},{40,48},{48,40},{56,32},{64,88... | collective-permute-start | bytes 786440 | tf_op jit(solution)/shard_map/ppermute | solution.py:341
  10.9 2.5 %collective-permute-start.3 = (bf16[2,64,1024]{2,1,0:T(8,128)(2,1)S(1)}, bf16[2,64,1024]{2,1,0:T(8,128)(2,1)S(1)}, u32[]{:S(2)}, u32[]{:S(2)}) collective-permute-start(bf16[2,64,1024]{2,1,0:T(8,128)(2,1)S(1)} %pad_maximum_fusion.3), channel_id=1, source_target_pairs={{0,96},{8,104},{16,112},{24,120},{32,64},{40,72},{48,80},{56,88},{... | collective-permute-start | bytes 786440 | tf_op jit(solution)/shard_map/ppermute | solution.py:341
  13.5 2.7 %collective-permute-done.2 = bf16[2,64,1024]{2,1,0:T(8,128)(2,1)S(1)} collective-permute-done((bf16[2,64,1024]{2,1,0:T(8,128)(2,1)S(1)}, bf16[2,64,1024]{2,1,0:T(8,128)(2,1)S(1)}, u32[]{:S(2)}, u32[]{:S(2)}) %collective-permute-start.2) | collective-permute-done | bytes 262176 | tf_op jit(solution)/shard_map/ppermute | solution.py:341
  16.3 2.4 %collective-permute-done.3 = bf16[2,64,1024]{2,1,0:T(8,128)(2,1)S(1)} collective-permute-done((bf16[2,64,1024]{2,1,0:T(8,128)(2,1)S(1)}, bf16[2,64,1024]{2,1,0:T(8,128)(2,1)S(1)}, u32[]{:S(2)}, u32[]{:S(2)}) %collective-permute-start.3) | collective-permute-done | bytes 262176 | tf_op jit(solution)/shard_map/ppermute | solution.py:341
  18.8 7.7 %take_chunks.1 = bf16[1024,4096]{1,0:T(8,128)(2,1)} custom-call(s32[3]{0:T(128)S(1)} %pad_add_fusion.place_ref, bf16[1024,8192]{1,0:T(8,128)(2,1)} %bitcast.13), custom_call_target="tpu_custom_call" | custom-call | bytes 16777216 | tf_op jit(solution)/shard_map/take_chunks/pallas_call | solution.py:262
  26.8 0.6 select_reduce_fusion
  27.4 2.8 %collective-permute-start.6 = (bf16[4,64,1024]{2,1,0:T(8,128)(2,1)S(1)}, bf16[4,64,1024]{2,1,0:T(8,128)(2,1)S(1)}, u32[]{:S(2)}, u32[]{:S(2)}) collective-permute-start(bf16[4,64,1024]{2,1,0:T(8,128)(2,1)S(1)} %pad_maximum_fusion.refs_0_), channel_id=1, source_target_pairs={{0,96},{8,104},{16,112},{24,120},{32,0},{40,8},{48,16},{56,24},{64... | collective-permute-start | bytes 1572872 | tf_op jit(solution)/shard_map/ppermute | solution.py:338
  30.3 0.5 collective-permute-start.7
  30.7 1.5 %collective-permute-start.5 = (bf16[4,64,1024]{2,1,0:T(8,128)(2,1)S(1)}, bf16[4,64,1024]{2,1,0:T(8,128)(2,1)S(1)}, u32[]{:S(2)}, u32[]{:S(2)}) collective-permute-start(bf16[4,64,1024]{2,1,0:T(8,128)(2,1)S(1)} %pad_maximum_fusion.1.refs_1_), channel_id=1, source_target_pairs={{0,8},{8,16},{16,24},{24,0},{32,40},{40,48},{48,56},{56,32},{64,72... | collective-permute-start | bytes 1572872 | tf_op jit(solution)/shard_map/ppermute | solution.py:338
  32.6 9.5 %collective-permute-done.6.refs_0_ = bf16[4,64,1024]{2,1,0:T(8,128)(2,1)S(1)} collective-permute-done((bf16[4,64,1024]{2,1,0:T(8,128)(2,1)S(1)}, bf16[4,64,1024]{2,1,0:T(8,128)(2,1)S(1)}, u32[]{:S(2)}, u32[]{:S(2)}) %collective-permute-start.6) | collective-permute-done | bytes 524320 | tf_op jit(solution)/shard_map/ppermute | solution.py:338
  42.1 3.4 %collective-permute-done.4.refs_0_ = bf16[4,64,1024]{2,1,0:T(8,128)(2,1)S(1)} collective-permute-done((bf16[4,64,1024]{2,1,0:T(8,128)(2,1)S(1)}, bf16[4,64,1024]{2,1,0:T(8,128)(2,1)S(1)}, u32[]{:S(2)}, u32[]{:S(2)}) %collective-permute-start.4) | collective-permute-done | bytes 524320 | tf_op jit(solution)/shard_map/ppermute | solution.py:338
  45.7 0.8 collective-permute-start.9
  46.5 2.2 %copy-done = bf16[1,8192,256]{2,1,0:T(8,128)(2,1)S(1)} copy-done((bf16[1,8192,256]{2,1,0:T(8,128)(2,1)S(1)}, bf16[1,8192,256]{2,1,0:T(8,128)(2,1)}, u32[]{:S(2)}) %copy-start) | copy-done | bytes 4194328
  48.7 5.3 %attend.5 = (bf16[4,144,512]{2,1,0:T(8,128)(2,1)S(1)}, bf16[4,144,512]{2,1,0:T(8,128)(2,1)S(1)}) custom-call(s32[3]{0:T(128)S(1)} %pad_add_fusion.place_ref, s32[32]{0:T(128)S(1)} %broadcast_add_fusion.count_ref, s32[512]{0:T(512)S(1)} %select_n.44.ids_ref, bf16[8192,256]{1,0:T(8,128)(2,1)S(1)} %bitcast.9, ...), custom_call_target="tpu_custom_call" | custom-call | flops 8000000000 | bytes 1048576 | tf_op jit(solution)/shard_map/attend/pallas_call | solution.py:178
  54.0 4.0 %collective-permute-start.8 = (bf16[4,144,512]{2,1,0:T(8,128)(2,1)S(1)}, bf16[4,144,512]{2,1,0:T(8,128)(2,1)S(1)}, u32[]{:S(2)}, u32[]{:S(2)}) collective-permute-start(bf16[4,144,512]{2,1,0:T(8,128)(2,1)S(1)} %get-tuple-element.39), channel_id=1, source_target_pairs={{0,32},{8,40},{16,48},{24,56},{32,64},{40,72},{48,80},{56,88},{64,... | collective-permute-start | bytes 1769480 | tf_op jit(solution)/shard_map/ppermute | solution.py:338
  57.9 1.1 collective-permute-start.14
  59.1 2.3 %collective-permute-done.9.refs_0_ = bf16[4,64,1024]{2,1,0:T(8,128)(2,1)S(1)} collective-permute-done((bf16[4,64,1024]{2,1,0:T(8,128)(2,1)S(1)}, bf16[4,64,1024]{2,1,0:T(8,128)(2,1)S(1)}, u32[]{:S(2)}, u32[]{:S(2)}) %collective-permute-start.9) | collective-permute-done | bytes 524320 | tf_op jit(solution)/shard_map/ppermute | solution.py:338
  61.4 11.1 %attend.7 = (bf16[4,144,512]{2,1,0:T(8,128)(2,1)S(1)}, bf16[4,144,512]{2,1,0:T(8,128)(2,1)S(1)}) custom-call(s32[3]{0:T(128)S(1)} %pad_add_fusion.place_ref, s32[32]{0:T(128)S(1)} %broadcast_add_fusion.count_ref, s32[512]{0:T(512)S(1)} %select_n.44.ids_ref, bf16[8192,256]{1,0:T(8,128)(2,1)S(1)} %bitcast.10, ...), custom_call_target="tpu_custom_call" | custom-call | flops 8000000000 | bytes 1048576 | tf_op jit(solution)/shard_map/attend/pallas_call | solution.py:178
  72.8 8.3 %attend.6 = (f32[4,144,512]{2,1,0:T(8,128)S(1)}, f32[4,144,512]{2,1,0:T(8,128)S(1)}) custom-call(s32[3]{0:T(128)S(1)} %pad_add_fusion.place_ref, s32[32]{0:T(128)S(1)} %broadcast_add_fusion.count_ref, s32[512]{0:T(512)S(1)} %select_n.44.ids_ref, bf16[8192,256]{1,0:T(8,128)(2,1)S(1)} %bitcast.11, bf16[4,64,1024]{2,1,0:T(8,128)(2,1)S(1)} %collective-permute-done.4.refs_0_, ...), custom_call_target="tpu_custom_call" | custom-call | flops 8000000000 | bytes 1048576 | tf_op jit(solution)/shard_map/attend/pallas_call | solution.py:178
  81.1 4.1 %collective-permute-done.11.a_far = bf16[4,144,512]{2,1,0:T(8,128)(2,1)S(1)} collective-permute-done((bf16[4,144,512]{2,1,0:T(8,128)(2,1)S(1)}, bf16[4,144,512]{2,1,0:T(8,128)(2,1)S(1)}, u32[]{:S(2)}, u32[]{:S(2)}) %collective-permute-start.11) | collective-permute-done | bytes 589856 | tf_op jit(solution)/shard_map/ppermute | solution.py:338
  85.3 0.4 join.1
  85.7 1.0 collective-permute-start.13
  86.7 1.7 %collective-permute-start.15 = (bf16[4,144,512]{2,1,0:T(8,128)(2,1)S(1)}, bf16[4,144,512]{2,1,0:T(8,128)(2,1)S(1)}, u32[]{:S(2)}, u32[]{:S(2)}) collective-permute-start(bf16[4,144,512]{2,1,0:T(8,128)(2,1)S(1)} %get-tuple-element.49), channel_id=1, source_target_pairs={{0,24},{8,0},{16,8},{24,16},{32,56},{40,32},{48,40},{56,48},{64,88... | collective-permute-start | bytes 1769480 | tf_op jit(solution)/shard_map/ppermute | solution.py:338
  88.4 7.5 %attend.4 = (f32[4,144,512]{2,1,0:T(8,128)S(1)}, f32[4,144,512]{2,1,0:T(8,128)S(1)}) custom-call(s32[3]{0:T(128)S(1)} %pad_add_fusion.place_ref, s32[32]{0:T(128)S(1)} %broadcast_add_fusion.count_ref, s32[512]{0:T(512)S(1)} %select_n.44.ids_ref, bf16[8192,256]{1,0:T(8,128)(2,1)S(1)} %bitcast.12, bf16[4,64,1024]{2,1,0:T(8,128)(2,1)S(1)} %pad_maximum_fusion.refs_0_, ...), custom_call_target="tpu_custom_call" | custom-call | flops 8000000000 | bytes 1048576 | tf_op jit(solution)/shard_map/attend/pallas_call | solution.py:178
  95.9 1.4 %collective-permute-done.13.refs_2_ = bf16[4,144,512]{2,1,0:T(8,128)(2,1)S(1)} collective-permute-done((bf16[4,144,512]{2,1,0:T(8,128)(2,1)S(1)}, bf16[4,144,512]{2,1,0:T(8,128)(2,1)S(1)}, u32[]{:S(2)}, u32[]{:S(2)}) %collective-permute-start.13) | collective-permute-done | bytes 589856 | tf_op jit(solution)/shard_map/ppermute | solution.py:338
  97.3 0.6 collective-permute-done.15.refs_5_
  97.9 0.7 stage.1
  98.6 3.7 %collective-permute-start.16 = (bf16[2,144,512]{2,1,0:T(8,128)(2,1)S(1)}, bf16[2,144,512]{2,1,0:T(8,128)(2,1)S(1)}, u32[]{:S(2)}, u32[]{:S(2)}) collective-permute-start(bf16[2,144,512]{2,1,0:T(8,128)(2,1)S(1)} %get-tuple-element.51), channel_id=1, source_target_pairs={{0,24},{8,16},{16,8},{24,0},{32,56},{40,48},{48,40},{56,32},{64,88... | collective-permute-start | bytes 884744 | tf_op jit(solution)/shard_map/ppermute | solution.py:341
  102.3 0.6 collective-permute-start.17
  102.9 4.1 %collective-permute-done.16.refs_1_ = bf16[2,144,512]{2,1,0:T(8,128)(2,1)S(1)} collective-permute-done((bf16[2,144,512]{2,1,0:T(8,128)(2,1)S(1)}, bf16[2,144,512]{2,1,0:T(8,128)(2,1)S(1)}, u32[]{:S(2)}, u32[]{:S(2)}) %collective-permute-start.16) | collective-permute-done | bytes 294944 | tf_op jit(solution)/shard_map/ppermute | solution.py:341
  107.0 3.2 %collective-permute-done.17.refs_3_ = bf16[2,144,512]{2,1,0:T(8,128)(2,1)S(1)} collective-permute-done((bf16[2,144,512]{2,1,0:T(8,128)(2,1)S(1)}, bf16[2,144,512]{2,1,0:T(8,128)(2,1)S(1)}, u32[]{:S(2)}, u32[]{:S(2)}) %collective-permute-start.17) | collective-permute-done | bytes 294944 | tf_op jit(solution)/shard_map/ppermute | solution.py:341
  110.7 5.0 %collective-permute-done.18.refs_1_ = bf16[1,144,512]{2,1,0:T(8,128)(2,1)S(1)} collective-permute-done((bf16[1,144,512]{2,1,0:T(8,128)(2,1)S(1)}, bf16[1,144,512]{2,1,0:T(8,128)(2,1)S(1)}, u32[]{:S(2)}, u32[]{:S(2)}) %collective-permute-start.18) | collective-permute-done | bytes 147488 | tf_op jit(solution)/shard_map/ppermute | solution.py:341
  116.1 1.5 %collective-permute-done.20.other_ref = bf16[128,1024]{1,0:T(8,128)(2,1)S(1)} collective-permute-done((bf16[128,1024]{1,0:T(8,128)(2,1)S(1)}, bf16[128,1024]{1,0:T(8,128)(2,1)S(1)}, u32[]{:S(2)}, u32[]{:S(2)}) %collective-permute-start.20) | collective-permute-done | bytes 262176 | tf_op jit(solution)/shard_map/ppermute | solution.py:344
  117.6 3.0 %project.5 = bf16[128,1024]{1,0:T(8,128)(2,1)S(1)} custom-call(s32[3]{0:T(128)S(1)} %pad_add_fusion.place_ref, bf16[128,1024]{1,0:T(8,128)(2,1)S(1)} %final.1.att_ref, bf16[128,1024]{1,0:T(8,128)(2,1)S(1)} %collective-permute-done.20.other_ref, bf16[1024,8192]{1,0:T(8,128)(2,1)} %bitcast.14, bf16[1024,4096]{1,0:T(8,128)(2,1)} %collective-permute-done.21.wo_ref), custom_call_target="tpu_custom_call" | custom-call | flops 536870912 | bytes 5242880 | tf_op jit(solution)/shard_map/project/pallas_call | solution.py:311
  120.6 1.7 %collective-permute-start.22 = (bf16[128,1024]{1,0:T(8,128)(2,1)S(1)}, bf16[128,1024]{1,0:T(8,128)(2,1)S(1)}, u32[]{:S(2)}, u32[]{:S(2)}) collective-permute-start(bf16[128,1024]{1,0:T(8,128)(2,1)S(1)} %project.5), channel_id=1, source_target_pairs={{0,2},{1,3},{2,4},{3,5},{4,6},{5,7},{6,0},{7,1},{8,10},{9,11},{10,... | collective-permute-start | bytes 786440 | tf_op jit(solution)/shard_map/ppermute | solution.py:344
  122.3 3.0 %project.6 = bf16[128,1024]{1,0:T(8,128)(2,1)S(1)} custom-call(s32[3]{0:T(128)S(1)} %pad_add_fusion.place_ref, bf16[128,1024]{1,0:T(8,128)(2,1)S(1)} %final.1.att_ref, bf16[128,1024]{1,0:T(8,128)(2,1)S(1)} %collective-permute-done.20.other_ref, bf16[1024,8192]{1,0:T(8,128)(2,1)} %bitcast.15, bf16[1024,4096]{1,0:T(8,128)(2,1)} %collective-permute-done.21.wo_ref), custom_call_target="tpu_custom_call" | custom-call | flops 536870912 | bytes 5242880 | tf_op jit(solution)/shard_map/project/pallas_call | solution.py:311
  125.3 3.0 %collective-permute-start.23 = (bf16[128,1024]{1,0:T(8,128)(2,1)S(1)}, bf16[128,1024]{1,0:T(8,128)(2,1)S(1)}, u32[]{:S(2)}, u32[]{:S(2)}) collective-permute-start(bf16[128,1024]{1,0:T(8,128)(2,1)S(1)} %project.6), channel_id=1, source_target_pairs={{0,4},{1,5},{2,6},{3,7},{4,0},{5,1},{6,2},{7,3},{8,12},{9,13},{10,... | collective-permute-start | bytes 786440 | tf_op jit(solution)/shard_map/ppermute | solution.py:344
  128.3 3.0 %project.7 = bf16[128,1024]{1,0:T(8,128)(2,1)S(1)} custom-call(s32[3]{0:T(128)S(1)} %pad_add_fusion.place_ref, bf16[128,1024]{1,0:T(8,128)(2,1)S(1)} %final.1.att_ref, bf16[128,1024]{1,0:T(8,128)(2,1)S(1)} %collective-permute-done.20.other_ref, bf16[1024,8192]{1,0:T(8,128)(2,1)} %bitcast.16, bf16[1024,4096]{1,0:T(8,128)(2,1)} %collective-permute-done.21.wo_ref), custom_call_target="tpu_custom_call" | custom-call | flops 536870912 | bytes 5242880 | tf_op jit(solution)/shard_map/project/pallas_call | solution.py:311
  131.3 1.4 %collective-permute-start.24 = (bf16[128,1024]{1,0:T(8,128)(2,1)S(1)}, bf16[128,1024]{1,0:T(8,128)(2,1)S(1)}, u32[]{:S(2)}, u32[]{:S(2)}) collective-permute-start(bf16[128,1024]{1,0:T(8,128)(2,1)S(1)} %project.7), channel_id=1, source_target_pairs={{0,6},{1,7},{2,0},{3,1},{4,2},{5,3},{6,4},{7,5},{8,14},{9,15},{10,... | collective-permute-start | bytes 786440 | tf_op jit(solution)/shard_map/ppermute | solution.py:344
  132.8 3.0 %project.4 = f32[128,1024]{1,0:T(8,128)S(1)} custom-call(s32[3]{0:T(128)S(1)} %pad_add_fusion.place_ref, bf16[128,1024]{1,0:T(8,128)(2,1)S(1)} %final.1.att_ref, bf16[128,1024]{1,0:T(8,128)(2,1)S(1)} %collective-permute-done.20.other_ref, bf16[1024,8192]{1,0:T(8,128)(2,1)} %bitcast.17, bf16[1024,4096]{1,0:T(8,128)(2,1)} %collective-permute-done.21.wo_ref), custom_call_target="tpu_custom_call" | custom-call | flops 536870912 | bytes 5242880 | tf_op jit(solution)/shard_map/project/pallas_call | solution.py:311
  135.8 1.3 collective-permute-done.23
  137.1 2.5 %collective-permute-done.24 = bf16[128,1024]{1,0:T(8,128)(2,1)S(1)} collective-permute-done((bf16[128,1024]{1,0:T(8,128)(2,1)S(1)}, bf16[128,1024]{1,0:T(8,128)(2,1)S(1)}, u32[]{:S(2)}, u32[]{:S(2)}) %collective-permute-start.24) | collective-permute-done | bytes 262176 | tf_op jit(solution)/shard_map/ppermute | solution.py:344
  139.7 0.9 convert_add_fusion
  (39 shorter events, 2.1 us)
Async XLA Ops:
  1.0 5.6 %collective-permute-start.1 = (bf16[1,64,1024]{2,1,0:T(8,128)(2,1)S(1)}, bf16[1,64,1024]{2,1,0:T(8,128)(2,1)S(1)}, u32[]{:S(2)}, u32[]{:S(2)}) collective-permute-start(bf16[1,64,1024]{2,1,0:T(8,128)(2,1)S(1)} %get-tuple-element.61), channel_id=1, source_target_pairs={{0,32},{8,40},{16,48},{24,56},{32,0},{40,8},{48,16},{56,24},{64,96... | collective-permute-start | bytes 393224 | tf_op jit(solution)/shard_map/ppermute | solution.py:341
  3.1 5.0 %collective-permute-start = (bf16[1,64,1024]{2,1,0:T(8,128)(2,1)S(1)}, bf16[1,64,1024]{2,1,0:T(8,128)(2,1)S(1)}, u32[]{:S(2)}, u32[]{:S(2)}) collective-permute-start(bf16[1,64,1024]{2,1,0:T(8,128)(2,1)S(1)} %get-tuple-element.62), channel_id=1, source_target_pairs={{0,8},{8,0},{16,24},{24,16},{32,40},{40,32},{48,56},{56,48},{64,72... | collective-permute-start | bytes 393224 | tf_op jit(solution)/shard_map/ppermute | solution.py:341
  8.1 8.1 %collective-permute-start.2 = (bf16[2,64,1024]{2,1,0:T(8,128)(2,1)S(1)}, bf16[2,64,1024]{2,1,0:T(8,128)(2,1)S(1)}, u32[]{:S(2)}, u32[]{:S(2)}) collective-permute-start(bf16[2,64,1024]{2,1,0:T(8,128)(2,1)S(1)} %pad_maximum_fusion.2), channel_id=1, source_target_pairs={{0,24},{8,16},{16,8},{24,0},{32,56},{40,48},{48,40},{56,32},{64,88... | collective-permute-start | bytes 786440 | tf_op jit(solution)/shard_map/ppermute | solution.py:341
  10.9 7.8 %collective-permute-start.3 = (bf16[2,64,1024]{2,1,0:T(8,128)(2,1)S(1)}, bf16[2,64,1024]{2,1,0:T(8,128)(2,1)S(1)}, u32[]{:S(2)}, u32[]{:S(2)}) collective-permute-start(bf16[2,64,1024]{2,1,0:T(8,128)(2,1)S(1)} %pad_maximum_fusion.3), channel_id=1, source_target_pairs={{0,96},{8,104},{16,112},{24,120},{32,64},{40,72},{48,80},{56,88},{... | collective-permute-start | bytes 786440 | tf_op jit(solution)/shard_map/ppermute | solution.py:341
  18.7 7.7 %copy-start.2 = (s32[32,64]{1,0:T(8,128)S(1)}, s32[32,64]{1,0:T(8,128)}, u32[]{:S(2)}) copy-start(s32[32,64]{1,0:T(8,128)} %param.6) | copy-start | bytes 24580
  26.5 91.1 %collective-permute-start.21 = (bf16[1024,4096]{1,0:T(8,128)(2,1)}, bf16[1024,4096]{1,0:T(8,128)(2,1)}, u32[]{:S(2)}, u32[]{:S(2)}) collective-permute-start(bf16[1024,4096]{1,0:T(8,128)(2,1)} %take_chunks.1), channel_id=1, source_target_pairs={{0,1},{1,0},{2,3},{3,2},{4,5},{5,4},{6,7},{7,6},{8,9},{9,8},{10,11... | collective-permute-start | bytes 25165832 | tf_op jit(solution)/shard_map/ppermute | solution.py:344
  27.4 14.7 %collective-permute-start.6 = (bf16[4,64,1024]{2,1,0:T(8,128)(2,1)S(1)}, bf16[4,64,1024]{2,1,0:T(8,128)(2,1)S(1)}, u32[]{:S(2)}, u32[]{:S(2)}) collective-permute-start(bf16[4,64,1024]{2,1,0:T(8,128)(2,1)S(1)} %pad_maximum_fusion.refs_0_), channel_id=1, source_target_pairs={{0,96},{8,104},{16,112},{24,120},{32,0},{40,8},{48,16},{56,24},{64... | collective-permute-start | bytes 1572872 | tf_op jit(solution)/shard_map/ppermute | solution.py:338
  30.3 15.3 %collective-permute-start.4 = (bf16[4,64,1024]{2,1,0:T(8,128)(2,1)S(1)}, bf16[4,64,1024]{2,1,0:T(8,128)(2,1)S(1)}, u32[]{:S(2)}, u32[]{:S(2)}) collective-permute-start(bf16[4,64,1024]{2,1,0:T(8,128)(2,1)S(1)} %pad_maximum_fusion.refs_0_), channel_id=1, source_target_pairs={{0,32},{8,40},{16,48},{24,56},{32,64},{40,72},{48,80},{56,88},{64,... | collective-permute-start | bytes 1572872 | tf_op jit(solution)/shard_map/ppermute | solution.py:338
  30.3 15.3 %collective-permute-start.7 = (bf16[4,64,1024]{2,1,0:T(8,128)(2,1)S(1)}, bf16[4,64,1024]{2,1,0:T(8,128)(2,1)S(1)}, u32[]{:S(2)}, u32[]{:S(2)}) collective-permute-start(bf16[4,64,1024]{2,1,0:T(8,128)(2,1)S(1)} %pad_maximum_fusion.1.refs_1_), channel_id=1, source_target_pairs={{0,24},{8,0},{16,8},{24,16},{32,56},{40,32},{48,40},{56,48},{64,88... | collective-permute-start | bytes 1572872 | tf_op jit(solution)/shard_map/ppermute | solution.py:338
  30.7 15.0 %collective-permute-start.5 = (bf16[4,64,1024]{2,1,0:T(8,128)(2,1)S(1)}, bf16[4,64,1024]{2,1,0:T(8,128)(2,1)S(1)}, u32[]{:S(2)}, u32[]{:S(2)}) collective-permute-start(bf16[4,64,1024]{2,1,0:T(8,128)(2,1)S(1)} %pad_maximum_fusion.1.refs_1_), channel_id=1, source_target_pairs={{0,8},{8,16},{16,24},{24,0},{32,40},{40,48},{48,56},{56,32},{64,72... | collective-permute-start | bytes 1572872 | tf_op jit(solution)/shard_map/ppermute | solution.py:338
  45.7 15.6 %collective-permute-start.9 = (bf16[4,64,1024]{2,1,0:T(8,128)(2,1)S(1)}, bf16[4,64,1024]{2,1,0:T(8,128)(2,1)S(1)}, u32[]{:S(2)}, u32[]{:S(2)}) collective-permute-start(bf16[4,64,1024]{2,1,0:T(8,128)(2,1)S(1)} %collective-permute-done.4.refs_0_), channel_id=1, source_target_pairs={{0,32},{8,40},{16,48},{24,56},{32,64},{40,72},{48,80},{56,88},{64,... | collective-permute-start | bytes 1572872 | tf_op jit(solution)/shard_map/ppermute | solution.py:338
  46.5 14.8 %collective-permute-start.10 = (bf16[4,64,1024]{2,1,0:T(8,128)(2,1)S(1)}, bf16[4,64,1024]{2,1,0:T(8,128)(2,1)S(1)}, u32[]{:S(2)}, u32[]{:S(2)}) collective-permute-start(bf16[4,64,1024]{2,1,0:T(8,128)(2,1)S(1)} %collective-permute-done.5.refs_1_), channel_id=1, source_target_pairs={{0,8},{8,16},{16,24},{24,0},{32,40},{40,48},{48,56},{56,32},{64,72... | collective-permute-start | bytes 1572872 | tf_op jit(solution)/shard_map/ppermute | solution.py:338
  46.5 2.2 %copy-start = (bf16[1,8192,256]{2,1,0:T(8,128)(2,1)S(1)}, bf16[1,8192,256]{2,1,0:T(8,128)(2,1)}, u32[]{:S(2)}) copy-start(bf16[1,8192,256]{2,1,0:T(8,128)(2,1)} %param.5) | copy-start | bytes 12582916
  54.0 41.9 %collective-permute-start.8 = (bf16[4,144,512]{2,1,0:T(8,128)(2,1)S(1)}, bf16[4,144,512]{2,1,0:T(8,128)(2,1)S(1)}, u32[]{:S(2)}, u32[]{:S(2)}) collective-permute-start(bf16[4,144,512]{2,1,0:T(8,128)(2,1)S(1)} %get-tuple-element.39), channel_id=1, source_target_pairs={{0,32},{8,40},{16,48},{24,56},{32,64},{40,72},{48,80},{56,88},{64,... | collective-permute-start | bytes 1769480 | tf_op jit(solution)/shard_map/ppermute | solution.py:338
  57.9 38.0 %collective-permute-start.14 = (bf16[4,144,512]{2,1,0:T(8,128)(2,1)S(1)}, bf16[4,144,512]{2,1,0:T(8,128)(2,1)S(1)}, u32[]{:S(2)}, u32[]{:S(2)}) collective-permute-start(bf16[4,144,512]{2,1,0:T(8,128)(2,1)S(1)} %get-tuple-element.48), channel_id=1, source_target_pairs={{0,8},{8,16},{16,24},{24,0},{32,40},{40,48},{48,56},{56,32},{64,72... | collective-permute-start | bytes 1769480 | tf_op jit(solution)/shard_map/ppermute | solution.py:338
  72.5 12.8 %collective-permute-start.11 = (bf16[4,144,512]{2,1,0:T(8,128)(2,1)S(1)}, bf16[4,144,512]{2,1,0:T(8,128)(2,1)S(1)}, u32[]{:S(2)}, u32[]{:S(2)}) collective-permute-start(bf16[4,144,512]{2,1,0:T(8,128)(2,1)S(1)} %get-tuple-element.43), channel_id=1, source_target_pairs={{0,96},{8,104},{16,112},{24,120},{32,0},{40,8},{48,16},{56,24},{64... | collective-permute-start | bytes 1769480 | tf_op jit(solution)/shard_map/ppermute | solution.py:338
  72.6 15.8 %copy-start.1 = (bf16[1,8192,256]{2,1,0:T(8,128)(2,1)S(1)}, bf16[1,8192,256]{2,1,0:T(8,128)(2,1)}, u32[]{:S(2)}) copy-start(bf16[1,8192,256]{2,1,0:T(8,128)(2,1)} %param.5) | copy-start | bytes 12582916
  72.6 12.7 %collective-permute-start.12 = (bf16[4,144,512]{2,1,0:T(8,128)(2,1)S(1)}, bf16[4,144,512]{2,1,0:T(8,128)(2,1)S(1)}, u32[]{:S(2)}, u32[]{:S(2)}) collective-permute-start(bf16[4,144,512]{2,1,0:T(8,128)(2,1)S(1)} %get-tuple-element.45), channel_id=1, source_target_pairs={{0,24},{8,0},{16,8},{24,16},{32,56},{40,32},{48,40},{56,48},{64,88... | collective-permute-start | bytes 1769480 | tf_op jit(solution)/shard_map/ppermute | solution.py:338
  85.7 11.6 %collective-permute-start.13 = (bf16[4,144,512]{2,1,0:T(8,128)(2,1)S(1)}, bf16[4,144,512]{2,1,0:T(8,128)(2,1)S(1)}, u32[]{:S(2)}, u32[]{:S(2)}) collective-permute-start(bf16[4,144,512]{2,1,0:T(8,128)(2,1)S(1)} %get-tuple-element.46), channel_id=1, source_target_pairs={{0,96},{8,104},{16,112},{24,120},{32,0},{40,8},{48,16},{56,24},{64... | collective-permute-start | bytes 1769480 | tf_op jit(solution)/shard_map/ppermute | solution.py:338
  86.7 11.2 %collective-permute-start.15 = (bf16[4,144,512]{2,1,0:T(8,128)(2,1)S(1)}, bf16[4,144,512]{2,1,0:T(8,128)(2,1)S(1)}, u32[]{:S(2)}, u32[]{:S(2)}) collective-permute-start(bf16[4,144,512]{2,1,0:T(8,128)(2,1)S(1)} %get-tuple-element.49), channel_id=1, source_target_pairs={{0,24},{8,0},{16,8},{24,16},{32,56},{40,32},{48,40},{56,48},{64,88... | collective-permute-start | bytes 1769480 | tf_op jit(solution)/shard_map/ppermute | solution.py:338
  98.6 8.4 %collective-permute-start.16 = (bf16[2,144,512]{2,1,0:T(8,128)(2,1)S(1)}, bf16[2,144,512]{2,1,0:T(8,128)(2,1)S(1)}, u32[]{:S(2)}, u32[]{:S(2)}) collective-permute-start(bf16[2,144,512]{2,1,0:T(8,128)(2,1)S(1)} %get-tuple-element.51), channel_id=1, source_target_pairs={{0,24},{8,16},{16,8},{24,0},{32,56},{40,48},{48,40},{56,32},{64,88... | collective-permute-start | bytes 884744 | tf_op jit(solution)/shard_map/ppermute | solution.py:341
  102.3 7.9 %collective-permute-start.17 = (bf16[2,144,512]{2,1,0:T(8,128)(2,1)S(1)}, bf16[2,144,512]{2,1,0:T(8,128)(2,1)S(1)}, u32[]{:S(2)}, u32[]{:S(2)}) collective-permute-start(bf16[2,144,512]{2,1,0:T(8,128)(2,1)S(1)} %get-tuple-element.53), channel_id=1, source_target_pairs={{0,96},{8,104},{16,112},{24,120},{32,64},{40,72},{48,80},{56,88},{... | collective-permute-start | bytes 884744 | tf_op jit(solution)/shard_map/ppermute | solution.py:341
  110.5 5.2 %collective-permute-start.18 = (bf16[1,144,512]{2,1,0:T(8,128)(2,1)S(1)}, bf16[1,144,512]{2,1,0:T(8,128)(2,1)S(1)}, u32[]{:S(2)}, u32[]{:S(2)}) collective-permute-start(bf16[1,144,512]{2,1,0:T(8,128)(2,1)S(1)} %get-tuple-element.55), channel_id=1, source_target_pairs={{0,8},{8,0},{16,24},{24,16},{32,40},{40,32},{48,56},{56,48},{64,72... | collective-permute-start | bytes 442376 | tf_op jit(solution)/shard_map/ppermute | solution.py:341
  110.6 5.2 %collective-permute-start.19 = (bf16[1,144,512]{2,1,0:T(8,128)(2,1)S(1)}, bf16[1,144,512]{2,1,0:T(8,128)(2,1)S(1)}, u32[]{:S(2)}, u32[]{:S(2)}) collective-permute-start(bf16[1,144,512]{2,1,0:T(8,128)(2,1)S(1)} %get-tuple-element.57), channel_id=1, source_target_pairs={{0,32},{8,40},{16,48},{24,56},{32,0},{40,8},{48,16},{56,24},{64,96... | collective-permute-start | bytes 442376 | tf_op jit(solution)/shard_map/ppermute | solution.py:341
  116.0 1.6 %collective-permute-start.20 = (bf16[128,1024]{1,0:T(8,128)(2,1)S(1)}, bf16[128,1024]{1,0:T(8,128)(2,1)S(1)}, u32[]{:S(2)}, u32[]{:S(2)}) collective-permute-start(bf16[128,1024]{1,0:T(8,128)(2,1)S(1)} %final.1.att_ref), channel_id=1, source_target_pairs={{0,1},{1,0},{2,3},{3,2},{4,5},{5,4},{6,7},{7,6},{8,9},{9,8},{10,11... | collective-permute-start | bytes 786440 | tf_op jit(solution)/shard_map/ppermute | solution.py:344
  120.6 15.2 %collective-permute-start.22 = (bf16[128,1024]{1,0:T(8,128)(2,1)S(1)}, bf16[128,1024]{1,0:T(8,128)(2,1)S(1)}, u32[]{:S(2)}, u32[]{:S(2)}) collective-permute-start(bf16[128,1024]{1,0:T(8,128)(2,1)S(1)} %project.5), channel_id=1, source_target_pairs={{0,2},{1,3},{2,4},{3,5},{4,6},{5,7},{6,0},{7,1},{8,10},{9,11},{10,... | collective-permute-start | bytes 786440 | tf_op jit(solution)/shard_map/ppermute | solution.py:344
  125.3 11.8 %collective-permute-start.23 = (bf16[128,1024]{1,0:T(8,128)(2,1)S(1)}, bf16[128,1024]{1,0:T(8,128)(2,1)S(1)}, u32[]{:S(2)}, u32[]{:S(2)}) collective-permute-start(bf16[128,1024]{1,0:T(8,128)(2,1)S(1)} %project.6), channel_id=1, source_target_pairs={{0,4},{1,5},{2,6},{3,7},{4,0},{5,1},{6,2},{7,3},{8,12},{9,13},{10,... | collective-permute-start | bytes 786440 | tf_op jit(solution)/shard_map/ppermute | solution.py:344
  131.3 8.3 %collective-permute-start.24 = (bf16[128,1024]{1,0:T(8,128)(2,1)S(1)}, bf16[128,1024]{1,0:T(8,128)(2,1)S(1)}, u32[]{:S(2)}, u32[]{:S(2)}) collective-permute-start(bf16[128,1024]{1,0:T(8,128)(2,1)S(1)} %project.7), channel_id=1, source_target_pairs={{0,6},{1,7},{2,0},{3,1},{4,2},{5,3},{6,4},{7,5},{8,14},{9,15},{10,... | collective-permute-start | bytes 786440 | tf_op jit(solution)/shard_map/ppermute | solution.py:344

commit v3 on v2

v3 whole, which is shorter than its diff:
```python
import functools
import math

import jax
import jax.numpy as jnp
from jax import lax
from jax.experimental import pallas as pl
from jax.experimental.pallas import tpu as pltpu
from jax.sharding import PartitionSpec as P

BLK = 64
MOST = 16
HD = 128
GROUP = 8
ROWS = BLK * GROUP
CHUNK = 4
FLIPS = (0, 1, 3, 2)
PAY = HD + 16
NEG = -1e30
SCALE = 1.0 / math.sqrt(HD)
LOG2E = math.log2(math.e)
BF = jnp.bfloat16
F32 = jnp.float32
COST = 4 * 10**9
VMEM_SOME = 16 * 2**20


def seq_shift(dz, dx):
    return [(z * 4 + x, ((z + dz) % 4) * 4 + (x + dx) % 4) for z in range(4) for x in range(4)]


def seq_flip(fz, fx):
    return [(z * 4 + x, (z ^ fz) * 4 + (x ^ fx)) for z in range(4) for x in range(4)]


def kvh_shift(dy, dc):
    return [(y * 2 + c, ((y + dy) % 4) * 2 + (c + dc) % 2) for y in range(4) for c in range(2)]


def pack(numer, peak, total):
    high = total.astype(BF).astype(F32)
    low = total - high
    row = lax.broadcasted_iota(jnp.int32, (16, ROWS), 0)
    tail = jnp.where(row == 0, peak, jnp.where(row == 1, high, jnp.where(row == 2, low, 0.0)))
    return numer, tail


def attend_kernel(place_ref, count_ref, ids_ref, kv_ref, *refs, far, cut):
    parts, per = 2, 4
    q_refs, refs = refs[:parts], refs[parts:]
    out_refs, refs = refs[: parts * cut], refs[parts * cut :]
    q_scr, o_scr, s_scr, diag_scr = refs
    total = parts * per
    pairs = total // 2
    step = CHUNK * BLK

    place = place_ref[0]
    z, x = place // 4, place % 4

    def qb_of(t):
        j = t % per
        f = j ^ (j // 2)
        qa = 2 * (((z + 4 - far) % 4) * 4 + (x ^ f))
        qb = 2 * ((z ^ f) * 4 + (x + 4 - far) % 4) + 1
        return jnp.where(t < per, qa, qb)

    def size(p):
        most = jnp.maximum(count_ref[qb_of(2 * p)], count_ref[qb_of(2 * p + 1)])
        return jnp.where(most <= CHUNK, 1, jnp.where(most <= 2 * CHUNK, 2, MOST // CHUNK))

    off = lax.broadcasted_iota(jnp.int32, (BLK, ROWS), 0)
    tok = lax.broadcasted_iota(jnp.int32, (BLK, ROWS), 1) % BLK
    diag_scr[...] = jnp.where((off > tok) & (place_ref[2] == 1), NEG, 0.0)
    for i, q_ref in enumerate(q_refs):
        q_scr[i * per : (i + 1) * per] = q_ref[...]

    def work(p, chunks):
        qbs = [qb_of(2 * p + u) for u in range(2)]
        counts = [count_ref[qb] for qb in qbs]

        def fetch(u, c, lo):
            ids = [ids_ref[qbs[u] * MOST + c * CHUNK + v] for v in range(CHUNK)]
            return jnp.concatenate(
                [kv_ref[pl.ds(pl.multiple_of(i * BLK, BLK), BLK), lo : lo + HD] for i in ids], axis=0
            )

        peaks = []
        for u in range(2):
            q = jnp.concatenate([q_scr[2 * p + u, :, g * HD : (g + 1) * HD] for g in range(GROUP)], axis=0)
            peak = None
            for c in range(chunks):
                s = lax.dot_general(
                    fetch(u, c, 0),
                    q,
                    (((1,), (1,)), ((), ())),
                    preferred_element_type=F32,
                )
                for v in range(CHUNK):
                    at = c * CHUNK + v
                    part = s[v * BLK : (v + 1) * BLK]
                    if at == 0:
                        part = part + diag_scr[...]
                    else:
                        part = part + jnp.where(at < counts[u], 0.0, NEG)
                    s_scr[u, at * BLK : (at + 1) * BLK, :] = part
                    part = jnp.max(part.reshape(BLK // 8, 8, ROWS), axis=0)
                    peak = part if peak is None else jnp.maximum(peak, part)
            peaks.append(jnp.max(peak, axis=0, keepdims=True))
        for u in range(2):
            peak = peaks[u]
            numer, mass = None, None
            for c in range(chunks):
                w = jnp.exp2((s_scr[u, c * step : (c + 1) * step, :] - peak) * (SCALE * LOG2E))
                part = lax.dot_general(
                    fetch(u, c, HD),
                    w.astype(BF),
                    (((0,), (0,)), ((), ())),
                    preferred_element_type=F32,
                )
                numer = part if numer is None else numer + part
                part = jnp.sum(w.reshape(step // 8, 8, ROWS), axis=0)
                mass = part if mass is None else mass + part
            mass = jnp.sum(mass, axis=0, keepdims=True)
            used = counts[u] > 0
            scaled = peak * SCALE
            near = scaled.astype(BF).astype(F32)
            gain = jnp.where(used, jnp.exp2((scaled - near) * LOG2E), 0.0)
            near = jnp.where(used, near, NEG)
            numer, mass = numer * gain, mass * gain
            numer, tail = pack(numer, near, mass)
            o_scr[2 * p + u, :HD] = numer.astype(o_scr.dtype)
            o_scr[2 * p + u, HD:] = tail.astype(o_scr.dtype)

    def one(p, carry):
        have = size(p)
        for chunks in (1, 2, MOST // CHUNK):

            @pl.when(have == chunks)
            def _(chunks=chunks):
                work(p, chunks)

        return carry

    lax.fori_loop(0, pairs, one, 0)
    for i, out_ref in enumerate(out_refs):
        out_ref[...] = o_scr[i * per // cut : (i + 1) * per // cut]


VM = pl.BlockSpec(memory_space=pltpu.VMEM)
SM = pl.BlockSpec(memory_space=pltpu.SMEM)


HB = pl.BlockSpec(memory_space=pltpu.HBM)
WIDE = 1024


def attend(place, counts, ids, kv, arrays, far, dtype, cut):
    parts, per = 2, 4
    total = parts * per
    return pl.pallas_call(
        functools.partial(attend_kernel, far=far, cut=cut),
        out_shape=[jax.ShapeDtypeStruct((per // cut, PAY, ROWS), dtype)] * (parts * cut),
        in_specs=[SM, SM, SM, VM] + [VM] * parts,
        out_specs=[VM] * (parts * cut),
        scratch_shapes=[
            pltpu.VMEM((total, BLK, GROUP * HD), BF),
            pltpu.VMEM((total, PAY, ROWS), dtype),
            pltpu.VMEM((2, MOST * BLK, ROWS), F32),
            pltpu.VMEM((BLK, ROWS), F32),
        ],
        compiler_params=pltpu.CompilerParams(vmem_limit_bytes=VMEM_SOME),
        cost_estimate=pl.CostEstimate(flops=COST, bytes_accessed=2**20, transcendentals=0),
        name="attend",
    )(place, counts, ids, kv, *arrays)


def merge(blocks):
    tails = [b[HD:].astype(F32) for b in blocks]
    peaks = [t[0:1] for t in tails]
    top = functools.reduce(jnp.maximum, peaks)
    gains = [jnp.exp2((p - top) * LOG2E) for p in peaks]
    numer = sum(b[:HD].astype(F32) * g for b, g in zip(blocks, gains))
    total = sum((t[1:2] + t[2:3]) * g for t, g in zip(tails, gains))
    return numer, top, total


def store(out, at, numer, peak, total):
    numer, tail = pack(numer, peak, total)
    out[at, :HD] = numer.astype(out.dtype)
    out[at, HD:] = tail.astype(out.dtype)


def join_kernel(*refs):
    ins, outs = refs[:8], refs[8:]
    for half in range(2):
        low, high, far_lo, far_hi = ins[half * 4 : half * 4 + 4]
        low_out, high_out = outs[half * 2 : half * 2 + 2]
        for slot in range(4):
            store(low_out, slot, *merge([low[slot], far_lo[slot]] if slot < 2 else [low[slot]]))
            store(high_out, slot, *merge([high[slot], far_hi[slot - 2]] if slot > 1 else [high[slot]]))


def stage_kernel(*refs):
    ins, outs = refs[:6], refs[6:]
    for half in range(2):
        for slot in range(4):
            store(outs[half * 4 + slot], 0, *merge([r[slot] for r in ins[half * 3 : half * 3 + 3]]))


def final_kernel(*refs):
    ins, out = refs[:8], refs[8]
    for half in range(2):
        numer, _, total = merge([r[0] for r in ins[half * 4 : half * 4 + 4]])
        att = numer / total
        for g in range(0, GROUP, 2):
            turned = att[:, g * BLK : (g + 2) * BLK].T.astype(BF)
            out[half * BLK : (half + 1) * BLK, g * HD : (g + 1) * HD] = turned[:BLK]
            out[half * BLK : (half + 1) * BLK, (g + 1) * HD : (g + 2) * HD] = turned[BLK:]


def local_call(kernel, out_shape, args, name):
    return pl.pallas_call(
        kernel,
        out_shape=out_shape,
        in_specs=[VM] * len(args),
        out_specs=jax.tree.map(lambda _: VM, out_shape),
        compiler_params=pltpu.CompilerParams(vmem_limit_bytes=VMEM_SOME),
        cost_estimate=pl.CostEstimate(flops=10**7, bytes_accessed=2 * 2**20, transcendentals=0),
        name=name,
    )(*args)


def project_kernel(place_ref, att_ref, other_ref, w_ref, wo_ref, *refs, fars):
    out_refs, (wo_scr, sems) = refs[: len(fars)], refs[len(fars) :]
    k = place_ref[1]
    cols = [pl.ds(pl.multiple_of((2 * ((k // 2 + far) % 4) + k % 2) * WIDE, WIDE), WIDE) for far in fars]
    copies = [pltpu.make_async_copy(wo_ref.at[:, c], wo_scr.at[n], sems.at[n]) for n, c in enumerate(cols)]
    for copy in copies:
        copy.start()
    for c, copy, wo, out_ref in zip(cols, copies, range(len(fars)), out_refs):
        value = jnp.dot(att_ref[...], w_ref[:, c], preferred_element_type=F32)
        copy.wait()
        value = value + jnp.dot(other_ref[...], wo_scr[wo], preferred_element_type=F32)
        out_ref[...] = value.astype(out_ref.dtype)


def project(place, att, other, w, wo, fars, dtypes):
    rows, depth = att.shape
    return pl.pallas_call(
        functools.partial(project_kernel, fars=fars),
        out_shape=[jax.ShapeDtypeStruct((rows, WIDE), t) for t in dtypes],
        in_specs=[SM, VM, VM, VM, HB],
        out_specs=[VM] * len(fars),
        scratch_shapes=[
            pltpu.VMEM((len(fars), depth, WIDE), BF),
            pltpu.SemaphoreType.DMA((len(fars),)),
        ],
        compiler_params=pltpu.CompilerParams(vmem_limit_bytes=30 * 2**20),
        cost_estimate=pl.CostEstimate(flops=2 * 10**9 * len(fars), bytes_accessed=2**20, transcendentals=0),
        name="project",
    )(place, att, other, w, wo)


def body(queries, kv_cache, block_list, out_weight):
    s = lax.axis_index("seq")
    k = lax.axis_index("kvh")
    last = lax.axis_size("seq") - 1
    place = jnp.stack([s, k, jnp.where(s == last, 1, 0)]).astype(jnp.int32)
    kv = kv_cache[0]
    w = out_weight[0]
    block_count = kv.shape[0] // BLK
    qb_count = block_list.shape[0]

    def zx(v, dz, dx):
        return lax.ppermute(v, "seq", seq_shift(dz % 4, dx % 4))

    def flip(v, fz, fx):
        return lax.ppermute(v, "seq", seq_flip(fz, fx))

    def yc(v, dy, dc):
        return lax.ppermute(v, "kvh", kvh_shift(dy % 4, dc))

    w_other = yc(w, 0, 1)

    q = queries[:, 0, :].reshape(2, BLK, GROUP * HD)
    a, b = q[0:1], q[1:2]
    a, b = lax.optimization_barrier((jnp.concatenate([a, flip(a, 0, 1)]), jnp.concatenate([b, flip(b, 1, 0)])))
    a, b = lax.optimization_barrier((jnp.concatenate([a, flip(a, 0, 3)]), jnp.concatenate([b, flip(b, 3, 0)])))
    au, bu, ad, bd = lax.optimization_barrier((zx(a, 1, 0), zx(b, 0, 1), zx(a, -1, 0), zx(b, 0, -1)))
    af, bf = zx(au, 1, 0), zx(bu, 0, 1)

    own_ids = (last + 1) * block_count - qb_count + jnp.arange(qb_count, dtype=jnp.int32)
    diag_here = (s == last).astype(jnp.int32)
    mine = (block_list // block_count == s) & (block_list != own_ids[:, None])
    rank = jnp.cumsum(mine.astype(jnp.int32), axis=1) - 1 + diag_here
    counts = jnp.sum(mine.astype(jnp.int32), axis=1) + diag_here
    slots = jnp.arange(MOST, dtype=jnp.int32)
    hit = mine[:, :, None] & (rank[:, :, None] == slots[None, None, :])
    ids = jnp.sum(jnp.where(hit, (block_list % block_count)[:, :, None], 0), axis=1)
    ids = jnp.where((slots[None, :] == 0) & (diag_here == 1), (own_ids % block_count)[:, None], ids)
    ids = ids.reshape(-1)

    def run(pair, far, dtype, cut=1):
        return attend(place, counts, ids, kv, pair, far, dtype, cut)

    ra1, rb1 = run([au, bu], 1, F32)
    ra3, rb3 = run([ad, bd], 3, F32)
    ra2_lo, ra2_hi, rb2_lo, rb2_hi = run([af, bf], 2, BF, 2)
    ra2_lo, ra2_hi = zx(ra2_lo, -1, 0), zx(ra2_hi, 1, 0)
    rb2_lo, rb2_hi = zx(rb2_lo, 0, -1), zx(rb2_hi, 0, 1)
    ao, bo = run([a, b], 0, F32)
    b_four, b_one = (jax.ShapeDtypeStruct((n, PAY, ROWS), BF) for n in (4, 1))
    f_one = jax.ShapeDtypeStruct((1, PAY, ROWS), F32)
    ra1, ra3, rb1, rb3 = local_call(
        join_kernel, [b_four] * 4, [ra1, ra3, ra2_lo, ra2_hi, rb1, rb3, rb2_lo, rb2_hi], "join"
    )
    ra1, rb1, ra3, rb3 = zx(ra1, -1, 0), zx(rb1, 0, -1), zx(ra3, 1, 0), zx(rb3, 0, 1)
    stage_in = [ao, ra3, ra1, bo, rb3, rb1]
    m = local_call(stage_kernel, [f_one, b_one, b_one, b_one] * 2, stage_in, "stage")
    final_in = [m[0]] + [flip(m[n], 0, FLIPS[n]) for n in (1, 2, 3)]
    final_in += [m[4]] + [flip(m[4 + n], FLIPS[n], 0) for n in (1, 2, 3)]
    att = local_call(final_kernel, jax.ShapeDtypeStruct((2 * BLK, GROUP * HD), BF), final_in, "final")

    other = yc(att, 0, 1)

    (p2,) = project(place, att, other, w, w_other, (2,), (BF,))
    r2 = yc(p2, 2, 0)
    p1, p3, own = project(place, att, other, w, w_other, (1, 3, 0), (BF, BF, F32))
    r1, r3 = yc(p1, 1, 0), yc(p3, 3, 0)
    return own + r1.astype(F32) + r2.astype(F32) + r3.astype(F32)


def solution(mesh):
    in_specs = (P("seq", "kvh", None), P("kvh", "seq", None), P(), P("kvh", None, None))
    out_specs = P("seq", "kvh")
    return jax.shard_map(body, mesh=mesh, in_specs=in_specs, out_specs=out_specs, check_vma=False)
```

time: 142 us -> 124 us (0.87)
  Pallas kernels: 53.5 us -> 26.4 us
  starting transfers between devices: 33.3 us -> 40.7 us
    pallas_call x9 -> x6, Pallas kernels: 52 us -> 24.8 us  [the longest x4 17.2 us: attend(): pl.pallas_call(functools.partial(attend_kernel, far=far, cut=cut), out_sh...]
    ppermute x8 -> x10, waiting for transfers between devices: 21 us -> 14 us  [flip(): return lax.ppermute(v, 'seq', seq_flip(fz, fx))]
    ppermute x8 -> x10, starting transfers between devices: 13.4 us -> 18.2 us  [flip(): return lax.ppermute(v, 'seq', seq_flip(fz, fx))]
    ppermute x5, waiting for transfers between devices: 5.39 us -> 9.74 us  [yc(): return lax.ppermute(v, 'kvh', kvh_shift(dy % 4, dc))]
    ppermute x12 -> x14, starting transfers between devices: 13.7 us -> 16.9 us  [zx(): return lax.ppermute(v, 'seq', seq_shift(dz % 4, dx % 4))]
    ppermute x12 -> x14, waiting for transfers between devices: 21.6 us -> 24.1 us  [zx(): return lax.ppermute(v, 'seq', seq_shift(dz % 4, dx % 4))]
    unnamed x6 -> x20, local copies, waits for them, and re-layouts: 2.2 us -> 3.02 us
  transfers between devices with their start and end apart: 25 -> 29, of which waited for: 18 -> 20; matrix products, arithmetic and copies ran while one was open for 1% -> 3% of each run, Pallas kernels for 30% -> 18%
where the time goes in v3:
time: 124 us; the launch traced here: 122 us
  waiting for transfers between devices  47.8 us (39%)
  starting transfers between devices  40.7 us (33%)
  Pallas kernels  26.4 us (21%)
  local copies, waits for them, and re-layouts  4.09 us (3%)
  other arithmetic  2.99 us (2%)
    ppermute x14, waiting for transfers between devices, zx(): return lax.ppermute(v, 'seq', seq_shift(dz % 4, dx % 4))  24.1 us
    ppermute x10, starting transfers between devices, flip(): return lax.ppermute(v, 'seq', seq_flip(fz, fx))  18.2 us
    pallas_call x4, Pallas kernels, attend(): pl.pallas_call(functools.partial(attend_kernel, far=far, cut=cut), out_sh...  17.2 us
    ppermute x14, starting transfers between devices, zx(): return lax.ppermute(v, 'seq', seq_shift(dz % 4, dx % 4))  16.9 us
    ppermute x10, waiting for transfers between devices, flip(): return lax.ppermute(v, 'seq', seq_flip(fz, fx))  14 us
    ppermute x5, waiting for transfers between devices, yc(): return lax.ppermute(v, 'kvh', kvh_shift(dy % 4, dc))  9.74 us
    pallas_call x2, Pallas kernels, project(): pl.pallas_call(functools.partial(project_kernel, fars=fars), out_shape=[j...  7.57 us
    ppermute x5, starting transfers between devices, yc(): return lax.ppermute(v, 'kvh', kvh_shift(dy % 4, dc))  5.68 us
  transfers between devices with their start and end apart: 29, of which 20 were waited for; matrix products, arithmetic and copies ran while one was open for 3% of the time, Pallas kernels for 18%

profile of v3, /device:TPU:0, one launch (start us, length us, event | category | flops | bytes accessed | tf_op | source)
XLA Modules:
  0.0 122.3 jit_solution(11476338498754101527)
XLA Ops:
  0.0 1.0 slice_bitcast_fusion
  1.0 2.1 %collective-permute-start.1 = (bf16[1,64,1024]{2,1,0:T(8,128)(2,1)S(1)}, bf16[1,64,1024]{2,1,0:T(8,128)(2,1)S(1)}, u32[]{:S(2)}, u32[]{:S(2)}) collective-permute-start(bf16[1,64,1024]{2,1,0:T(8,128)(2,1)S(1)} %get-tuple-element.73), channel_id=1, source_target_pairs={{0,32},{8,40},{16,48},{24,56},{32,0},{40,8},{48,16},{56,24},{64,96... | collective-permute-start | bytes 393224 | tf_op jit(solution)/shard_map/ppermute | solution.py:278
  3.1 1.5 %collective-permute-start = (bf16[1,64,1024]{2,1,0:T(8,128)(2,1)S(1)}, bf16[1,64,1024]{2,1,0:T(8,128)(2,1)S(1)}, u32[]{:S(2)}, u32[]{:S(2)}) collective-permute-start(bf16[1,64,1024]{2,1,0:T(8,128)(2,1)S(1)} %get-tuple-element.74), channel_id=1, source_target_pairs={{0,8},{8,0},{16,24},{24,16},{32,40},{40,32},{48,56},{56,48},{64,72... | collective-permute-start | bytes 393224 | tf_op jit(solution)/shard_map/ppermute | solution.py:278
  4.6 0.8 fusion.5
  5.4 1.9 %collective-permute-done.1 = bf16[1,64,1024]{2,1,0:T(8,128)(2,1)S(1)} collective-permute-done((bf16[1,64,1024]{2,1,0:T(8,128)(2,1)S(1)}, bf16[1,64,1024]{2,1,0:T(8,128)(2,1)S(1)}, u32[]{:S(2)}, u32[]{:S(2)}) %collective-permute-start.1) | collective-permute-done | bytes 131104 | tf_op jit(solution)/shard_map/ppermute | solution.py:278
  7.3 1.4 %collective-permute-done = bf16[1,64,1024]{2,1,0:T(8,128)(2,1)S(1)} collective-permute-done((bf16[1,64,1024]{2,1,0:T(8,128)(2,1)S(1)}, bf16[1,64,1024]{2,1,0:T(8,128)(2,1)S(1)}, u32[]{:S(2)}, u32[]{:S(2)}) %collective-permute-start) | collective-permute-done | bytes 131104 | tf_op jit(solution)/shard_map/ppermute | solution.py:278
  8.7 2.8 %collective-permute-start.2 = (bf16[2,64,1024]{2,1,0:T(8,128)(2,1)S(1)}, bf16[2,64,1024]{2,1,0:T(8,128)(2,1)S(1)}, u32[]{:S(2)}, u32[]{:S(2)}) collective-permute-start(bf16[2,64,1024]{2,1,0:T(8,128)(2,1)S(1)} %pad_maximum_fusion.2), channel_id=1, source_target_pairs={{0,24},{8,16},{16,8},{24,0},{32,56},{40,48},{48,40},{56,32},{64,88... | collective-permute-start | bytes 786440 | tf_op jit(solution)/shard_map/ppermute | solution.py:278
  11.6 2.5 %collective-permute-start.3 = (bf16[2,64,1024]{2,1,0:T(8,128)(2,1)S(1)}, bf16[2,64,1024]{2,1,0:T(8,128)(2,1)S(1)}, u32[]{:S(2)}, u32[]{:S(2)}) collective-permute-start(bf16[2,64,1024]{2,1,0:T(8,128)(2,1)S(1)} %pad_maximum_fusion.3), channel_id=1, source_target_pairs={{0,96},{8,104},{16,112},{24,120},{32,64},{40,72},{48,80},{56,88},{... | collective-permute-start | bytes 786440 | tf_op jit(solution)/shard_map/ppermute | solution.py:278
  14.4 3.2 %collective-permute-done.2 = bf16[2,64,1024]{2,1,0:T(8,128)(2,1)S(1)} collective-permute-done((bf16[2,64,1024]{2,1,0:T(8,128)(2,1)S(1)}, bf16[2,64,1024]{2,1,0:T(8,128)(2,1)S(1)}, u32[]{:S(2)}, u32[]{:S(2)}) %collective-permute-start.2) | collective-permute-done | bytes 262176 | tf_op jit(solution)/shard_map/ppermute | solution.py:278
  17.7 2.4 %collective-permute-done.3 = bf16[2,64,1024]{2,1,0:T(8,128)(2,1)S(1)} collective-permute-done((bf16[2,64,1024]{2,1,0:T(8,128)(2,1)S(1)}, bf16[2,64,1024]{2,1,0:T(8,128)(2,1)S(1)}, u32[]{:S(2)}, u32[]{:S(2)}) %collective-permute-start.3) | collective-permute-done | bytes 262176 | tf_op jit(solution)/shard_map/ppermute | solution.py:278
  20.2 2.8 %collective-permute-start.6 = (bf16[4,64,1024]{2,1,0:T(8,128)(2,1)S(1)}, bf16[4,64,1024]{2,1,0:T(8,128)(2,1)S(1)}, u32[]{:S(2)}, u32[]{:S(2)}) collective-permute-start(bf16[4,64,1024]{2,1,0:T(8,128)(2,1)S(1)} %pad_maximum_fusion.refs_0_), channel_id=1, source_target_pairs={{0,96},{8,104},{16,112},{24,120},{32,0},{40,8},{48,16},{56,24},{64... | collective-permute-start | bytes 1572872 | tf_op jit(solution)/shard_map/ppermute | solution.py:275
  23.5 1.5 %collective-permute-start.5 = (bf16[4,64,1024]{2,1,0:T(8,128)(2,1)S(1)}, bf16[4,64,1024]{2,1,0:T(8,128)(2,1)S(1)}, u32[]{:S(2)}, u32[]{:S(2)}) collective-permute-start(bf16[4,64,1024]{2,1,0:T(8,128)(2,1)S(1)} %pad_maximum_fusion.1.refs_1_), channel_id=1, source_target_pairs={{0,8},{8,16},{16,24},{24,0},{32,40},{40,48},{48,56},{56,32},{64,72... | collective-permute-start | bytes 1572872 | tf_op jit(solution)/shard_map/ppermute | solution.py:275
  25.1 0.8 copy-done.2
  26.6 6.3 %collective-permute-done.6.refs_0_ = bf16[4,64,1024]{2,1,0:T(8,128)(2,1)S(1)} collective-permute-done((bf16[4,64,1024]{2,1,0:T(8,128)(2,1)S(1)}, bf16[4,64,1024]{2,1,0:T(8,128)(2,1)S(1)}, u32[]{:S(2)}, u32[]{:S(2)}) %collective-permute-start.6) | collective-permute-done | bytes 524320 | tf_op jit(solution)/shard_map/ppermute | solution.py:275
  32.8 3.4 %collective-permute-done.4.refs_0_ = bf16[4,64,1024]{2,1,0:T(8,128)(2,1)S(1)} collective-permute-done((bf16[4,64,1024]{2,1,0:T(8,128)(2,1)S(1)}, bf16[4,64,1024]{2,1,0:T(8,128)(2,1)S(1)}, u32[]{:S(2)}, u32[]{:S(2)}) %collective-permute-start.4) | collective-permute-done | bytes 524320 | tf_op jit(solution)/shard_map/ppermute | solution.py:275
  36.6 1.2 collective-permute-start.8
  37.9 2.2 %copy-done.4 = bf16[1,8192,256]{2,1,0:T(8,128)(2,1)S(1)} copy-done((bf16[1,8192,256]{2,1,0:T(8,128)(2,1)S(1)}, bf16[1,8192,256]{2,1,0:T(8,128)(2,1)}, u32[]{:S(2)}) %copy-start.4) | copy-done | bytes 4194328
  40.1 3.5 %attend.5 = (f32[4,144,512]{2,1,0:T(8,128)S(1)}, f32[4,144,512]{2,1,0:T(8,128)S(1)}) custom-call(s32[3]{0:T(128)S(1)} %pad_add_fusion.place_ref, s32[32]{0:T(128)S(1)} %broadcast_add_fusion.count_ref, s32[512]{0:T(512)S(1)} %select_n.44.ids_ref, bf16[8192,256]{1,0:T(8,128)(2,1)S(1)} %bitcast.14, bf16[4,64,1024]{2,1,0:T(8,128)(2,1)S(1)} %collective-permute-done.4.refs_0_, ...), custom_call_target="tpu_custom_call" | custom-call | flops 4000000000 | bytes 1048576 | tf_op jit(solution)/shard_map/attend/pallas_call | solution.py:160
  43.7 5.1 %collective-permute-done.8.refs_0_ = bf16[4,64,1024]{2,1,0:T(8,128)(2,1)S(1)} collective-permute-done((bf16[4,64,1024]{2,1,0:T(8,128)(2,1)S(1)}, bf16[4,64,1024]{2,1,0:T(8,128)(2,1)S(1)}, u32[]{:S(2)}, u32[]{:S(2)}) %collective-permute-start.8) | collective-permute-done | bytes 524320 | tf_op jit(solution)/shard_map/ppermute | solution.py:275
  48.8 0.8 collective-permute-done.9.refs_1_
  49.6 4.2 %attend.7 = (bf16[2,144,512]{2,1,0:T(8,128)(2,1)S(1)}, bf16[2,144,512]{2,1,0:T(8,128)(2,1)S(1)}, bf16[2,144,512]{2,1,0:T(8,128)(2,1)S(1)}, bf16[2,144,512]{2,1,0:T(8,128)(2,1)S(1)}) custom-call(s32[3]{0:T(128)S(1)} %pad_add_fusion.place_ref, s32[32]{0:T(128)S(1)} %broadcast_add_fusion.count_ref, s32[512]{0:T(512)S(1)} %select_n.44.ids_ref, ...), custom_call_target="tpu_custom_call" | custom-call | flops 4000000000 | bytes 1048576 | tf_op jit(solution)/shard_map/attend/pallas_call | solution.py:160
  53.9 2.3 %collective-permute-start.10 = (bf16[2,144,512]{2,1,0:T(8,128)(2,1)S(1)}, bf16[2,144,512]{2,1,0:T(8,128)(2,1)S(1)}, u32[]{:S(2)}, u32[]{:S(2)}) collective-permute-start(bf16[2,144,512]{2,1,0:T(8,128)(2,1)S(1)} %get-tuple-element.49), channel_id=1, source_target_pairs={{0,96},{8,104},{16,112},{24,120},{32,0},{40,8},{48,16},{56,24},{64... | collective-permute-start | bytes 884744 | tf_op jit(solution)/shard_map/ppermute | solution.py:275
  56.3 1.9 %collective-permute-start.13 = (bf16[2,144,512]{2,1,0:T(8,128)(2,1)S(1)}, bf16[2,144,512]{2,1,0:T(8,128)(2,1)S(1)}, u32[]{:S(2)}, u32[]{:S(2)}) collective-permute-start(bf16[2,144,512]{2,1,0:T(8,128)(2,1)S(1)} %get-tuple-element.54), channel_id=1, source_target_pairs={{0,8},{8,16},{16,24},{24,0},{32,40},{40,48},{48,56},{56,32},{64,72... | collective-permute-start | bytes 884744 | tf_op jit(solution)/shard_map/ppermute | solution.py:275
  58.2 3.8 %attend.6 = (f32[4,144,512]{2,1,0:T(8,128)S(1)}, f32[4,144,512]{2,1,0:T(8,128)S(1)}) custom-call(s32[3]{0:T(128)S(1)} %pad_add_fusion.place_ref, s32[32]{0:T(128)S(1)} %broadcast_add_fusion.count_ref, s32[512]{0:T(512)S(1)} %select_n.44.ids_ref, bf16[8192,256]{1,0:T(8,128)(2,1)S(1)} %bitcast.16, bf16[4,64,1024]{2,1,0:T(8,128)(2,1)S(1)} %collective-permute-done.6.refs_0_, ...), custom_call_target="tpu_custom_call" | custom-call | flops 4000000000 | bytes 1048576 | tf_op jit(solution)/shard_map/attend/pallas_call | solution.py:160
  62.1 2.7 %collective-permute-done.11.refs_3_ = bf16[2,144,512]{2,1,0:T(8,128)(2,1)S(1)} collective-permute-done((bf16[2,144,512]{2,1,0:T(8,128)(2,1)S(1)}, bf16[2,144,512]{2,1,0:T(8,128)(2,1)S(1)}, u32[]{:S(2)}, u32[]{:S(2)}) %collective-permute-start.11) | collective-permute-done | bytes 294944 | tf_op jit(solution)/shard_map/ppermute | solution.py:275
  65.4 1.4 %collective-permute-start.14 = (bf16[4,144,512]{2,1,0:T(8,128)(2,1)S(1)}, bf16[4,144,512]{2,1,0:T(8,128)(2,1)S(1)}, u32[]{:S(2)}, u32[]{:S(2)}) collective-permute-start(bf16[4,144,512]{2,1,0:T(8,128)(2,1)S(1)} %get-tuple-element.55), channel_id=1, source_target_pairs={{0,32},{8,40},{16,48},{24,56},{32,64},{40,72},{48,80},{56,88},{64,... | collective-permute-start | bytes 1769480 | tf_op jit(solution)/shard_map/ppermute | solution.py:275
  66.8 1.9 %collective-permute-start.15 = (bf16[4,144,512]{2,1,0:T(8,128)(2,1)S(1)}, bf16[4,144,512]{2,1,0:T(8,128)(2,1)S(1)}, u32[]{:S(2)}, u32[]{:S(2)}) collective-permute-start(bf16[4,144,512]{2,1,0:T(8,128)(2,1)S(1)} %get-tuple-element.56), channel_id=1, source_target_pairs={{0,96},{8,104},{16,112},{24,120},{32,0},{40,8},{48,16},{56,24},{64... | collective-permute-start | bytes 1769480 | tf_op jit(solution)/shard_map/ppermute | solution.py:275
  68.7 1.2 collective-permute-start.16
  69.9 2.0 %collective-permute-start.17 = (bf16[4,144,512]{2,1,0:T(8,128)(2,1)S(1)}, bf16[4,144,512]{2,1,0:T(8,128)(2,1)S(1)}, u32[]{:S(2)}, u32[]{:S(2)}) collective-permute-start(bf16[4,144,512]{2,1,0:T(8,128)(2,1)S(1)} %get-tuple-element.59), channel_id=1, source_target_pairs={{0,24},{8,0},{16,8},{24,16},{32,56},{40,32},{48,40},{56,48},{64,88... | collective-permute-start | bytes 1769480 | tf_op jit(solution)/shard_map/ppermute | solution.py:275
  71.9 5.6 %attend.4 = (f32[4,144,512]{2,1,0:T(8,128)S(1)}, f32[4,144,512]{2,1,0:T(8,128)S(1)}) custom-call(s32[3]{0:T(128)S(1)} %pad_add_fusion.place_ref, s32[32]{0:T(128)S(1)} %broadcast_add_fusion.count_ref, s32[512]{0:T(512)S(1)} %select_n.44.ids_ref, bf16[8192,256]{1,0:T(8,128)(2,1)S(1)} %bitcast.17, bf16[4,64,1024]{2,1,0:T(8,128)(2,1)S(1)} %copy-done.1, ...), custom_call_target="tpu_custom_call" | custom-call | flops 4000000000 | bytes 1048576 | tf_op jit(solution)/shard_map/attend/pallas_call | solution.py:160
  77.6 5.4 %collective-permute-done.16.refs_4_ = bf16[4,144,512]{2,1,0:T(8,128)(2,1)S(1)} collective-permute-done((bf16[4,144,512]{2,1,0:T(8,128)(2,1)S(1)}, bf16[4,144,512]{2,1,0:T(8,128)(2,1)S(1)}, u32[]{:S(2)}, u32[]{:S(2)}) %collective-permute-start.16) | collective-permute-done | bytes 589856 | tf_op jit(solution)/shard_map/ppermute | solution.py:275
  82.9 0.7 stage.1
  83.7 3.3 %collective-permute-start.19 = (bf16[1,144,512]{2,1,0:T(8,128)(2,1)S(1)}, bf16[1,144,512]{2,1,0:T(8,128)(2,1)S(1)}, u32[]{:S(2)}, u32[]{:S(2)}) collective-permute-start(bf16[1,144,512]{2,1,0:T(8,128)(2,1)S(1)} %get-tuple-element.62), channel_id=1, source_target_pairs={{0,24},{8,16},{16,8},{24,0},{32,56},{40,48},{48,40},{56,32},{64,88... | collective-permute-start | bytes 442376 | tf_op jit(solution)/shard_map/ppermute | solution.py:278
  87.0 1.4 %collective-permute-start.20 = (bf16[1,144,512]{2,1,0:T(8,128)(2,1)S(1)}, bf16[1,144,512]{2,1,0:T(8,128)(2,1)S(1)}, u32[]{:S(2)}, u32[]{:S(2)}) collective-permute-start(bf16[1,144,512]{2,1,0:T(8,128)(2,1)S(1)} %get-tuple-element.63), channel_id=1, source_target_pairs={{0,16},{8,24},{16,0},{24,8},{32,48},{40,56},{48,32},{56,40},{64,80... | collective-permute-start | bytes 442376 | tf_op jit(solution)/shard_map/ppermute | solution.py:278
  88.9 2.3 %collective-permute-start.22 = (bf16[1,144,512]{2,1,0:T(8,128)(2,1)S(1)}, bf16[1,144,512]{2,1,0:T(8,128)(2,1)S(1)}, u32[]{:S(2)}, u32[]{:S(2)}) collective-permute-start(bf16[1,144,512]{2,1,0:T(8,128)(2,1)S(1)} %get-tuple-element.66), channel_id=1, source_target_pairs={{0,96},{8,104},{16,112},{24,120},{32,64},{40,72},{48,80},{56,88},{... | collective-permute-start | bytes 442376 | tf_op jit(solution)/shard_map/ppermute | solution.py:278
  91.3 2.0 %collective-permute-start.23 = (bf16[1,144,512]{2,1,0:T(8,128)(2,1)S(1)}, bf16[1,144,512]{2,1,0:T(8,128)(2,1)S(1)}, u32[]{:S(2)}, u32[]{:S(2)}) collective-permute-start(bf16[1,144,512]{2,1,0:T(8,128)(2,1)S(1)} %get-tuple-element.67), channel_id=1, source_target_pairs={{0,64},{8,72},{16,80},{24,88},{32,96},{40,104},{48,112},{56,120},{... | collective-permute-start | bytes 442376 | tf_op jit(solution)/shard_map/ppermute | solution.py:278
  93.7 1.5 %collective-permute-done.22.refs_6_ = bf16[1,144,512]{2,1,0:T(8,128)(2,1)S(1)} collective-permute-done((bf16[1,144,512]{2,1,0:T(8,128)(2,1)S(1)}, bf16[1,144,512]{2,1,0:T(8,128)(2,1)S(1)}, u32[]{:S(2)}, u32[]{:S(2)}) %collective-permute-start.22) | collective-permute-done | bytes 147488 | tf_op jit(solution)/shard_map/ppermute | solution.py:278
  95.2 2.8 %collective-permute-done.23.refs_7_ = bf16[1,144,512]{2,1,0:T(8,128)(2,1)S(1)} collective-permute-done((bf16[1,144,512]{2,1,0:T(8,128)(2,1)S(1)}, bf16[1,144,512]{2,1,0:T(8,128)(2,1)S(1)}, u32[]{:S(2)}, u32[]{:S(2)}) %collective-permute-start.23) | collective-permute-done | bytes 147488 | tf_op jit(solution)/shard_map/ppermute | solution.py:278
  98.6 1.5 %collective-permute-done.24.other_ref = bf16[128,1024]{1,0:T(8,128)(2,1)S(1)} collective-permute-done((bf16[128,1024]{1,0:T(8,128)(2,1)S(1)}, bf16[128,1024]{1,0:T(8,128)(2,1)S(1)}, u32[]{:S(2)}, u32[]{:S(2)}) %collective-permute-start.24) | collective-permute-done | bytes 262176 | tf_op jit(solution)/shard_map/ppermute | solution.py:281
  100.2 4.7 %project.2 = (bf16[128,1024]{1,0:T(8,128)(2,1)S(1)}, bf16[128,1024]{1,0:T(8,128)(2,1)S(1)}, f32[128,1024]{1,0:T(8,128)S(1)}) custom-call(s32[3]{0:T(128)S(1)} %pad_add_fusion.place_ref, bf16[128,1024]{1,0:T(8,128)(2,1)S(1)} %final.1.att_ref, bf16[128,1024]{1,0:T(8,128)(2,1)S(1)} %collective-permute-done.24.other_ref, bf16[1024,8192]{1,0:T(8,128)(2,1)S(1)} %bitcast.12, ...), custom_call_target="tpu_custom_call" | custom-call | flops 6000000000 | bytes 1048576 | tf_op jit(solution)/shard_map/project/pallas_call | solution.py:249
  104.9 1.6 %collective-permute-start.26 = (bf16[128,1024]{1,0:T(8,128)(2,1)S(1)}, bf16[128,1024]{1,0:T(8,128)(2,1)S(1)}, u32[]{:S(2)}, u32[]{:S(2)}) collective-permute-start(bf16[128,1024]{1,0:T(8,128)(2,1)S(1)} %get-tuple-element.69), channel_id=1, source_target_pairs={{0,2},{1,3},{2,4},{3,5},{4,6},{5,7},{6,0},{7,1},{8,10},{9,11},{10,... | collective-permute-start | bytes 786440 | tf_op jit(solution)/shard_map/ppermute | solution.py:281
  106.5 1.7 %collective-permute-start.28 = (bf16[128,1024]{1,0:T(8,128)(2,1)S(1)}, bf16[128,1024]{1,0:T(8,128)(2,1)S(1)}, u32[]{:S(2)}, u32[]{:S(2)}) collective-permute-start(bf16[128,1024]{1,0:T(8,128)(2,1)S(1)} %get-tuple-element.70), channel_id=1, source_target_pairs={{0,6},{1,7},{2,0},{3,1},{4,2},{5,3},{6,4},{7,5},{8,14},{9,15},{10,... | collective-permute-start | bytes 786440 | tf_op jit(solution)/shard_map/ppermute | solution.py:281
  108.2 2.9 %project.3 = bf16[128,1024]{1,0:T(8,128)(2,1)S(1)} custom-call(s32[3]{0:T(128)S(1)} %pad_add_fusion.place_ref, bf16[128,1024]{1,0:T(8,128)(2,1)S(1)} %final.1.att_ref, bf16[128,1024]{1,0:T(8,128)(2,1)S(1)} %collective-permute-done.24.other_ref, bf16[1024,8192]{1,0:T(8,128)(2,1)S(1)} %bitcast.13, bf16[1024,8192]{1,0:T(8,128)(2,1)} %collective-permute-done.25.wo_ref), custom_call_target="tpu_custom_call" | custom-call | flops 2000000000 | bytes 1048576 | tf_op jit(solution)/shard_map/project/pallas_call | solution.py:249
  111.0 2.1 %collective-permute-start.27 = (bf16[128,1024]{1,0:T(8,128)(2,1)S(1)}, bf16[128,1024]{1,0:T(8,128)(2,1)S(1)}, u32[]{:S(2)}, u32[]{:S(2)}) collective-permute-start(bf16[128,1024]{1,0:T(8,128)(2,1)S(1)} %project.3), channel_id=1, source_target_pairs={{0,4},{1,5},{2,6},{3,7},{4,0},{5,1},{6,2},{7,3},{8,12},{9,13},{10,... | collective-permute-start | bytes 786440 | tf_op jit(solution)/shard_map/ppermute | solution.py:281
  113.1 1.4 %collective-permute-done.26 = bf16[128,1024]{1,0:T(8,128)(2,1)S(1)} collective-permute-done((bf16[128,1024]{1,0:T(8,128)(2,1)S(1)}, bf16[128,1024]{1,0:T(8,128)(2,1)S(1)}, u32[]{:S(2)}, u32[]{:S(2)}) %collective-permute-start.26) | collective-permute-done | bytes 262176 | tf_op jit(solution)/shard_map/ppermute | solution.py:281
  114.5 5.0 %collective-permute-done.28 = bf16[128,1024]{1,0:T(8,128)(2,1)S(1)} collective-permute-done((bf16[128,1024]{1,0:T(8,128)(2,1)S(1)}, bf16[128,1024]{1,0:T(8,128)(2,1)S(1)}, u32[]{:S(2)}, u32[]{:S(2)}) %collective-permute-start.28) | collective-permute-done | bytes 262176 | tf_op jit(solution)/shard_map/ppermute | solution.py:281
  119.5 1.8 %collective-permute-done.27 = bf16[128,1024]{1,0:T(8,128)(2,1)S(1)} collective-permute-done((bf16[128,1024]{1,0:T(8,128)(2,1)S(1)}, bf16[128,1024]{1,0:T(8,128)(2,1)S(1)}, u32[]{:S(2)}, u32[]{:S(2)}) %collective-permute-start.27) | collective-permute-done | bytes 262176 | tf_op jit(solution)/shard_map/ppermute | solution.py:281
  121.3 0.9 convert_add_fusion
  (58 shorter events, 4.6 us)
Async XLA Ops:
  0.0 100.1 %collective-permute-start.25 = (bf16[1024,8192]{1,0:T(8,128)(2,1)}, bf16[1024,8192]{1,0:T(8,128)(2,1)}, u32[]{:S(2)}, u32[]{:S(2)}) collective-permute-start(bf16[1024,8192]{1,0:T(8,128)(2,1)} %bitcast.9), channel_id=1, source_target_pairs={{0,1},{1,0},{2,3},{3,2},{4,5},{5,4},{6,7},{7,6},{8,9},{9,8},{10,11... | collective-permute-start | bytes 50331656 | tf_op jit(solution)/shard_map/ppermute | solution.py:281
  1.0 6.2 %collective-permute-start.1 = (bf16[1,64,1024]{2,1,0:T(8,128)(2,1)S(1)}, bf16[1,64,1024]{2,1,0:T(8,128)(2,1)S(1)}, u32[]{:S(2)}, u32[]{:S(2)}) collective-permute-start(bf16[1,64,1024]{2,1,0:T(8,128)(2,1)S(1)} %get-tuple-element.73), channel_id=1, source_target_pairs={{0,32},{8,40},{16,48},{24,56},{32,0},{40,8},{48,16},{56,24},{64,96... | collective-permute-start | bytes 393224 | tf_op jit(solution)/shard_map/ppermute | solution.py:278
  3.1 5.6 %collective-permute-start = (bf16[1,64,1024]{2,1,0:T(8,128)(2,1)S(1)}, bf16[1,64,1024]{2,1,0:T(8,128)(2,1)S(1)}, u32[]{:S(2)}, u32[]{:S(2)}) collective-permute-start(bf16[1,64,1024]{2,1,0:T(8,128)(2,1)S(1)} %get-tuple-element.74), channel_id=1, source_target_pairs={{0,8},{8,0},{16,24},{24,16},{32,40},{40,32},{48,56},{56,48},{64,72... | collective-permute-start | bytes 393224 | tf_op jit(solution)/shard_map/ppermute | solution.py:278
  8.7 17.1 %copy-start.5 = (s32[32,64]{1,0:T(8,128)S(1)}, s32[32,64]{1,0:T(8,128)}, u32[]{:S(2)}) copy-start(s32[32,64]{1,0:T(8,128)} %param.6) | copy-start | bytes 24580
  8.7 8.9 %collective-permute-start.2 = (bf16[2,64,1024]{2,1,0:T(8,128)(2,1)S(1)}, bf16[2,64,1024]{2,1,0:T(8,128)(2,1)S(1)}, u32[]{:S(2)}, u32[]{:S(2)}) collective-permute-start(bf16[2,64,1024]{2,1,0:T(8,128)(2,1)S(1)} %pad_maximum_fusion.2), channel_id=1, source_target_pairs={{0,24},{8,16},{16,8},{24,0},{32,56},{40,48},{48,40},{56,32},{64,88... | collective-permute-start | bytes 786440 | tf_op jit(solution)/shard_map/ppermute | solution.py:278
  11.6 8.5 %collective-permute-start.3 = (bf16[2,64,1024]{2,1,0:T(8,128)(2,1)S(1)}, bf16[2,64,1024]{2,1,0:T(8,128)(2,1)S(1)}, u32[]{:S(2)}, u32[]{:S(2)}) collective-permute-start(bf16[2,64,1024]{2,1,0:T(8,128)(2,1)S(1)} %pad_maximum_fusion.3), channel_id=1, source_target_pairs={{0,96},{8,104},{16,112},{24,120},{32,64},{40,72},{48,80},{56,88},{... | collective-permute-start | bytes 786440 | tf_op jit(solution)/shard_map/ppermute | solution.py:278
  17.7 5.3 %copy-start = (bf16[4,64,1024]{2,1,0:T(8,128)(2,1)}, bf16[4,64,1024]{2,1,0:T(8,128)(2,1)S(1)}, u32[]{:S(2)}) copy-start(bf16[4,64,1024]{2,1,0:T(8,128)(2,1)S(1)} %pad_maximum_fusion.refs_0_) | copy-start | bytes 1572868
  20.2 12.6 %collective-permute-start.6 = (bf16[4,64,1024]{2,1,0:T(8,128)(2,1)S(1)}, bf16[4,64,1024]{2,1,0:T(8,128)(2,1)S(1)}, u32[]{:S(2)}, u32[]{:S(2)}) collective-permute-start(bf16[4,64,1024]{2,1,0:T(8,128)(2,1)S(1)} %pad_maximum_fusion.refs_0_), channel_id=1, source_target_pairs={{0,96},{8,104},{16,112},{24,120},{32,0},{40,8},{48,16},{56,24},{64... | collective-permute-start | bytes 1572872 | tf_op jit(solution)/shard_map/ppermute | solution.py:275
  23.0 13.2 %collective-permute-start.4 = (bf16[4,64,1024]{2,1,0:T(8,128)(2,1)S(1)}, bf16[4,64,1024]{2,1,0:T(8,128)(2,1)S(1)}, u32[]{:S(2)}, u32[]{:S(2)}) collective-permute-start(bf16[4,64,1024]{2,1,0:T(8,128)(2,1)S(1)} %pad_maximum_fusion.refs_0_), channel_id=1, source_target_pairs={{0,32},{8,40},{16,48},{24,56},{32,64},{40,72},{48,80},{56,88},{64,... | collective-permute-start | bytes 1572872 | tf_op jit(solution)/shard_map/ppermute | solution.py:275
  23.0 13.2 %collective-permute-start.7 = (bf16[4,64,1024]{2,1,0:T(8,128)(2,1)S(1)}, bf16[4,64,1024]{2,1,0:T(8,128)(2,1)S(1)}, u32[]{:S(2)}, u32[]{:S(2)}) collective-permute-start(bf16[4,64,1024]{2,1,0:T(8,128)(2,1)S(1)} %pad_maximum_fusion.1.refs_1_), channel_id=1, source_target_pairs={{0,24},{8,0},{16,8},{24,16},{32,56},{40,32},{48,40},{56,48},{64,88... | collective-permute-start | bytes 1572872 | tf_op jit(solution)/shard_map/ppermute | solution.py:275
  23.5 13.1 %collective-permute-start.5 = (bf16[4,64,1024]{2,1,0:T(8,128)(2,1)S(1)}, bf16[4,64,1024]{2,1,0:T(8,128)(2,1)S(1)}, u32[]{:S(2)}, u32[]{:S(2)}) collective-permute-start(bf16[4,64,1024]{2,1,0:T(8,128)(2,1)S(1)} %pad_maximum_fusion.1.refs_1_), channel_id=1, source_target_pairs={{0,8},{8,16},{16,24},{24,0},{32,40},{40,48},{48,56},{56,32},{64,72... | collective-permute-start | bytes 1572872 | tf_op jit(solution)/shard_map/ppermute | solution.py:275
  25.1 0.8 copy-start.2
  36.6 12.2 %collective-permute-start.8 = (bf16[4,64,1024]{2,1,0:T(8,128)(2,1)S(1)}, bf16[4,64,1024]{2,1,0:T(8,128)(2,1)S(1)}, u32[]{:S(2)}, u32[]{:S(2)}) collective-permute-start(bf16[4,64,1024]{2,1,0:T(8,128)(2,1)S(1)} %collective-permute-done.4.refs_0_), channel_id=1, source_target_pairs={{0,32},{8,40},{16,48},{24,56},{32,64},{40,72},{48,80},{56,88},{64,... | collective-permute-start | bytes 1572872 | tf_op jit(solution)/shard_map/ppermute | solution.py:275
  37.8 11.9 %collective-permute-start.9 = (bf16[4,64,1024]{2,1,0:T(8,128)(2,1)S(1)}, bf16[4,64,1024]{2,1,0:T(8,128)(2,1)}, u32[]{:S(2)}, u32[]{:S(2)}) collective-permute-start(bf16[4,64,1024]{2,1,0:T(8,128)(2,1)S(1)} %collective-permute-done.5.refs_1_), channel_id=1, source_target_pairs={{0,8},{8,16},{16,24},{24,0},{32,40},{40,48},{48,56},{56,32},{64,72... | collective-permute-start | bytes 1572872 | tf_op jit(solution)/shard_map/ppermute | solution.py:275
  37.9 2.2 %copy-start.4 = (bf16[1,8192,256]{2,1,0:T(8,128)(2,1)S(1)}, bf16[1,8192,256]{2,1,0:T(8,128)(2,1)}, u32[]{:S(2)}) copy-start(bf16[1,8192,256]{2,1,0:T(8,128)(2,1)} %param.5) | copy-start | bytes 12582916
  53.9 8.2 %collective-permute-start.10 = (bf16[2,144,512]{2,1,0:T(8,128)(2,1)S(1)}, bf16[2,144,512]{2,1,0:T(8,128)(2,1)S(1)}, u32[]{:S(2)}, u32[]{:S(2)}) collective-permute-start(bf16[2,144,512]{2,1,0:T(8,128)(2,1)S(1)} %get-tuple-element.49), channel_id=1, source_target_pairs={{0,96},{8,104},{16,112},{24,120},{32,0},{40,8},{48,16},{56,24},{64... | collective-permute-start | bytes 884744 | tf_op jit(solution)/shard_map/ppermute | solution.py:275
  56.2 8.5 %collective-permute-start.11 = (bf16[2,144,512]{2,1,0:T(8,128)(2,1)S(1)}, bf16[2,144,512]{2,1,0:T(8,128)(2,1)S(1)}, u32[]{:S(2)}, u32[]{:S(2)}) collective-permute-start(bf16[2,144,512]{2,1,0:T(8,128)(2,1)S(1)} %get-tuple-element.50), channel_id=1, source_target_pairs={{0,32},{8,40},{16,48},{24,56},{32,64},{40,72},{48,80},{56,88},{64,... | collective-permute-start | bytes 884744 | tf_op jit(solution)/shard_map/ppermute | solution.py:275
  56.2 8.5 %collective-permute-start.12 = (bf16[2,144,512]{2,1,0:T(8,128)(2,1)S(1)}, bf16[2,144,512]{2,1,0:T(8,128)(2,1)S(1)}, u32[]{:S(2)}, u32[]{:S(2)}) collective-permute-start(bf16[2,144,512]{2,1,0:T(8,128)(2,1)S(1)} %get-tuple-element.53), channel_id=1, source_target_pairs={{0,24},{8,0},{16,8},{24,16},{32,56},{40,32},{48,40},{56,48},{64,88... | collective-permute-start | bytes 884744 | tf_op jit(solution)/shard_map/ppermute | solution.py:275
  56.3 8.4 %collective-permute-start.13 = (bf16[2,144,512]{2,1,0:T(8,128)(2,1)S(1)}, bf16[2,144,512]{2,1,0:T(8,128)(2,1)S(1)}, u32[]{:S(2)}, u32[]{:S(2)}) collective-permute-start(bf16[2,144,512]{2,1,0:T(8,128)(2,1)S(1)} %get-tuple-element.54), channel_id=1, source_target_pairs={{0,8},{8,16},{16,24},{24,0},{32,40},{40,48},{48,56},{56,32},{64,72... | collective-permute-start | bytes 884744 | tf_op jit(solution)/shard_map/ppermute | solution.py:275
  58.2 41.9 %slice-start = ((s8[16777216]{0:T(1024)(128)(4,1)}), s8[4194304]{0:T(1024)(128)(4,1)S(1)}, s32[]{:S(2)}) async-start(s8[16777216]{0:T(1024)(128)(4,1)} %bitcast.10), calls=%async_computation | async-start | bytes 8388608
  58.2 41.9 %slice-start.1 = ((s8[16777216]{0:T(1024)(128)(4,1)}), s8[4194304]{0:T(1024)(128)(4,1)S(1)}, s32[]{:S(2)}) async-start(s8[16777216]{0:T(1024)(128)(4,1)} %bitcast.10), calls=%async_computation.1 | async-start | bytes 8388608
  64.7 7.2 %copy-start.1 = (bf16[4,64,1024]{2,1,0:T(8,128)(2,1)S(1)}, bf16[4,64,1024]{2,1,0:T(8,128)(2,1)}, u32[]{:S(2)}) copy-start(bf16[4,64,1024]{2,1,0:T(8,128)(2,1)} %copy-done) | copy-start | bytes 1572868
  64.7 7.2 %copy-start.3 = (bf16[4,64,1024]{2,1,0:T(8,128)(2,1)S(1)}, bf16[4,64,1024]{2,1,0:T(8,128)(2,1)}, u32[]{:S(2)}) copy-start(bf16[4,64,1024]{2,1,0:T(8,128)(2,1)} %copy-done.2) | copy-start | bytes 1572868
  65.4 12.2 %collective-permute-start.14 = (bf16[4,144,512]{2,1,0:T(8,128)(2,1)S(1)}, bf16[4,144,512]{2,1,0:T(8,128)(2,1)S(1)}, u32[]{:S(2)}, u32[]{:S(2)}) collective-permute-start(bf16[4,144,512]{2,1,0:T(8,128)(2,1)S(1)} %get-tuple-element.55), channel_id=1, source_target_pairs={{0,32},{8,40},{16,48},{24,56},{32,64},{40,72},{48,80},{56,88},{64,... | collective-permute-start | bytes 1769480 | tf_op jit(solution)/shard_map/ppermute | solution.py:275
  66.8 10.8 %collective-permute-start.15 = (bf16[4,144,512]{2,1,0:T(8,128)(2,1)S(1)}, bf16[4,144,512]{2,1,0:T(8,128)(2,1)S(1)}, u32[]{:S(2)}, u32[]{:S(2)}) collective-permute-start(bf16[4,144,512]{2,1,0:T(8,128)(2,1)S(1)} %get-tuple-element.56), channel_id=1, source_target_pairs={{0,96},{8,104},{16,112},{24,120},{32,0},{40,8},{48,16},{56,24},{64... | collective-permute-start | bytes 1769480 | tf_op jit(solution)/shard_map/ppermute | solution.py:275
  68.7 14.3 %collective-permute-start.16 = (bf16[4,144,512]{2,1,0:T(8,128)(2,1)S(1)}, bf16[4,144,512]{2,1,0:T(8,128)(2,1)S(1)}, u32[]{:S(2)}, u32[]{:S(2)}) collective-permute-start(bf16[4,144,512]{2,1,0:T(8,128)(2,1)S(1)} %get-tuple-element.58), channel_id=1, source_target_pairs={{0,8},{8,16},{16,24},{24,0},{32,40},{40,48},{48,56},{56,32},{64,72... | collective-permute-start | bytes 1769480 | tf_op jit(solution)/shard_map/ppermute | solution.py:275
  69.9 30.3 %slice-start.2 = ((s8[16777216]{0:T(1024)(128)(4,1)}), s8[4194304]{0:T(1024)(128)(4,1)S(1)}, s32[]{:S(2)}) async-start(s8[16777216]{0:T(1024)(128)(4,1)} %bitcast.10), calls=%async_computation.2 | async-start | bytes 8388608
  69.9 30.3 %slice-start.3 = ((s8[16777216]{0:T(1024)(128)(4,1)}), s8[4194304]{0:T(1024)(128)(4,1)S(1)}, s32[]{:S(2)}) async-start(s8[16777216]{0:T(1024)(128)(4,1)} %bitcast.10), calls=%async_computation.3 | async-start | bytes 8388608
  69.9 13.1 %collective-permute-start.17 = (bf16[4,144,512]{2,1,0:T(8,128)(2,1)S(1)}, bf16[4,144,512]{2,1,0:T(8,128)(2,1)S(1)}, u32[]{:S(2)}, u32[]{:S(2)}) collective-permute-start(bf16[4,144,512]{2,1,0:T(8,128)(2,1)S(1)} %get-tuple-element.59), channel_id=1, source_target_pairs={{0,24},{8,0},{16,8},{24,16},{32,56},{40,32},{48,40},{56,48},{64,88... | collective-permute-start | bytes 1769480 | tf_op jit(solution)/shard_map/ppermute | solution.py:275
  83.6 5.2 %collective-permute-start.18 = (bf16[1,144,512]{2,1,0:T(8,128)(2,1)S(1)}, bf16[1,144,512]{2,1,0:T(8,128)(2,1)S(1)}, u32[]{:S(2)}, u32[]{:S(2)}) collective-permute-start(bf16[1,144,512]{2,1,0:T(8,128)(2,1)S(1)} %get-tuple-element.61), channel_id=1, source_target_pairs={{0,8},{8,0},{16,24},{24,16},{32,40},{40,32},{48,56},{56,48},{64,72... | collective-permute-start | bytes 442376 | tf_op jit(solution)/shard_map/ppermute | solution.py:278
  83.7 7.6 %collective-permute-start.19 = (bf16[1,144,512]{2,1,0:T(8,128)(2,1)S(1)}, bf16[1,144,512]{2,1,0:T(8,128)(2,1)S(1)}, u32[]{:S(2)}, u32[]{:S(2)}) collective-permute-start(bf16[1,144,512]{2,1,0:T(8,128)(2,1)S(1)} %get-tuple-element.62), channel_id=1, source_target_pairs={{0,24},{8,16},{16,8},{24,0},{32,56},{40,48},{48,40},{56,32},{64,88... | collective-permute-start | bytes 442376 | tf_op jit(solution)/shard_map/ppermute | solution.py:278
  87.0 6.6 %collective-permute-start.20 = (bf16[1,144,512]{2,1,0:T(8,128)(2,1)S(1)}, bf16[1,144,512]{2,1,0:T(8,128)(2,1)S(1)}, u32[]{:S(2)}, u32[]{:S(2)}) collective-permute-start(bf16[1,144,512]{2,1,0:T(8,128)(2,1)S(1)} %get-tuple-element.63), channel_id=1, source_target_pairs={{0,16},{8,24},{16,0},{24,8},{32,48},{40,56},{48,32},{56,40},{64,80... | collective-permute-start | bytes 442376 | tf_op jit(solution)/shard_map/ppermute | solution.py:278
  88.4 5.3 %collective-permute-start.21 = (bf16[1,144,512]{2,1,0:T(8,128)(2,1)S(1)}, bf16[1,144,512]{2,1,0:T(8,128)(2,1)S(1)}, u32[]{:S(2)}, u32[]{:S(2)}) collective-permute-start(bf16[1,144,512]{2,1,0:T(8,128)(2,1)S(1)} %get-tuple-element.65), channel_id=1, source_target_pairs={{0,32},{8,40},{16,48},{24,56},{32,0},{40,8},{48,16},{56,24},{64,96... | collective-permute-start | bytes 442376 | tf_op jit(solution)/shard_map/ppermute | solution.py:278
  88.9 6.4 %collective-permute-start.22 = (bf16[1,144,512]{2,1,0:T(8,128)(2,1)S(1)}, bf16[1,144,512]{2,1,0:T(8,128)(2,1)S(1)}, u32[]{:S(2)}, u32[]{:S(2)}) collective-permute-start(bf16[1,144,512]{2,1,0:T(8,128)(2,1)S(1)} %get-tuple-element.66), channel_id=1, source_target_pairs={{0,96},{8,104},{16,112},{24,120},{32,64},{40,72},{48,80},{56,88},{... | collective-permute-start | bytes 442376 | tf_op jit(solution)/shard_map/ppermute | solution.py:278
  91.3 6.6 %collective-permute-start.23 = (bf16[1,144,512]{2,1,0:T(8,128)(2,1)S(1)}, bf16[1,144,512]{2,1,0:T(8,128)(2,1)S(1)}, u32[]{:S(2)}, u32[]{:S(2)}) collective-permute-start(bf16[1,144,512]{2,1,0:T(8,128)(2,1)S(1)} %get-tuple-element.67), channel_id=1, source_target_pairs={{0,64},{8,72},{16,80},{24,88},{32,96},{40,104},{48,112},{56,120},{... | collective-permute-start | bytes 442376 | tf_op jit(solution)/shard_map/ppermute | solution.py:278
  98.3 1.8 %collective-permute-start.24 = (bf16[128,1024]{1,0:T(8,128)(2,1)S(1)}, bf16[128,1024]{1,0:T(8,128)(2,1)S(1)}, u32[]{:S(2)}, u32[]{:S(2)}) collective-permute-start(bf16[128,1024]{1,0:T(8,128)(2,1)S(1)} %final.1.att_ref), channel_id=1, source_target_pairs={{0,1},{1,0},{2,3},{3,2},{4,5},{5,4},{6,7},{7,6},{8,9},{9,8},{10,11... | collective-permute-start | bytes 786440 | tf_op jit(solution)/shard_map/ppermute | solution.py:281
  104.9 9.7 %collective-permute-start.26 = (bf16[128,1024]{1,0:T(8,128)(2,1)S(1)}, bf16[128,1024]{1,0:T(8,128)(2,1)S(1)}, u32[]{:S(2)}, u32[]{:S(2)}) collective-permute-start(bf16[128,1024]{1,0:T(8,128)(2,1)S(1)} %get-tuple-element.69), channel_id=1, source_target_pairs={{0,2},{1,3},{2,4},{3,5},{4,6},{5,7},{6,0},{7,1},{8,10},{9,11},{10,... | collective-permute-start | bytes 786440 | tf_op jit(solution)/shard_map/ppermute | solution.py:281
  106.5 13.0 %collective-permute-start.28 = (bf16[128,1024]{1,0:T(8,128)(2,1)S(1)}, bf16[128,1024]{1,0:T(8,128)(2,1)S(1)}, u32[]{:S(2)}, u32[]{:S(2)}) collective-permute-start(bf16[128,1024]{1,0:T(8,128)(2,1)S(1)} %get-tuple-element.70), channel_id=1, source_target_pairs={{0,6},{1,7},{2,0},{3,1},{4,2},{5,3},{6,4},{7,5},{8,14},{9,15},{10,... | collective-permute-start | bytes 786440 | tf_op jit(solution)/shard_map/ppermute | solution.py:281
  111.0 10.3 %collective-permute-start.27 = (bf16[128,1024]{1,0:T(8,128)(2,1)S(1)}, bf16[128,1024]{1,0:T(8,128)(2,1)S(1)}, u32[]{:S(2)}, u32[]{:S(2)}) collective-permute-start(bf16[128,1024]{1,0:T(8,128)(2,1)S(1)} %project.3), channel_id=1, source_target_pairs={{0,4},{1,5},{2,6},{3,7},{4,0},{5,1},{6,2},{7,3},{8,12},{9,13},{10,... | collective-permute-start | bytes 786440 | tf_op jit(solution)/shard_map/ppermute | solution.py:281

commit v4 on v3

--- a/solution.py
+++ b/solution.py
@@ -256,7 +256,7 @@
             pltpu.SemaphoreType.DMA((len(fars),)),
         ],
         compiler_params=pltpu.CompilerParams(vmem_limit_bytes=30 * 2**20),
-        cost_estimate=pl.CostEstimate(flops=2 * 10**9 * len(fars), bytes_accessed=2**20, transcendentals=0),
+        cost_estimate=pl.CostEstimate(flops=3 * 10**9 * len(fars), bytes_accessed=2**20, transcendentals=0),
         name="project",
     )(place, att, other, w, wo)
 
@@ -323,10 +323,11 @@
 
     other = yc(att, 0, 1)
 
+    p1, p3 = project(place, att, other, w, w_other, (1, 3), (BF, BF))
+    r1, r3 = yc(p1, 1, 0), yc(p3, 3, 0)
     (p2,) = project(place, att, other, w, w_other, (2,), (BF,))
     r2 = yc(p2, 2, 0)
-    p1, p3, own = project(place, att, other, w, w_other, (1, 3, 0), (BF, BF, F32))
-    r1, r3 = yc(p1, 1, 0), yc(p3, 3, 0)
+    (own,) = project(place, att, other, w, w_other, (0,), (F32,))
     return own + r1.astype(F32) + r2.astype(F32) + r3.astype(F32)
 
 

time: 124 us -> 122 us (0.984)
  waiting for transfers between devices: 47.8 us -> 45.5 us
  Pallas kernels: 26.4 us -> 28.3 us
    ppermute x5, waiting for transfers between devices: 9.74 us -> 4.67 us  [yc(): return lax.ppermute(v, 'kvh', kvh_shift(dy % 4, dc))]
    pallas_call x2 -> x3, Pallas kernels: 7.57 us -> 9.54 us  [project(): pl.pallas_call(functools.partial(project_kernel, fars=fars), out_shape=[j...]
    ppermute x10, waiting for transfers between devices: 14 us -> 15.6 us  [flip(): return lax.ppermute(v, 'seq', seq_flip(fz, fx))]
    ppermute x10, starting transfers between devices: 18.2 us -> 16.6 us  [flip(): return lax.ppermute(v, 'seq', seq_flip(fz, fx))]
    unnamed x20 -> x16, local copies, waits for them, and re-layouts: 3.02 us -> 3.01 us
  transfers between devices with their start and end apart: 29 -> 29, of which waited for: 20 -> 20; matrix products, arithmetic and copies ran while one was open for 3% -> 3% of each run, Pallas kernels for 18% -> 21%
where the time goes in v4:
time: 122 us; the launch traced here: 121 us
  waiting for transfers between devices  45.5 us (37%)
  starting transfers between devices  40.4 us (33%)
  Pallas kernels  28.3 us (23%)
  local copies, waits for them, and re-layouts  4.07 us (3%)
  other arithmetic  3 us (2%)
    ppermute x14, waiting for transfers between devices, zx(): return lax.ppermute(v, 'seq', seq_shift(dz % 4, dx % 4))  25.2 us
    pallas_call x4, Pallas kernels, attend(): pl.pallas_call(functools.partial(attend_kernel, far=far, cut=cut), out_sh...  17.1 us
    ppermute x14, starting transfers between devices, zx(): return lax.ppermute(v, 'seq', seq_shift(dz % 4, dx % 4))  16.9 us
    ppermute x10, starting transfers between devices, flip(): return lax.ppermute(v, 'seq', seq_flip(fz, fx))  16.6 us
    ppermute x10, waiting for transfers between devices, flip(): return lax.ppermute(v, 'seq', seq_flip(fz, fx))  15.6 us
    pallas_call x3, Pallas kernels, project(): pl.pallas_call(functools.partial(project_kernel, fars=fars), out_shape=[j...  9.54 us
    ppermute x5, starting transfers between devices, yc(): return lax.ppermute(v, 'kvh', kvh_shift(dy % 4, dc))  6.88 us
    ppermute x5, waiting for transfers between devices, yc(): return lax.ppermute(v, 'kvh', kvh_shift(dy % 4, dc))  4.67 us
  transfers between devices with their start and end apart: 29, of which 20 were waited for; matrix products, arithmetic and copies ran while one was open for 3% of the time, Pallas kernels for 21%

profile of v4, /device:TPU:0, one launch (start us, length us, event | category | flops | bytes accessed | tf_op | source)
XLA Modules:
  0.0 121.4 jit_solution(5177421641454035651)
XLA Ops:
  0.0 1.0 slice_bitcast_fusion
  1.0 2.1 %collective-permute-start.1 = (bf16[1,64,1024]{2,1,0:T(8,128)(2,1)S(1)}, bf16[1,64,1024]{2,1,0:T(8,128)(2,1)S(1)}, u32[]{:S(2)}, u32[]{:S(2)}) collective-permute-start(bf16[1,64,1024]{2,1,0:T(8,128)(2,1)S(1)} %get-tuple-element.71), channel_id=1, source_target_pairs={{0,32},{8,40},{16,48},{24,56},{32,0},{40,8},{48,16},{56,24},{64,96... | collective-permute-start | bytes 393224 | tf_op jit(solution)/shard_map/ppermute | solution.py:278
  3.1 1.5 %collective-permute-start = (bf16[1,64,1024]{2,1,0:T(8,128)(2,1)S(1)}, bf16[1,64,1024]{2,1,0:T(8,128)(2,1)S(1)}, u32[]{:S(2)}, u32[]{:S(2)}) collective-permute-start(bf16[1,64,1024]{2,1,0:T(8,128)(2,1)S(1)} %get-tuple-element.72), channel_id=1, source_target_pairs={{0,8},{8,0},{16,24},{24,16},{32,40},{40,32},{48,56},{56,48},{64,72... | collective-permute-start | bytes 393224 | tf_op jit(solution)/shard_map/ppermute | solution.py:278
  4.6 0.8 fusion.5
  5.4 1.9 %collective-permute-done.1 = bf16[1,64,1024]{2,1,0:T(8,128)(2,1)S(1)} collective-permute-done((bf16[1,64,1024]{2,1,0:T(8,128)(2,1)S(1)}, bf16[1,64,1024]{2,1,0:T(8,128)(2,1)S(1)}, u32[]{:S(2)}, u32[]{:S(2)}) %collective-permute-start.1) | collective-permute-done | bytes 131104 | tf_op jit(solution)/shard_map/ppermute | solution.py:278
  7.3 1.4 %collective-permute-done = bf16[1,64,1024]{2,1,0:T(8,128)(2,1)S(1)} collective-permute-done((bf16[1,64,1024]{2,1,0:T(8,128)(2,1)S(1)}, bf16[1,64,1024]{2,1,0:T(8,128)(2,1)S(1)}, u32[]{:S(2)}, u32[]{:S(2)}) %collective-permute-start) | collective-permute-done | bytes 131104 | tf_op jit(solution)/shard_map/ppermute | solution.py:278
  8.7 2.8 %collective-permute-start.2 = (bf16[2,64,1024]{2,1,0:T(8,128)(2,1)S(1)}, bf16[2,64,1024]{2,1,0:T(8,128)(2,1)S(1)}, u32[]{:S(2)}, u32[]{:S(2)}) collective-permute-start(bf16[2,64,1024]{2,1,0:T(8,128)(2,1)S(1)} %pad_maximum_fusion.2), channel_id=1, source_target_pairs={{0,24},{8,16},{16,8},{24,0},{32,56},{40,48},{48,40},{56,32},{64,88... | collective-permute-start | bytes 786440 | tf_op jit(solution)/shard_map/ppermute | solution.py:278
  11.6 2.5 %collective-permute-start.3 = (bf16[2,64,1024]{2,1,0:T(8,128)(2,1)S(1)}, bf16[2,64,1024]{2,1,0:T(8,128)(2,1)S(1)}, u32[]{:S(2)}, u32[]{:S(2)}) collective-permute-start(bf16[2,64,1024]{2,1,0:T(8,128)(2,1)S(1)} %pad_maximum_fusion.3), channel_id=1, source_target_pairs={{0,96},{8,104},{16,112},{24,120},{32,64},{40,72},{48,80},{56,88},{... | collective-permute-start | bytes 786440 | tf_op jit(solution)/shard_map/ppermute | solution.py:278
  14.4 3.2 %collective-permute-done.2 = bf16[2,64,1024]{2,1,0:T(8,128)(2,1)S(1)} collective-permute-done((bf16[2,64,1024]{2,1,0:T(8,128)(2,1)S(1)}, bf16[2,64,1024]{2,1,0:T(8,128)(2,1)S(1)}, u32[]{:S(2)}, u32[]{:S(2)}) %collective-permute-start.2) | collective-permute-done | bytes 262176 | tf_op jit(solution)/shard_map/ppermute | solution.py:278
  17.7 2.4 %collective-permute-done.3 = bf16[2,64,1024]{2,1,0:T(8,128)(2,1)S(1)} collective-permute-done((bf16[2,64,1024]{2,1,0:T(8,128)(2,1)S(1)}, bf16[2,64,1024]{2,1,0:T(8,128)(2,1)S(1)}, u32[]{:S(2)}, u32[]{:S(2)}) %collective-permute-start.3) | collective-permute-done | bytes 262176 | tf_op jit(solution)/shard_map/ppermute | solution.py:278
  20.2 2.8 %collective-permute-start.6 = (bf16[4,64,1024]{2,1,0:T(8,128)(2,1)S(1)}, bf16[4,64,1024]{2,1,0:T(8,128)(2,1)S(1)}, u32[]{:S(2)}, u32[]{:S(2)}) collective-permute-start(bf16[4,64,1024]{2,1,0:T(8,128)(2,1)S(1)} %pad_maximum_fusion.refs_0_), channel_id=1, source_target_pairs={{0,96},{8,104},{16,112},{24,120},{32,0},{40,8},{48,16},{56,24},{64... | collective-permute-start | bytes 1572872 | tf_op jit(solution)/shard_map/ppermute | solution.py:275
  23.5 1.5 %collective-permute-start.5 = (bf16[4,64,1024]{2,1,0:T(8,128)(2,1)S(1)}, bf16[4,64,1024]{2,1,0:T(8,128)(2,1)S(1)}, u32[]{:S(2)}, u32[]{:S(2)}) collective-permute-start(bf16[4,64,1024]{2,1,0:T(8,128)(2,1)S(1)} %pad_maximum_fusion.1.refs_1_), channel_id=1, source_target_pairs={{0,8},{8,16},{16,24},{24,0},{32,40},{40,48},{48,56},{56,32},{64,72... | collective-permute-start | bytes 1572872 | tf_op jit(solution)/shard_map/ppermute | solution.py:275
  25.1 0.8 copy-done
  26.6 6.3 %collective-permute-done.6.refs_0_ = bf16[4,64,1024]{2,1,0:T(8,128)(2,1)S(1)} collective-permute-done((bf16[4,64,1024]{2,1,0:T(8,128)(2,1)S(1)}, bf16[4,64,1024]{2,1,0:T(8,128)(2,1)S(1)}, u32[]{:S(2)}, u32[]{:S(2)}) %collective-permute-start.6) | collective-permute-done | bytes 524320 | tf_op jit(solution)/shard_map/ppermute | solution.py:275
  32.8 3.4 %collective-permute-done.4.refs_0_ = bf16[4,64,1024]{2,1,0:T(8,128)(2,1)S(1)} collective-permute-done((bf16[4,64,1024]{2,1,0:T(8,128)(2,1)S(1)}, bf16[4,64,1024]{2,1,0:T(8,128)(2,1)S(1)}, u32[]{:S(2)}, u32[]{:S(2)}) %collective-permute-start.4) | collective-permute-done | bytes 524320 | tf_op jit(solution)/shard_map/ppermute | solution.py:275
  37.4 2.2 %copy-done.2 = bf16[1,8192,256]{2,1,0:T(8,128)(2,1)S(1)} copy-done((bf16[1,8192,256]{2,1,0:T(8,128)(2,1)S(1)}, bf16[1,8192,256]{2,1,0:T(8,128)(2,1)}, u32[]{:S(2)}) %copy-start.2) | copy-done | bytes 4194328
  39.5 3.8 %attend.5 = (f32[4,144,512]{2,1,0:T(8,128)S(1)}, f32[4,144,512]{2,1,0:T(8,128)S(1)}) custom-call(s32[3]{0:T(128)S(1)} %pad_add_fusion.place_ref, s32[32]{0:T(128)S(1)} %broadcast_add_fusion.count_ref, s32[512]{0:T(512)S(1)} %select_n.44.ids_ref, bf16[8192,256]{1,0:T(8,128)(2,1)S(1)} %bitcast.15, bf16[4,64,1024]{2,1,0:T(8,128)(2,1)S(1)} %collective-permute-done.4.refs_0_, ...), custom_call_target="tpu_custom_call" | custom-call | flops 4000000000 | bytes 1048576 | tf_op jit(solution)/shard_map/attend/pallas_call | solution.py:160
  43.4 5.5 %collective-permute-done.8.refs_0_ = bf16[4,64,1024]{2,1,0:T(8,128)(2,1)} collective-permute-done((bf16[4,64,1024]{2,1,0:T(8,128)(2,1)S(1)}, bf16[4,64,1024]{2,1,0:T(8,128)(2,1)}, u32[]{:S(2)}, u32[]{:S(2)}) %collective-permute-start.8) | collective-permute-done | bytes 524320 | tf_op jit(solution)/shard_map/ppermute | solution.py:275
  49.1 5.0 %attend.7 = (bf16[2,144,512]{2,1,0:T(8,128)(2,1)S(1)}, bf16[2,144,512]{2,1,0:T(8,128)(2,1)S(1)}, bf16[2,144,512]{2,1,0:T(8,128)(2,1)S(1)}, bf16[2,144,512]{2,1,0:T(8,128)(2,1)S(1)}) custom-call(s32[3]{0:T(128)S(1)} %pad_add_fusion.place_ref, s32[32]{0:T(128)S(1)} %broadcast_add_fusion.count_ref, s32[512]{0:T(512)S(1)} %select_n.44.ids_ref, ...), custom_call_target="tpu_custom_call" | custom-call | flops 4000000000 | bytes 1048576 | tf_op jit(solution)/shard_map/attend/pallas_call | solution.py:160
  54.1 2.8 %collective-permute-start.10 = (bf16[2,144,512]{2,1,0:T(8,128)(2,1)S(1)}, bf16[2,144,512]{2,1,0:T(8,128)(2,1)S(1)}, u32[]{:S(2)}, u32[]{:S(2)}) collective-permute-start(bf16[2,144,512]{2,1,0:T(8,128)(2,1)S(1)} %get-tuple-element.48), channel_id=1, source_target_pairs={{0,96},{8,104},{16,112},{24,120},{32,0},{40,8},{48,16},{56,24},{64... | collective-permute-start | bytes 884744 | tf_op jit(solution)/shard_map/ppermute | solution.py:275
  56.9 0.9 collective-permute-start.12
  57.8 1.2 collective-permute-start.13
  58.9 4.4 %attend.6 = (f32[4,144,512]{2,1,0:T(8,128)S(1)}, f32[4,144,512]{2,1,0:T(8,128)S(1)}) custom-call(s32[3]{0:T(128)S(1)} %pad_add_fusion.place_ref, s32[32]{0:T(128)S(1)} %broadcast_add_fusion.count_ref, s32[512]{0:T(512)S(1)} %select_n.44.ids_ref, bf16[8192,256]{1,0:T(8,128)(2,1)S(1)} %bitcast.17, bf16[4,64,1024]{2,1,0:T(8,128)(2,1)S(1)} %collective-permute-done.6.refs_0_, ...), custom_call_target="tpu_custom_call" | custom-call | flops 4000000000 | bytes 1048576 | tf_op jit(solution)/shard_map/attend/pallas_call | solution.py:160
  63.4 1.5 %collective-permute-done.11.refs_3_ = bf16[2,144,512]{2,1,0:T(8,128)(2,1)S(1)} collective-permute-done((bf16[2,144,512]{2,1,0:T(8,128)(2,1)S(1)}, bf16[2,144,512]{2,1,0:T(8,128)(2,1)S(1)}, u32[]{:S(2)}, u32[]{:S(2)}) %collective-permute-start.11) | collective-permute-done | bytes 294944 | tf_op jit(solution)/shard_map/ppermute | solution.py:275
  64.9 0.8 collective-permute-done.13.refs_7_
  66.5 3.1 %collective-permute-start.15 = (bf16[4,144,512]{2,1,0:T(8,128)(2,1)S(1)}, bf16[4,144,512]{2,1,0:T(8,128)(2,1)S(1)}, u32[]{:S(2)}, u32[]{:S(2)}) collective-permute-start(bf16[4,144,512]{2,1,0:T(8,128)(2,1)S(1)} %get-tuple-element.55), channel_id=1, source_target_pairs={{0,96},{8,104},{16,112},{24,120},{32,0},{40,8},{48,16},{56,24},{64... | collective-permute-start | bytes 1769480 | tf_op jit(solution)/shard_map/ppermute | solution.py:275
  69.6 1.0 collective-permute-start.16
  70.6 2.3 %collective-permute-start.17 = (bf16[4,144,512]{2,1,0:T(8,128)(2,1)S(1)}, bf16[4,144,512]{2,1,0:T(8,128)(2,1)S(1)}, u32[]{:S(2)}, u32[]{:S(2)}) collective-permute-start(bf16[4,144,512]{2,1,0:T(8,128)(2,1)S(1)} %get-tuple-element.58), channel_id=1, source_target_pairs={{0,24},{8,0},{16,8},{24,16},{32,56},{40,32},{48,40},{56,48},{64,88... | collective-permute-start | bytes 1769480 | tf_op jit(solution)/shard_map/ppermute | solution.py:275
  72.9 3.8 %attend.4 = (f32[4,144,512]{2,1,0:T(8,128)S(1)}, f32[4,144,512]{2,1,0:T(8,128)S(1)}) custom-call(s32[3]{0:T(128)S(1)} %pad_add_fusion.place_ref, s32[32]{0:T(128)S(1)} %broadcast_add_fusion.count_ref, s32[512]{0:T(512)S(1)} %select_n.44.ids_ref, bf16[8192,256]{1,0:T(8,128)(2,1)S(1)} %bitcast.18, bf16[4,64,1024]{2,1,0:T(8,128)(2,1)S(1)} %pad_maximum_fusion.refs_0_, ...), custom_call_target="tpu_custom_call" | custom-call | flops 4000000000 | bytes 1048576 | tf_op jit(solution)/shard_map/attend/pallas_call | solution.py:160
  76.7 0.8 collective-permute-done.14.refs_1_
  77.5 6.4 %collective-permute-done.16.refs_4_ = bf16[4,144,512]{2,1,0:T(8,128)(2,1)S(1)} collective-permute-done((bf16[4,144,512]{2,1,0:T(8,128)(2,1)S(1)}, bf16[4,144,512]{2,1,0:T(8,128)(2,1)S(1)}, u32[]{:S(2)}, u32[]{:S(2)}) %collective-permute-start.16) | collective-permute-done | bytes 589856 | tf_op jit(solution)/shard_map/ppermute | solution.py:275
  84.7 3.3 %collective-permute-start.19 = (bf16[1,144,512]{2,1,0:T(8,128)(2,1)S(1)}, bf16[1,144,512]{2,1,0:T(8,128)(2,1)S(1)}, u32[]{:S(2)}, u32[]{:S(2)}) collective-permute-start(bf16[1,144,512]{2,1,0:T(8,128)(2,1)S(1)} %get-tuple-element.61), channel_id=1, source_target_pairs={{0,24},{8,16},{16,8},{24,0},{32,56},{40,48},{48,40},{56,32},{64,88... | collective-permute-start | bytes 442376 | tf_op jit(solution)/shard_map/ppermute | solution.py:278
  88.0 1.4 %collective-permute-start.20 = (bf16[1,144,512]{2,1,0:T(8,128)(2,1)S(1)}, bf16[1,144,512]{2,1,0:T(8,128)(2,1)S(1)}, u32[]{:S(2)}, u32[]{:S(2)}) collective-permute-start(bf16[1,144,512]{2,1,0:T(8,128)(2,1)S(1)} %get-tuple-element.62), channel_id=1, source_target_pairs={{0,16},{8,24},{16,0},{24,8},{32,48},{40,56},{48,32},{56,40},{64,80... | collective-permute-start | bytes 442376 | tf_op jit(solution)/shard_map/ppermute | solution.py:278
  89.8 1.7 %collective-permute-start.22 = (bf16[1,144,512]{2,1,0:T(8,128)(2,1)S(1)}, bf16[1,144,512]{2,1,0:T(8,128)(2,1)S(1)}, u32[]{:S(2)}, u32[]{:S(2)}) collective-permute-start(bf16[1,144,512]{2,1,0:T(8,128)(2,1)S(1)} %get-tuple-element.65), channel_id=1, source_target_pairs={{0,96},{8,104},{16,112},{24,120},{32,64},{40,72},{48,80},{56,88},{... | collective-permute-start | bytes 442376 | tf_op jit(solution)/shard_map/ppermute | solution.py:278
  91.5 0.8 collective-permute-done.19.refs_2_
  92.3 1.2 collective-permute-start.23
  93.5 1.2 collective-permute-done.20.refs_3_
  94.7 1.5 %collective-permute-done.22.refs_6_ = bf16[1,144,512]{2,1,0:T(8,128)(2,1)S(1)} collective-permute-done((bf16[1,144,512]{2,1,0:T(8,128)(2,1)S(1)}, bf16[1,144,512]{2,1,0:T(8,128)(2,1)S(1)}, u32[]{:S(2)}, u32[]{:S(2)}) %collective-permute-start.22) | collective-permute-done | bytes 147488 | tf_op jit(solution)/shard_map/ppermute | solution.py:278
  96.2 2.8 %collective-permute-done.23.refs_7_ = bf16[1,144,512]{2,1,0:T(8,128)(2,1)S(1)} collective-permute-done((bf16[1,144,512]{2,1,0:T(8,128)(2,1)S(1)}, bf16[1,144,512]{2,1,0:T(8,128)(2,1)S(1)}, u32[]{:S(2)}, u32[]{:S(2)}) %collective-permute-start.23) | collective-permute-done | bytes 147488 | tf_op jit(solution)/shard_map/ppermute | solution.py:278
  99.3 1.5 %collective-permute-done.24.other_ref = bf16[128,1024]{1,0:T(8,128)(2,1)S(1)} collective-permute-done((bf16[128,1024]{1,0:T(8,128)(2,1)S(1)}, bf16[128,1024]{1,0:T(8,128)(2,1)S(1)}, u32[]{:S(2)}, u32[]{:S(2)}) %collective-permute-start.24) | collective-permute-done | bytes 262176 | tf_op jit(solution)/shard_map/ppermute | solution.py:281
  100.9 2.9 %project.5 = bf16[128,1024]{1,0:T(8,128)(2,1)S(1)} custom-call(s32[3]{0:T(128)S(1)} %pad_add_fusion.place_ref, bf16[128,1024]{1,0:T(8,128)(2,1)S(1)} %final.1.att_ref, bf16[128,1024]{1,0:T(8,128)(2,1)S(1)} %collective-permute-done.24.other_ref, bf16[1024,8192]{1,0:T(8,128)(2,1)S(1)} %bitcast.12, bf16[1024,8192]{1,0:T(8,128)(2,1)} %collective-permute-done.25.wo_ref), custom_call_target="tpu_custom_call" | custom-call | flops 3000000000 | bytes 1048576 | tf_op jit(solution)/shard_map/project/pallas_call | solution.py:249
  103.8 3.5 %collective-permute-start.27 = (bf16[128,1024]{1,0:T(8,128)(2,1)S(1)}, bf16[128,1024]{1,0:T(8,128)(2,1)S(1)}, u32[]{:S(2)}, u32[]{:S(2)}) collective-permute-start(bf16[128,1024]{1,0:T(8,128)(2,1)S(1)} %project.5), channel_id=1, source_target_pairs={{0,4},{1,5},{2,6},{3,7},{4,0},{5,1},{6,2},{7,3},{8,12},{9,13},{10,... | collective-permute-start | bytes 786440 | tf_op jit(solution)/shard_map/ppermute | solution.py:281
  107.3 3.8 %project.4 = (bf16[128,1024]{1,0:T(8,128)(2,1)S(1)}, bf16[128,1024]{1,0:T(8,128)(2,1)S(1)}) custom-call(s32[3]{0:T(128)S(1)} %pad_add_fusion.place_ref, bf16[128,1024]{1,0:T(8,128)(2,1)S(1)} %final.1.att_ref, bf16[128,1024]{1,0:T(8,128)(2,1)S(1)} %collective-permute-done.24.other_ref, bf16[1024,8192]{1,0:T(8,128)(2,1)S(1)} %bitcast.13, ...), custom_call_target="tpu_custom_call" | custom-call | flops 6000000000 | bytes 1048576 | tf_op jit(solution)/shard_map/project/pallas_call | solution.py:249
  111.1 0.7 collective-permute-start.26
  111.8 2.6 %collective-permute-start.28 = (bf16[128,1024]{1,0:T(8,128)(2,1)S(1)}, bf16[128,1024]{1,0:T(8,128)(2,1)S(1)}, u32[]{:S(2)}, u32[]{:S(2)}) collective-permute-start(bf16[128,1024]{1,0:T(8,128)(2,1)S(1)} %get-tuple-element.68), channel_id=1, source_target_pairs={{0,6},{1,7},{2,0},{3,1},{4,2},{5,3},{6,4},{7,5},{8,14},{9,15},{10,... | collective-permute-start | bytes 786440 | tf_op jit(solution)/shard_map/ppermute | solution.py:281
  114.4 2.9 %project.3 = f32[128,1024]{1,0:T(8,128)S(1)} custom-call(s32[3]{0:T(128)S(1)} %pad_add_fusion.place_ref, bf16[128,1024]{1,0:T(8,128)(2,1)S(1)} %final.1.att_ref, bf16[128,1024]{1,0:T(8,128)(2,1)S(1)} %collective-permute-done.24.other_ref, bf16[1024,8192]{1,0:T(8,128)(2,1)S(1)} %bitcast.14, bf16[1024,8192]{1,0:T(8,128)(2,1)} %collective-permute-done.25.wo_ref), custom_call_target="tpu_custom_call" | custom-call | flops 3000000000 | bytes 1048576 | tf_op jit(solution)/shard_map/project/pallas_call | solution.py:249
  117.3 3.1 %collective-permute-done.26 = bf16[128,1024]{1,0:T(8,128)(2,1)S(1)} collective-permute-done((bf16[128,1024]{1,0:T(8,128)(2,1)S(1)}, bf16[128,1024]{1,0:T(8,128)(2,1)S(1)}, u32[]{:S(2)}, u32[]{:S(2)}) %collective-permute-start.26) | collective-permute-done | bytes 262176 | tf_op jit(solution)/shard_map/ppermute | solution.py:281
  120.4 0.9 convert_add_fusion
  (55 shorter events, 5.5 us)
Async XLA Ops:
  0.0 100.9 %collective-permute-start.25 = (bf16[1024,8192]{1,0:T(8,128)(2,1)}, bf16[1024,8192]{1,0:T(8,128)(2,1)}, u32[]{:S(2)}, u32[]{:S(2)}) collective-permute-start(bf16[1024,8192]{1,0:T(8,128)(2,1)} %bitcast.9), channel_id=1, source_target_pairs={{0,1},{1,0},{2,3},{3,2},{4,5},{5,4},{6,7},{7,6},{8,9},{9,8},{10,11... | collective-permute-start | bytes 50331656 | tf_op jit(solution)/shard_map/ppermute | solution.py:281
  1.0 6.2 %collective-permute-start.1 = (bf16[1,64,1024]{2,1,0:T(8,128)(2,1)S(1)}, bf16[1,64,1024]{2,1,0:T(8,128)(2,1)S(1)}, u32[]{:S(2)}, u32[]{:S(2)}) collective-permute-start(bf16[1,64,1024]{2,1,0:T(8,128)(2,1)S(1)} %get-tuple-element.71), channel_id=1, source_target_pairs={{0,32},{8,40},{16,48},{24,56},{32,0},{40,8},{48,16},{56,24},{64,96... | collective-permute-start | bytes 393224 | tf_op jit(solution)/shard_map/ppermute | solution.py:278
  3.1 5.6 %collective-permute-start = (bf16[1,64,1024]{2,1,0:T(8,128)(2,1)S(1)}, bf16[1,64,1024]{2,1,0:T(8,128)(2,1)S(1)}, u32[]{:S(2)}, u32[]{:S(2)}) collective-permute-start(bf16[1,64,1024]{2,1,0:T(8,128)(2,1)S(1)} %get-tuple-element.72), channel_id=1, source_target_pairs={{0,8},{8,0},{16,24},{24,16},{32,40},{40,32},{48,56},{56,48},{64,72... | collective-permute-start | bytes 393224 | tf_op jit(solution)/shard_map/ppermute | solution.py:278
  8.7 17.1 %copy-start.3 = (s32[32,64]{1,0:T(8,128)S(1)}, s32[32,64]{1,0:T(8,128)}, u32[]{:S(2)}) copy-start(s32[32,64]{1,0:T(8,128)} %param.6) | copy-start | bytes 24580
  8.7 8.9 %collective-permute-start.2 = (bf16[2,64,1024]{2,1,0:T(8,128)(2,1)S(1)}, bf16[2,64,1024]{2,1,0:T(8,128)(2,1)S(1)}, u32[]{:S(2)}, u32[]{:S(2)}) collective-permute-start(bf16[2,64,1024]{2,1,0:T(8,128)(2,1)S(1)} %pad_maximum_fusion.2), channel_id=1, source_target_pairs={{0,24},{8,16},{16,8},{24,0},{32,56},{40,48},{48,40},{56,32},{64,88... | collective-permute-start | bytes 786440 | tf_op jit(solution)/shard_map/ppermute | solution.py:278
  11.6 8.5 %collective-permute-start.3 = (bf16[2,64,1024]{2,1,0:T(8,128)(2,1)S(1)}, bf16[2,64,1024]{2,1,0:T(8,128)(2,1)S(1)}, u32[]{:S(2)}, u32[]{:S(2)}) collective-permute-start(bf16[2,64,1024]{2,1,0:T(8,128)(2,1)S(1)} %pad_maximum_fusion.3), channel_id=1, source_target_pairs={{0,96},{8,104},{16,112},{24,120},{32,64},{40,72},{48,80},{56,88},{... | collective-permute-start | bytes 786440 | tf_op jit(solution)/shard_map/ppermute | solution.py:278
  20.2 12.6 %collective-permute-start.6 = (bf16[4,64,1024]{2,1,0:T(8,128)(2,1)S(1)}, bf16[4,64,1024]{2,1,0:T(8,128)(2,1)S(1)}, u32[]{:S(2)}, u32[]{:S(2)}) collective-permute-start(bf16[4,64,1024]{2,1,0:T(8,128)(2,1)S(1)} %pad_maximum_fusion.refs_0_), channel_id=1, source_target_pairs={{0,96},{8,104},{16,112},{24,120},{32,0},{40,8},{48,16},{56,24},{64... | collective-permute-start | bytes 1572872 | tf_op jit(solution)/shard_map/ppermute | solution.py:275
  23.0 13.2 %collective-permute-start.4 = (bf16[4,64,1024]{2,1,0:T(8,128)(2,1)S(1)}, bf16[4,64,1024]{2,1,0:T(8,128)(2,1)S(1)}, u32[]{:S(2)}, u32[]{:S(2)}) collective-permute-start(bf16[4,64,1024]{2,1,0:T(8,128)(2,1)S(1)} %pad_maximum_fusion.refs_0_), channel_id=1, source_target_pairs={{0,32},{8,40},{16,48},{24,56},{32,64},{40,72},{48,80},{56,88},{64,... | collective-permute-start | bytes 1572872 | tf_op jit(solution)/shard_map/ppermute | solution.py:275
  23.0 13.2 %collective-permute-start.7 = (bf16[4,64,1024]{2,1,0:T(8,128)(2,1)S(1)}, bf16[4,64,1024]{2,1,0:T(8,128)(2,1)S(1)}, u32[]{:S(2)}, u32[]{:S(2)}) collective-permute-start(bf16[4,64,1024]{2,1,0:T(8,128)(2,1)S(1)} %pad_maximum_fusion.1.refs_1_), channel_id=1, source_target_pairs={{0,24},{8,0},{16,8},{24,16},{32,56},{40,32},{48,40},{56,48},{64,88... | collective-permute-start | bytes 1572872 | tf_op jit(solution)/shard_map/ppermute | solution.py:275
  23.5 13.1 %collective-permute-start.5 = (bf16[4,64,1024]{2,1,0:T(8,128)(2,1)S(1)}, bf16[4,64,1024]{2,1,0:T(8,128)(2,1)S(1)}, u32[]{:S(2)}, u32[]{:S(2)}) collective-permute-start(bf16[4,64,1024]{2,1,0:T(8,128)(2,1)S(1)} %pad_maximum_fusion.1.refs_1_), channel_id=1, source_target_pairs={{0,8},{8,16},{16,24},{24,0},{32,40},{40,48},{48,56},{56,32},{64,72... | collective-permute-start | bytes 1572872 | tf_op jit(solution)/shard_map/ppermute | solution.py:275
  25.1 0.8 copy-start
  36.6 12.3 %collective-permute-start.8 = (bf16[4,64,1024]{2,1,0:T(8,128)(2,1)S(1)}, bf16[4,64,1024]{2,1,0:T(8,128)(2,1)}, u32[]{:S(2)}, u32[]{:S(2)}) collective-permute-start(bf16[4,64,1024]{2,1,0:T(8,128)(2,1)S(1)} %collective-permute-done.4.refs_0_), channel_id=1, source_target_pairs={{0,32},{8,40},{16,48},{24,56},{32,64},{40,72},{48,80},{56,88},{64,... | collective-permute-start | bytes 1572872 | tf_op jit(solution)/shard_map/ppermute | solution.py:275
  37.2 11.9 %collective-permute-start.9 = (bf16[4,64,1024]{2,1,0:T(8,128)(2,1)S(1)}, bf16[4,64,1024]{2,1,0:T(8,128)(2,1)}, u32[]{:S(2)}, u32[]{:S(2)}) collective-permute-start(bf16[4,64,1024]{2,1,0:T(8,128)(2,1)S(1)} %collective-permute-done.5.refs_1_), channel_id=1, source_target_pairs={{0,8},{8,16},{16,24},{24,0},{32,40},{40,48},{48,56},{56,32},{64,72... | collective-permute-start | bytes 1572872 | tf_op jit(solution)/shard_map/ppermute | solution.py:275
  37.4 2.2 %copy-start.2 = (bf16[1,8192,256]{2,1,0:T(8,128)(2,1)S(1)}, bf16[1,8192,256]{2,1,0:T(8,128)(2,1)}, u32[]{:S(2)}) copy-start(bf16[1,8192,256]{2,1,0:T(8,128)(2,1)} %param.5) | copy-start | bytes 12582916
  54.1 9.3 %collective-permute-start.10 = (bf16[2,144,512]{2,1,0:T(8,128)(2,1)S(1)}, bf16[2,144,512]{2,1,0:T(8,128)(2,1)S(1)}, u32[]{:S(2)}, u32[]{:S(2)}) collective-permute-start(bf16[2,144,512]{2,1,0:T(8,128)(2,1)S(1)} %get-tuple-element.48), channel_id=1, source_target_pairs={{0,96},{8,104},{16,112},{24,120},{32,0},{40,8},{48,16},{56,24},{64... | collective-permute-start | bytes 884744 | tf_op jit(solution)/shard_map/ppermute | solution.py:275
  56.9 8.0 %collective-permute-start.11 = (bf16[2,144,512]{2,1,0:T(8,128)(2,1)S(1)}, bf16[2,144,512]{2,1,0:T(8,128)(2,1)S(1)}, u32[]{:S(2)}, u32[]{:S(2)}) collective-permute-start(bf16[2,144,512]{2,1,0:T(8,128)(2,1)S(1)} %get-tuple-element.49), channel_id=1, source_target_pairs={{0,32},{8,40},{16,48},{24,56},{32,64},{40,72},{48,80},{56,88},{64,... | collective-permute-start | bytes 884744 | tf_op jit(solution)/shard_map/ppermute | solution.py:275
  56.9 8.0 %collective-permute-start.12 = (bf16[2,144,512]{2,1,0:T(8,128)(2,1)S(1)}, bf16[2,144,512]{2,1,0:T(8,128)(2,1)S(1)}, u32[]{:S(2)}, u32[]{:S(2)}) collective-permute-start(bf16[2,144,512]{2,1,0:T(8,128)(2,1)S(1)} %get-tuple-element.52), channel_id=1, source_target_pairs={{0,24},{8,0},{16,8},{24,16},{32,56},{40,32},{48,40},{56,48},{64,88... | collective-permute-start | bytes 884744 | tf_op jit(solution)/shard_map/ppermute | solution.py:275
  57.8 7.9 %collective-permute-start.13 = (bf16[2,144,512]{2,1,0:T(8,128)(2,1)S(1)}, bf16[2,144,512]{2,1,0:T(8,128)(2,1)S(1)}, u32[]{:S(2)}, u32[]{:S(2)}) collective-permute-start(bf16[2,144,512]{2,1,0:T(8,128)(2,1)S(1)} %get-tuple-element.53), channel_id=1, source_target_pairs={{0,8},{8,16},{16,24},{24,0},{32,40},{40,48},{48,56},{56,32},{64,72... | collective-permute-start | bytes 884744 | tf_op jit(solution)/shard_map/ppermute | solution.py:275
  58.9 41.9 %slice-start = ((s8[16777216]{0:T(1024)(128)(4,1)}), s8[4194304]{0:T(1024)(128)(4,1)S(1)}, s32[]{:S(2)}) async-start(s8[16777216]{0:T(1024)(128)(4,1)} %bitcast.10), calls=%async_computation | async-start | bytes 8388608
  58.9 41.9 %slice-start.1 = ((s8[16777216]{0:T(1024)(128)(4,1)}), s8[4194304]{0:T(1024)(128)(4,1)S(1)}, s32[]{:S(2)}) async-start(s8[16777216]{0:T(1024)(128)(4,1)} %bitcast.10), calls=%async_computation.1 | async-start | bytes 8388608
  65.7 7.2 %copy-start.1 = (bf16[4,64,1024]{2,1,0:T(8,128)(2,1)S(1)}, bf16[4,64,1024]{2,1,0:T(8,128)(2,1)}, u32[]{:S(2)}) copy-start(bf16[4,64,1024]{2,1,0:T(8,128)(2,1)} %copy-done) | copy-start | bytes 1572868
  66.3 11.2 %collective-permute-start.14 = (bf16[4,144,512]{2,1,0:T(8,128)(2,1)S(1)}, bf16[4,144,512]{2,1,0:T(8,128)(2,1)S(1)}, u32[]{:S(2)}, u32[]{:S(2)}) collective-permute-start(bf16[4,144,512]{2,1,0:T(8,128)(2,1)S(1)} %get-tuple-element.54), channel_id=1, source_target_pairs={{0,32},{8,40},{16,48},{24,56},{32,64},{40,72},{48,80},{56,88},{64,... | collective-permute-start | bytes 1769480 | tf_op jit(solution)/shard_map/ppermute | solution.py:275
  66.5 11.0 %collective-permute-start.15 = (bf16[4,144,512]{2,1,0:T(8,128)(2,1)S(1)}, bf16[4,144,512]{2,1,0:T(8,128)(2,1)S(1)}, u32[]{:S(2)}, u32[]{:S(2)}) collective-permute-start(bf16[4,144,512]{2,1,0:T(8,128)(2,1)S(1)} %get-tuple-element.55), channel_id=1, source_target_pairs={{0,96},{8,104},{16,112},{24,120},{32,0},{40,8},{48,16},{56,24},{64... | collective-permute-start | bytes 1769480 | tf_op jit(solution)/shard_map/ppermute | solution.py:275
  69.6 14.3 %collective-permute-start.16 = (bf16[4,144,512]{2,1,0:T(8,128)(2,1)S(1)}, bf16[4,144,512]{2,1,0:T(8,128)(2,1)S(1)}, u32[]{:S(2)}, u32[]{:S(2)}) collective-permute-start(bf16[4,144,512]{2,1,0:T(8,128)(2,1)S(1)} %get-tuple-element.57), channel_id=1, source_target_pairs={{0,8},{8,16},{16,24},{24,0},{32,40},{40,48},{48,56},{56,32},{64,72... | collective-permute-start | bytes 1769480 | tf_op jit(solution)/shard_map/ppermute | solution.py:275
  70.6 30.3 %slice-start.2 = ((s8[16777216]{0:T(1024)(128)(4,1)}), s8[4194304]{0:T(1024)(128)(4,1)S(1)}, s32[]{:S(2)}) async-start(s8[16777216]{0:T(1024)(128)(4,1)} %bitcast.10), calls=%async_computation.2 | async-start | bytes 8388608
  70.6 30.3 %slice-start.3 = ((s8[16777216]{0:T(1024)(128)(4,1)}), s8[4194304]{0:T(1024)(128)(4,1)S(1)}, s32[]{:S(2)}) async-start(s8[16777216]{0:T(1024)(128)(4,1)} %bitcast.10), calls=%async_computation.3 | async-start | bytes 8388608
  70.6 13.3 %collective-permute-start.17 = (bf16[4,144,512]{2,1,0:T(8,128)(2,1)S(1)}, bf16[4,144,512]{2,1,0:T(8,128)(2,1)S(1)}, u32[]{:S(2)}, u32[]{:S(2)}) collective-permute-start(bf16[4,144,512]{2,1,0:T(8,128)(2,1)S(1)} %get-tuple-element.58), channel_id=1, source_target_pairs={{0,24},{8,0},{16,8},{24,16},{32,56},{40,32},{48,40},{56,48},{64,88... | collective-permute-start | bytes 1769480 | tf_op jit(solution)/shard_map/ppermute | solution.py:275
  84.6 5.2 %collective-permute-start.18 = (bf16[1,144,512]{2,1,0:T(8,128)(2,1)S(1)}, bf16[1,144,512]{2,1,0:T(8,128)(2,1)S(1)}, u32[]{:S(2)}, u32[]{:S(2)}) collective-permute-start(bf16[1,144,512]{2,1,0:T(8,128)(2,1)S(1)} %get-tuple-element.60), channel_id=1, source_target_pairs={{0,8},{8,0},{16,24},{24,16},{32,40},{40,32},{48,56},{56,48},{64,72... | collective-permute-start | bytes 442376 | tf_op jit(solution)/shard_map/ppermute | solution.py:278
  84.7 7.6 %collective-permute-start.19 = (bf16[1,144,512]{2,1,0:T(8,128)(2,1)S(1)}, bf16[1,144,512]{2,1,0:T(8,128)(2,1)S(1)}, u32[]{:S(2)}, u32[]{:S(2)}) collective-permute-start(bf16[1,144,512]{2,1,0:T(8,128)(2,1)S(1)} %get-tuple-element.61), channel_id=1, source_target_pairs={{0,24},{8,16},{16,8},{24,0},{32,56},{40,48},{48,40},{56,32},{64,88... | collective-permute-start | bytes 442376 | tf_op jit(solution)/shard_map/ppermute | solution.py:278
  88.0 6.6 %collective-permute-start.20 = (bf16[1,144,512]{2,1,0:T(8,128)(2,1)S(1)}, bf16[1,144,512]{2,1,0:T(8,128)(2,1)S(1)}, u32[]{:S(2)}, u32[]{:S(2)}) collective-permute-start(bf16[1,144,512]{2,1,0:T(8,128)(2,1)S(1)} %get-tuple-element.62), channel_id=1, source_target_pairs={{0,16},{8,24},{16,0},{24,8},{32,48},{40,56},{48,32},{56,40},{64,80... | collective-permute-start | bytes 442376 | tf_op jit(solution)/shard_map/ppermute | solution.py:278
  89.4 5.3 %collective-permute-start.21 = (bf16[1,144,512]{2,1,0:T(8,128)(2,1)S(1)}, bf16[1,144,512]{2,1,0:T(8,128)(2,1)S(1)}, u32[]{:S(2)}, u32[]{:S(2)}) collective-permute-start(bf16[1,144,512]{2,1,0:T(8,128)(2,1)S(1)} %get-tuple-element.64), channel_id=1, source_target_pairs={{0,32},{8,40},{16,48},{24,56},{32,0},{40,8},{48,16},{56,24},{64,96... | collective-permute-start | bytes 442376 | tf_op jit(solution)/shard_map/ppermute | solution.py:278
  89.8 6.4 %collective-permute-start.22 = (bf16[1,144,512]{2,1,0:T(8,128)(2,1)S(1)}, bf16[1,144,512]{2,1,0:T(8,128)(2,1)S(1)}, u32[]{:S(2)}, u32[]{:S(2)}) collective-permute-start(bf16[1,144,512]{2,1,0:T(8,128)(2,1)S(1)} %get-tuple-element.65), channel_id=1, source_target_pairs={{0,96},{8,104},{16,112},{24,120},{32,64},{40,72},{48,80},{56,88},{... | collective-permute-start | bytes 442376 | tf_op jit(solution)/shard_map/ppermute | solution.py:278
  92.3 6.6 %collective-permute-start.23 = (bf16[1,144,512]{2,1,0:T(8,128)(2,1)S(1)}, bf16[1,144,512]{2,1,0:T(8,128)(2,1)S(1)}, u32[]{:S(2)}, u32[]{:S(2)}) collective-permute-start(bf16[1,144,512]{2,1,0:T(8,128)(2,1)S(1)} %get-tuple-element.66), channel_id=1, source_target_pairs={{0,64},{8,72},{16,80},{24,88},{32,96},{40,104},{48,112},{56,120},{... | collective-permute-start | bytes 442376 | tf_op jit(solution)/shard_map/ppermute | solution.py:278
  99.2 1.6 %collective-permute-start.24 = (bf16[128,1024]{1,0:T(8,128)(2,1)S(1)}, bf16[128,1024]{1,0:T(8,128)(2,1)S(1)}, u32[]{:S(2)}, u32[]{:S(2)}) collective-permute-start(bf16[128,1024]{1,0:T(8,128)(2,1)S(1)} %final.1.att_ref), channel_id=1, source_target_pairs={{0,1},{1,0},{2,3},{3,2},{4,5},{5,4},{6,7},{7,6},{8,9},{9,8},{10,11... | collective-permute-start | bytes 786440 | tf_op jit(solution)/shard_map/ppermute | solution.py:281
  103.8 13.5 %collective-permute-start.27 = (bf16[128,1024]{1,0:T(8,128)(2,1)S(1)}, bf16[128,1024]{1,0:T(8,128)(2,1)S(1)}, u32[]{:S(2)}, u32[]{:S(2)}) collective-permute-start(bf16[128,1024]{1,0:T(8,128)(2,1)S(1)} %project.5), channel_id=1, source_target_pairs={{0,4},{1,5},{2,6},{3,7},{4,0},{5,1},{6,2},{7,3},{8,12},{9,13},{10,... | collective-permute-start | bytes 786440 | tf_op jit(solution)/shard_map/ppermute | solution.py:281
  111.1 9.3 %collective-permute-start.26 = (bf16[128,1024]{1,0:T(8,128)(2,1)S(1)}, bf16[128,1024]{1,0:T(8,128)(2,1)S(1)}, u32[]{:S(2)}, u32[]{:S(2)}) collective-permute-start(bf16[128,1024]{1,0:T(8,128)(2,1)S(1)} %get-tuple-element.67), channel_id=1, source_target_pairs={{0,2},{1,3},{2,4},{3,5},{4,6},{5,7},{6,0},{7,1},{8,10},{9,11},{10,... | collective-permute-start | bytes 786440 | tf_op jit(solution)/shard_map/ppermute | solution.py:281
  111.8 8.6 %collective-permute-start.28 = (bf16[128,1024]{1,0:T(8,128)(2,1)S(1)}, bf16[128,1024]{1,0:T(8,128)(2,1)S(1)}, u32[]{:S(2)}, u32[]{:S(2)}) collective-permute-start(bf16[128,1024]{1,0:T(8,128)(2,1)S(1)} %get-tuple-element.68), channel_id=1, source_target_pairs={{0,6},{1,7},{2,0},{3,1},{4,2},{5,3},{6,4},{7,5},{8,14},{9,15},{10,... | collective-permute-start | bytes 786440 | tf_op jit(solution)/shard_map/ppermute | solution.py:281

commit v5 on v4

--- a/solution.py
+++ b/solution.py
@@ -286,7 +286,7 @@
     a, b = q[0:1], q[1:2]
     a, b = lax.optimization_barrier((jnp.concatenate([a, flip(a, 0, 1)]), jnp.concatenate([b, flip(b, 1, 0)])))
     a, b = lax.optimization_barrier((jnp.concatenate([a, flip(a, 0, 3)]), jnp.concatenate([b, flip(b, 3, 0)])))
-    au, bu, ad, bd = lax.optimization_barrier((zx(a, 1, 0), zx(b, 0, 1), zx(a, -1, 0), zx(b, 0, -1)))
+    au, bu, ad, bd = zx(a, 1, 0), zx(b, 0, 1), zx(a, -1, 0), zx(b, 0, -1)
     af, bf = zx(au, 1, 0), zx(bu, 0, 1)
 
     own_ids = (last + 1) * block_count - qb_count + jnp.arange(qb_count, dtype=jnp.int32)

time: 122 us -> 120 us (0.984); the launches traced: 121 us -> 118 us
  waiting for transfers between devices: 45.5 us -> 39.2 us
  starting transfers between devices: 40.4 us -> 42.1 us
  Pallas kernels: 28.3 us -> 29.9 us
    ppermute x14, waiting for transfers between devices: 25.2 us -> 19.6 us  [zx(): return lax.ppermute(v, 'seq', seq_shift(dz % 4, dx % 4))]
    pallas_call x4, Pallas kernels: 17.1 us -> 18.8 us  [attend(): pl.pallas_call(functools.partial(attend_kernel, far=far, cut=cut), out_sh...]
  transfers between devices with their start and end apart: 29 -> 29, of which waited for: 20 -> 17; matrix products, arithmetic and copies ran while one was open for 3% -> 3% of each run, Pallas kernels for 21% -> 23%
where the time goes in v5:
time: 120 us; the launch traced here: 118 us
  starting transfers between devices  42.1 us (35%)
  waiting for transfers between devices  39.2 us (33%)
  Pallas kernels  29.9 us (25%)
  local copies, waits for them, and re-layouts  3.28 us (3%)
  other arithmetic  3 us (2%)
    ppermute x14, waiting for transfers between devices, zx(): return lax.ppermute(v, 'seq', seq_shift(dz % 4, dx % 4))  19.6 us
    pallas_call x4, Pallas kernels, attend(): pl.pallas_call(functools.partial(attend_kernel, far=far, cut=cut), out_sh...  18.8 us
    ppermute x14, starting transfers between devices, zx(): return lax.ppermute(v, 'seq', seq_shift(dz % 4, dx % 4))  17.9 us
    ppermute x10, starting transfers between devices, flip(): return lax.ppermute(v, 'seq', seq_flip(fz, fx))  17.3 us
    ppermute x10, waiting for transfers between devices, flip(): return lax.ppermute(v, 'seq', seq_flip(fz, fx))  14.9 us
    pallas_call x3, Pallas kernels, project(): pl.pallas_call(functools.partial(project_kernel, fars=fars), out_shape=[j...  9.54 us
    ppermute x5, starting transfers between devices, yc(): return lax.ppermute(v, 'kvh', kvh_shift(dy % 4, dc))  6.89 us
    ppermute x5, waiting for transfers between devices, yc(): return lax.ppermute(v, 'kvh', kvh_shift(dy % 4, dc))  4.67 us
  transfers between devices with their start and end apart: 29, of which 17 were waited for; matrix products, arithmetic and copies ran while one was open for 3% of the time, Pallas kernels for 23%

profile of v5, /device:TPU:0, one launch (start us, length us, event | category | flops | bytes accessed | tf_op | source)
XLA Modules:
  0.0 117.7 jit_solution(14050034369971547784)
XLA Ops:
  0.0 1.0 slice_bitcast_fusion
  1.0 2.1 %collective-permute-start.1 = (bf16[1,64,1024]{2,1,0:T(8,128)(2,1)S(1)}, bf16[1,64,1024]{2,1,0:T(8,128)(2,1)S(1)}, u32[]{:S(2)}, u32[]{:S(2)}) collective-permute-start(bf16[1,64,1024]{2,1,0:T(8,128)(2,1)S(1)} %get-tuple-element.63), channel_id=1, source_target_pairs={{0,32},{8,40},{16,48},{24,56},{32,0},{40,8},{48,16},{56,24},{64,96... | collective-permute-start | bytes 393224 | tf_op jit(solution)/shard_map/ppermute | solution.py:278
  3.1 1.5 %collective-permute-start = (bf16[1,64,1024]{2,1,0:T(8,128)(2,1)S(1)}, bf16[1,64,1024]{2,1,0:T(8,128)(2,1)S(1)}, u32[]{:S(2)}, u32[]{:S(2)}) collective-permute-start(bf16[1,64,1024]{2,1,0:T(8,128)(2,1)S(1)} %get-tuple-element.64), channel_id=1, source_target_pairs={{0,8},{8,0},{16,24},{24,16},{32,40},{40,32},{48,56},{56,48},{64,72... | collective-permute-start | bytes 393224 | tf_op jit(solution)/shard_map/ppermute | solution.py:278
  4.6 0.8 fusion.5
  5.4 1.9 %collective-permute-done.1 = bf16[1,64,1024]{2,1,0:T(8,128)(2,1)S(1)} collective-permute-done((bf16[1,64,1024]{2,1,0:T(8,128)(2,1)S(1)}, bf16[1,64,1024]{2,1,0:T(8,128)(2,1)S(1)}, u32[]{:S(2)}, u32[]{:S(2)}) %collective-permute-start.1) | collective-permute-done | bytes 131104 | tf_op jit(solution)/shard_map/ppermute | solution.py:278
  7.3 1.4 %collective-permute-done = bf16[1,64,1024]{2,1,0:T(8,128)(2,1)S(1)} collective-permute-done((bf16[1,64,1024]{2,1,0:T(8,128)(2,1)S(1)}, bf16[1,64,1024]{2,1,0:T(8,128)(2,1)S(1)}, u32[]{:S(2)}, u32[]{:S(2)}) %collective-permute-start) | collective-permute-done | bytes 131104 | tf_op jit(solution)/shard_map/ppermute | solution.py:278
  8.7 2.8 %collective-permute-start.2 = (bf16[2,64,1024]{2,1,0:T(8,128)(2,1)S(1)}, bf16[2,64,1024]{2,1,0:T(8,128)(2,1)S(1)}, u32[]{:S(2)}, u32[]{:S(2)}) collective-permute-start(bf16[2,64,1024]{2,1,0:T(8,128)(2,1)S(1)} %pad_maximum_fusion.2), channel_id=1, source_target_pairs={{0,24},{8,16},{16,8},{24,0},{32,56},{40,48},{48,40},{56,32},{64,88... | collective-permute-start | bytes 786440 | tf_op jit(solution)/shard_map/ppermute | solution.py:278
  11.6 2.5 %collective-permute-start.3 = (bf16[2,64,1024]{2,1,0:T(8,128)(2,1)S(1)}, bf16[2,64,1024]{2,1,0:T(8,128)(2,1)S(1)}, u32[]{:S(2)}, u32[]{:S(2)}) collective-permute-start(bf16[2,64,1024]{2,1,0:T(8,128)(2,1)S(1)} %pad_maximum_fusion.3), channel_id=1, source_target_pairs={{0,96},{8,104},{16,112},{24,120},{32,64},{40,72},{48,80},{56,88},{... | collective-permute-start | bytes 786440 | tf_op jit(solution)/shard_map/ppermute | solution.py:278
  14.4 3.2 %collective-permute-done.2 = bf16[2,64,1024]{2,1,0:T(8,128)(2,1)S(1)} collective-permute-done((bf16[2,64,1024]{2,1,0:T(8,128)(2,1)S(1)}, bf16[2,64,1024]{2,1,0:T(8,128)(2,1)S(1)}, u32[]{:S(2)}, u32[]{:S(2)}) %collective-permute-start.2) | collective-permute-done | bytes 262176 | tf_op jit(solution)/shard_map/ppermute | solution.py:278
  17.7 2.4 %collective-permute-done.3 = bf16[2,64,1024]{2,1,0:T(8,128)(2,1)S(1)} collective-permute-done((bf16[2,64,1024]{2,1,0:T(8,128)(2,1)S(1)}, bf16[2,64,1024]{2,1,0:T(8,128)(2,1)S(1)}, u32[]{:S(2)}, u32[]{:S(2)}) %collective-permute-start.3) | collective-permute-done | bytes 262176 | tf_op jit(solution)/shard_map/ppermute | solution.py:278
  20.2 0.7 collective-permute-start.4
  21.1 0.6 select_reduce_fusion
  21.8 11.8 %collective-permute-done.4.refs_0_ = bf16[4,64,1024]{2,1,0:T(8,128)(2,1)S(1)} collective-permute-done((bf16[4,64,1024]{2,1,0:T(8,128)(2,1)S(1)}, bf16[4,64,1024]{2,1,0:T(8,128)(2,1)S(1)}, u32[]{:S(2)}, u32[]{:S(2)}) %collective-permute-start.4) | collective-permute-done | bytes 524320 | tf_op jit(solution)/shard_map/ppermute | solution.py:275
  33.6 0.5 collective-permute-done.5.refs_1_
  34.3 2.9 %collective-permute-start.6 = (bf16[4,64,1024]{2,1,0:T(8,128)(2,1)S(1)}, bf16[4,64,1024]{2,1,0:T(8,128)(2,1)S(1)}, u32[]{:S(2)}, u32[]{:S(2)}) collective-permute-start(bf16[4,64,1024]{2,1,0:T(8,128)(2,1)S(1)} %pad_maximum_fusion.refs_0_), channel_id=1, source_target_pairs={{0,96},{8,104},{16,112},{24,120},{32,0},{40,8},{48,16},{56,24},{64... | collective-permute-start | bytes 1572872 | tf_op jit(solution)/shard_map/ppermute | solution.py:275
  37.2 3.0 %collective-permute-start.7 = (bf16[4,64,1024]{2,1,0:T(8,128)(2,1)S(1)}, bf16[4,64,1024]{2,1,0:T(8,128)(2,1)S(1)}, u32[]{:S(2)}, u32[]{:S(2)}) collective-permute-start(bf16[4,64,1024]{2,1,0:T(8,128)(2,1)S(1)} %pad_maximum_fusion.1.refs_1_), channel_id=1, source_target_pairs={{0,24},{8,0},{16,8},{24,16},{32,56},{40,32},{48,40},{56,48},{64,88... | collective-permute-start | bytes 1572872 | tf_op jit(solution)/shard_map/ppermute | solution.py:275
  40.2 2.2 %copy-done.2 = bf16[1,8192,256]{2,1,0:T(8,128)(2,1)S(1)} copy-done((bf16[1,8192,256]{2,1,0:T(8,128)(2,1)S(1)}, bf16[1,8192,256]{2,1,0:T(8,128)(2,1)}, u32[]{:S(2)}) %copy-start.2) | copy-done | bytes 4194328
  42.4 4.1 %attend.5 = (f32[4,144,512]{2,1,0:T(8,128)S(1)}, f32[4,144,512]{2,1,0:T(8,128)S(1)}) custom-call(s32[3]{0:T(128)S(1)} %pad_add_fusion.place_ref, s32[32]{0:T(128)S(1)} %broadcast_add_fusion.count_ref, s32[512]{0:T(512)S(1)} %select_n.44.ids_ref, bf16[8192,256]{1,0:T(8,128)(2,1)S(1)} %bitcast.15, bf16[4,64,1024]{2,1,0:T(8,128)(2,1)S(1)} %collective-permute-done.4.refs_0_, ...), custom_call_target="tpu_custom_call" | custom-call | flops 4000000000 | bytes 1048576 | tf_op jit(solution)/shard_map/attend/pallas_call | solution.py:160
  46.6 4.6 %attend.7 = (bf16[2,144,512]{2,1,0:T(8,128)(2,1)S(1)}, bf16[2,144,512]{2,1,0:T(8,128)(2,1)S(1)}, bf16[2,144,512]{2,1,0:T(8,128)(2,1)S(1)}, bf16[2,144,512]{2,1,0:T(8,128)(2,1)S(1)}) custom-call(s32[3]{0:T(128)S(1)} %pad_add_fusion.place_ref, s32[32]{0:T(128)S(1)} %broadcast_add_fusion.count_ref, s32[512]{0:T(512)S(1)} %select_n.44.ids_ref, ...), custom_call_target="tpu_custom_call" | custom-call | flops 4000000000 | bytes 1048576 | tf_op jit(solution)/shard_map/attend/pallas_call | solution.py:160
  51.2 2.5 %collective-permute-start.10 = (bf16[2,144,512]{2,1,0:T(8,128)(2,1)S(1)}, bf16[2,144,512]{2,1,0:T(8,128)(2,1)S(1)}, u32[]{:S(2)}, u32[]{:S(2)}) collective-permute-start(bf16[2,144,512]{2,1,0:T(8,128)(2,1)S(1)} %get-tuple-element.40), channel_id=1, source_target_pairs={{0,96},{8,104},{16,112},{24,120},{32,0},{40,8},{48,16},{56,24},{64... | collective-permute-start | bytes 884744 | tf_op jit(solution)/shard_map/ppermute | solution.py:275
  54.1 1.6 %collective-permute-start.13 = (bf16[2,144,512]{2,1,0:T(8,128)(2,1)S(1)}, bf16[2,144,512]{2,1,0:T(8,128)(2,1)S(1)}, u32[]{:S(2)}, u32[]{:S(2)}) collective-permute-start(bf16[2,144,512]{2,1,0:T(8,128)(2,1)S(1)} %get-tuple-element.45), channel_id=1, source_target_pairs={{0,8},{8,16},{16,24},{24,0},{32,40},{40,48},{48,56},{56,32},{64,72... | collective-permute-start | bytes 884744 | tf_op jit(solution)/shard_map/ppermute | solution.py:275
  55.7 5.3 %attend.6 = (f32[4,144,512]{2,1,0:T(8,128)S(1)}, f32[4,144,512]{2,1,0:T(8,128)S(1)}) custom-call(s32[3]{0:T(128)S(1)} %pad_add_fusion.place_ref, s32[32]{0:T(128)S(1)} %broadcast_add_fusion.count_ref, s32[512]{0:T(512)S(1)} %select_n.44.ids_ref, bf16[8192,256]{1,0:T(8,128)(2,1)S(1)} %bitcast.17, bf16[4,64,1024]{2,1,0:T(8,128)(2,1)S(1)} %collective-permute-done.6.refs_0_, ...), custom_call_target="tpu_custom_call" | custom-call | flops 4000000000 | bytes 1048576 | tf_op jit(solution)/shard_map/attend/pallas_call | solution.py:160
  61.0 0.7 collective-permute-done.11.refs_3_
  62.1 0.6 join.1
  62.7 1.1 collective-permute-start.14
  63.8 2.2 %collective-permute-start.15 = (bf16[4,144,512]{2,1,0:T(8,128)(2,1)S(1)}, bf16[4,144,512]{2,1,0:T(8,128)(2,1)S(1)}, u32[]{:S(2)}, u32[]{:S(2)}) collective-permute-start(bf16[4,144,512]{2,1,0:T(8,128)(2,1)S(1)} %get-tuple-element.47), channel_id=1, source_target_pairs={{0,96},{8,104},{16,112},{24,120},{32,0},{40,8},{48,16},{56,24},{64... | collective-permute-start | bytes 1769480 | tf_op jit(solution)/shard_map/ppermute | solution.py:275
  66.0 1.2 collective-permute-start.16
  67.1 2.1 %collective-permute-start.17 = (bf16[4,144,512]{2,1,0:T(8,128)(2,1)S(1)}, bf16[4,144,512]{2,1,0:T(8,128)(2,1)S(1)}, u32[]{:S(2)}, u32[]{:S(2)}) collective-permute-start(bf16[4,144,512]{2,1,0:T(8,128)(2,1)S(1)} %get-tuple-element.50), channel_id=1, source_target_pairs={{0,24},{8,0},{16,8},{24,16},{32,56},{40,32},{48,40},{56,48},{64,88... | collective-permute-start | bytes 1769480 | tf_op jit(solution)/shard_map/ppermute | solution.py:275
  69.2 4.7 %attend.4 = (f32[4,144,512]{2,1,0:T(8,128)S(1)}, f32[4,144,512]{2,1,0:T(8,128)S(1)}) custom-call(s32[3]{0:T(128)S(1)} %pad_add_fusion.place_ref, s32[32]{0:T(128)S(1)} %broadcast_add_fusion.count_ref, s32[512]{0:T(512)S(1)} %select_n.44.ids_ref, bf16[8192,256]{1,0:T(8,128)(2,1)S(1)} %bitcast.18, bf16[4,64,1024]{2,1,0:T(8,128)(2,1)S(1)} %pad_maximum_fusion.refs_0_, ...), custom_call_target="tpu_custom_call" | custom-call | flops 4000000000 | bytes 1048576 | tf_op jit(solution)/shard_map/attend/pallas_call | solution.py:160
  74.2 6.0 %collective-permute-done.16.refs_4_ = bf16[4,144,512]{2,1,0:T(8,128)(2,1)S(1)} collective-permute-done((bf16[4,144,512]{2,1,0:T(8,128)(2,1)S(1)}, bf16[4,144,512]{2,1,0:T(8,128)(2,1)S(1)}, u32[]{:S(2)}, u32[]{:S(2)}) %collective-permute-start.16) | collective-permute-done | bytes 589856 | tf_op jit(solution)/shard_map/ppermute | solution.py:275
  80.2 0.7 stage.1
  81.0 3.3 %collective-permute-start.19 = (bf16[1,144,512]{2,1,0:T(8,128)(2,1)S(1)}, bf16[1,144,512]{2,1,0:T(8,128)(2,1)S(1)}, u32[]{:S(2)}, u32[]{:S(2)}) collective-permute-start(bf16[1,144,512]{2,1,0:T(8,128)(2,1)S(1)} %get-tuple-element.53), channel_id=1, source_target_pairs={{0,24},{8,16},{16,8},{24,0},{32,56},{40,48},{48,40},{56,32},{64,88... | collective-permute-start | bytes 442376 | tf_op jit(solution)/shard_map/ppermute | solution.py:278
  84.4 1.4 %collective-permute-start.20 = (bf16[1,144,512]{2,1,0:T(8,128)(2,1)S(1)}, bf16[1,144,512]{2,1,0:T(8,128)(2,1)S(1)}, u32[]{:S(2)}, u32[]{:S(2)}) collective-permute-start(bf16[1,144,512]{2,1,0:T(8,128)(2,1)S(1)} %get-tuple-element.54), channel_id=1, source_target_pairs={{0,16},{8,24},{16,0},{24,8},{32,48},{40,56},{48,32},{56,40},{64,80... | collective-permute-start | bytes 442376 | tf_op jit(solution)/shard_map/ppermute | solution.py:278
  86.2 1.9 %collective-permute-start.22 = (bf16[1,144,512]{2,1,0:T(8,128)(2,1)S(1)}, bf16[1,144,512]{2,1,0:T(8,128)(2,1)S(1)}, u32[]{:S(2)}, u32[]{:S(2)}) collective-permute-start(bf16[1,144,512]{2,1,0:T(8,128)(2,1)S(1)} %get-tuple-element.57), channel_id=1, source_target_pairs={{0,96},{8,104},{16,112},{24,120},{32,64},{40,72},{48,80},{56,88},{... | collective-permute-start | bytes 442376 | tf_op jit(solution)/shard_map/ppermute | solution.py:278
  88.1 0.6 collective-permute-done.19.refs_2_
  88.6 1.7 %collective-permute-start.23 = (bf16[1,144,512]{2,1,0:T(8,128)(2,1)S(1)}, bf16[1,144,512]{2,1,0:T(8,128)(2,1)S(1)}, u32[]{:S(2)}, u32[]{:S(2)}) collective-permute-start(bf16[1,144,512]{2,1,0:T(8,128)(2,1)S(1)} %get-tuple-element.58), channel_id=1, source_target_pairs={{0,64},{8,72},{16,80},{24,88},{32,96},{40,104},{48,112},{56,120},{... | collective-permute-start | bytes 442376 | tf_op jit(solution)/shard_map/ppermute | solution.py:278
  90.3 0.7 collective-permute-done.20.refs_3_
  91.0 1.5 %collective-permute-done.22.refs_6_ = bf16[1,144,512]{2,1,0:T(8,128)(2,1)S(1)} collective-permute-done((bf16[1,144,512]{2,1,0:T(8,128)(2,1)S(1)}, bf16[1,144,512]{2,1,0:T(8,128)(2,1)S(1)}, u32[]{:S(2)}, u32[]{:S(2)}) %collective-permute-start.22) | collective-permute-done | bytes 147488 | tf_op jit(solution)/shard_map/ppermute | solution.py:278
  92.5 2.8 %collective-permute-done.23.refs_7_ = bf16[1,144,512]{2,1,0:T(8,128)(2,1)S(1)} collective-permute-done((bf16[1,144,512]{2,1,0:T(8,128)(2,1)S(1)}, bf16[1,144,512]{2,1,0:T(8,128)(2,1)S(1)}, u32[]{:S(2)}, u32[]{:S(2)}) %collective-permute-start.23) | collective-permute-done | bytes 147488 | tf_op jit(solution)/shard_map/ppermute | solution.py:278
  95.7 1.5 %collective-permute-done.24.other_ref = bf16[128,1024]{1,0:T(8,128)(2,1)S(1)} collective-permute-done((bf16[128,1024]{1,0:T(8,128)(2,1)S(1)}, bf16[128,1024]{1,0:T(8,128)(2,1)S(1)}, u32[]{:S(2)}, u32[]{:S(2)}) %collective-permute-start.24) | collective-permute-done | bytes 262176 | tf_op jit(solution)/shard_map/ppermute | solution.py:281
  97.2 2.9 %project.5 = bf16[128,1024]{1,0:T(8,128)(2,1)S(1)} custom-call(s32[3]{0:T(128)S(1)} %pad_add_fusion.place_ref, bf16[128,1024]{1,0:T(8,128)(2,1)S(1)} %final.1.att_ref, bf16[128,1024]{1,0:T(8,128)(2,1)S(1)} %collective-permute-done.24.other_ref, bf16[1024,8192]{1,0:T(8,128)(2,1)S(1)} %bitcast.12, bf16[1024,8192]{1,0:T(8,128)(2,1)} %collective-permute-done.25.wo_ref), custom_call_target="tpu_custom_call" | custom-call | flops 3000000000 | bytes 1048576 | tf_op jit(solution)/shard_map/project/pallas_call | solution.py:249
  100.1 3.5 %collective-permute-start.27 = (bf16[128,1024]{1,0:T(8,128)(2,1)S(1)}, bf16[128,1024]{1,0:T(8,128)(2,1)S(1)}, u32[]{:S(2)}, u32[]{:S(2)}) collective-permute-start(bf16[128,1024]{1,0:T(8,128)(2,1)S(1)} %project.5), channel_id=1, source_target_pairs={{0,4},{1,5},{2,6},{3,7},{4,0},{5,1},{6,2},{7,3},{8,12},{9,13},{10,... | collective-permute-start | bytes 786440 | tf_op jit(solution)/shard_map/ppermute | solution.py:281
  103.6 3.8 %project.4 = (bf16[128,1024]{1,0:T(8,128)(2,1)S(1)}, bf16[128,1024]{1,0:T(8,128)(2,1)S(1)}) custom-call(s32[3]{0:T(128)S(1)} %pad_add_fusion.place_ref, bf16[128,1024]{1,0:T(8,128)(2,1)S(1)} %final.1.att_ref, bf16[128,1024]{1,0:T(8,128)(2,1)S(1)} %collective-permute-done.24.other_ref, bf16[1024,8192]{1,0:T(8,128)(2,1)S(1)} %bitcast.13, ...), custom_call_target="tpu_custom_call" | custom-call | flops 6000000000 | bytes 1048576 | tf_op jit(solution)/shard_map/project/pallas_call | solution.py:249
  107.4 0.8 collective-permute-start.26
  108.2 2.6 %collective-permute-start.28 = (bf16[128,1024]{1,0:T(8,128)(2,1)S(1)}, bf16[128,1024]{1,0:T(8,128)(2,1)S(1)}, u32[]{:S(2)}, u32[]{:S(2)}) collective-permute-start(bf16[128,1024]{1,0:T(8,128)(2,1)S(1)} %get-tuple-element.60), channel_id=1, source_target_pairs={{0,6},{1,7},{2,0},{3,1},{4,2},{5,3},{6,4},{7,5},{8,14},{9,15},{10,... | collective-permute-start | bytes 786440 | tf_op jit(solution)/shard_map/ppermute | solution.py:281
  110.7 2.9 %project.3 = f32[128,1024]{1,0:T(8,128)S(1)} custom-call(s32[3]{0:T(128)S(1)} %pad_add_fusion.place_ref, bf16[128,1024]{1,0:T(8,128)(2,1)S(1)} %final.1.att_ref, bf16[128,1024]{1,0:T(8,128)(2,1)S(1)} %collective-permute-done.24.other_ref, bf16[1024,8192]{1,0:T(8,128)(2,1)S(1)} %bitcast.14, bf16[1024,8192]{1,0:T(8,128)(2,1)} %collective-permute-done.25.wo_ref), custom_call_target="tpu_custom_call" | custom-call | flops 3000000000 | bytes 1048576 | tf_op jit(solution)/shard_map/project/pallas_call | solution.py:249
  113.6 3.1 %collective-permute-done.26 = bf16[128,1024]{1,0:T(8,128)(2,1)S(1)} collective-permute-done((bf16[128,1024]{1,0:T(8,128)(2,1)S(1)}, bf16[128,1024]{1,0:T(8,128)(2,1)S(1)}, u32[]{:S(2)}, u32[]{:S(2)}) %collective-permute-start.26) | collective-permute-done | bytes 262176 | tf_op jit(solution)/shard_map/ppermute | solution.py:281
  116.8 0.9 convert_add_fusion
  (55 shorter events, 3.0 us)
Async XLA Ops:
  0.0 97.2 %collective-permute-start.25 = (bf16[1024,8192]{1,0:T(8,128)(2,1)}, bf16[1024,8192]{1,0:T(8,128)(2,1)}, u32[]{:S(2)}, u32[]{:S(2)}) collective-permute-start(bf16[1024,8192]{1,0:T(8,128)(2,1)} %bitcast.9), channel_id=1, source_target_pairs={{0,1},{1,0},{2,3},{3,2},{4,5},{5,4},{6,7},{7,6},{8,9},{9,8},{10,11... | collective-permute-start | bytes 50331656 | tf_op jit(solution)/shard_map/ppermute | solution.py:281
  1.0 6.2 %collective-permute-start.1 = (bf16[1,64,1024]{2,1,0:T(8,128)(2,1)S(1)}, bf16[1,64,1024]{2,1,0:T(8,128)(2,1)S(1)}, u32[]{:S(2)}, u32[]{:S(2)}) collective-permute-start(bf16[1,64,1024]{2,1,0:T(8,128)(2,1)S(1)} %get-tuple-element.63), channel_id=1, source_target_pairs={{0,32},{8,40},{16,48},{24,56},{32,0},{40,8},{48,16},{56,24},{64,96... | collective-permute-start | bytes 393224 | tf_op jit(solution)/shard_map/ppermute | solution.py:278
  3.1 5.6 %collective-permute-start = (bf16[1,64,1024]{2,1,0:T(8,128)(2,1)S(1)}, bf16[1,64,1024]{2,1,0:T(8,128)(2,1)S(1)}, u32[]{:S(2)}, u32[]{:S(2)}) collective-permute-start(bf16[1,64,1024]{2,1,0:T(8,128)(2,1)S(1)} %get-tuple-element.64), channel_id=1, source_target_pairs={{0,8},{8,0},{16,24},{24,16},{32,40},{40,32},{48,56},{56,48},{64,72... | collective-permute-start | bytes 393224 | tf_op jit(solution)/shard_map/ppermute | solution.py:278
  8.7 12.4 %copy-start.3 = (s32[32,64]{1,0:T(8,128)S(1)}, s32[32,64]{1,0:T(8,128)}, u32[]{:S(2)}) copy-start(s32[32,64]{1,0:T(8,128)} %param.6) | copy-start | bytes 24580
  8.7 8.9 %collective-permute-start.2 = (bf16[2,64,1024]{2,1,0:T(8,128)(2,1)S(1)}, bf16[2,64,1024]{2,1,0:T(8,128)(2,1)S(1)}, u32[]{:S(2)}, u32[]{:S(2)}) collective-permute-start(bf16[2,64,1024]{2,1,0:T(8,128)(2,1)S(1)} %pad_maximum_fusion.2), channel_id=1, source_target_pairs={{0,24},{8,16},{16,8},{24,0},{32,56},{40,48},{48,40},{56,32},{64,88... | collective-permute-start | bytes 786440 | tf_op jit(solution)/shard_map/ppermute | solution.py:278
  11.6 8.5 %collective-permute-start.3 = (bf16[2,64,1024]{2,1,0:T(8,128)(2,1)S(1)}, bf16[2,64,1024]{2,1,0:T(8,128)(2,1)S(1)}, u32[]{:S(2)}, u32[]{:S(2)}) collective-permute-start(bf16[2,64,1024]{2,1,0:T(8,128)(2,1)S(1)} %pad_maximum_fusion.3), channel_id=1, source_target_pairs={{0,96},{8,104},{16,112},{24,120},{32,64},{40,72},{48,80},{56,88},{... | collective-permute-start | bytes 786440 | tf_op jit(solution)/shard_map/ppermute | solution.py:278
  20.2 26.4 %copy-start = (bf16[4,64,1024]{2,1,0:T(8,128)(2,1)}, bf16[4,64,1024]{2,1,0:T(8,128)(2,1)S(1)}, u32[]{:S(2)}) copy-start(bf16[4,64,1024]{2,1,0:T(8,128)(2,1)S(1)} %pad_maximum_fusion.1.refs_1_) | copy-start | bytes 1572868
  20.2 13.4 %collective-permute-start.4 = (bf16[4,64,1024]{2,1,0:T(8,128)(2,1)S(1)}, bf16[4,64,1024]{2,1,0:T(8,128)(2,1)S(1)}, u32[]{:S(2)}, u32[]{:S(2)}) collective-permute-start(bf16[4,64,1024]{2,1,0:T(8,128)(2,1)S(1)} %pad_maximum_fusion.refs_0_), channel_id=1, source_target_pairs={{0,32},{8,40},{16,48},{24,56},{32,64},{40,72},{48,80},{56,88},{64,... | collective-permute-start | bytes 1572872 | tf_op jit(solution)/shard_map/ppermute | solution.py:275
  20.9 13.2 %collective-permute-start.5 = (bf16[4,64,1024]{2,1,0:T(8,128)(2,1)S(1)}, bf16[4,64,1024]{2,1,0:T(8,128)(2,1)S(1)}, u32[]{:S(2)}, u32[]{:S(2)}) collective-permute-start(bf16[4,64,1024]{2,1,0:T(8,128)(2,1)S(1)} %pad_maximum_fusion.1.refs_1_), channel_id=1, source_target_pairs={{0,8},{8,16},{16,24},{24,0},{32,40},{40,48},{48,56},{56,32},{64,72... | collective-permute-start | bytes 1572872 | tf_op jit(solution)/shard_map/ppermute | solution.py:275
  33.6 13.0 %collective-permute-start.8 = (bf16[4,64,1024]{2,1,0:T(8,128)(2,1)S(1)}, bf16[4,64,1024]{2,1,0:T(8,128)(2,1)S(1)}, u32[]{:S(2)}, u32[]{:S(2)}) collective-permute-start(bf16[4,64,1024]{2,1,0:T(8,128)(2,1)S(1)} %collective-permute-done.4.refs_0_), channel_id=1, source_target_pairs={{0,32},{8,40},{16,48},{24,56},{32,64},{40,72},{48,80},{56,88},{64,... | collective-permute-start | bytes 1572872 | tf_op jit(solution)/shard_map/ppermute | solution.py:275
  34.1 12.5 %collective-permute-start.9 = (bf16[4,64,1024]{2,1,0:T(8,128)(2,1)S(1)}, bf16[4,64,1024]{2,1,0:T(8,128)(2,1)}, u32[]{:S(2)}, u32[]{:S(2)}) collective-permute-start(bf16[4,64,1024]{2,1,0:T(8,128)(2,1)S(1)} %collective-permute-done.5.refs_1_), channel_id=1, source_target_pairs={{0,8},{8,16},{16,24},{24,0},{32,40},{40,48},{48,56},{56,32},{64,72... | collective-permute-start | bytes 1572872 | tf_op jit(solution)/shard_map/ppermute | solution.py:275
  34.3 19.4 %collective-permute-start.6 = (bf16[4,64,1024]{2,1,0:T(8,128)(2,1)S(1)}, bf16[4,64,1024]{2,1,0:T(8,128)(2,1)S(1)}, u32[]{:S(2)}, u32[]{:S(2)}) collective-permute-start(bf16[4,64,1024]{2,1,0:T(8,128)(2,1)S(1)} %pad_maximum_fusion.refs_0_), channel_id=1, source_target_pairs={{0,96},{8,104},{16,112},{24,120},{32,0},{40,8},{48,16},{56,24},{64... | collective-permute-start | bytes 1572872 | tf_op jit(solution)/shard_map/ppermute | solution.py:275
  37.2 16.9 %collective-permute-start.7 = (bf16[4,64,1024]{2,1,0:T(8,128)(2,1)S(1)}, bf16[4,64,1024]{2,1,0:T(8,128)(2,1)S(1)}, u32[]{:S(2)}, u32[]{:S(2)}) collective-permute-start(bf16[4,64,1024]{2,1,0:T(8,128)(2,1)S(1)} %pad_maximum_fusion.1.refs_1_), channel_id=1, source_target_pairs={{0,24},{8,0},{16,8},{24,16},{32,56},{40,32},{48,40},{56,48},{64,88... | collective-permute-start | bytes 1572872 | tf_op jit(solution)/shard_map/ppermute | solution.py:275
  40.2 2.2 %copy-start.2 = (bf16[1,8192,256]{2,1,0:T(8,128)(2,1)S(1)}, bf16[1,8192,256]{2,1,0:T(8,128)(2,1)}, u32[]{:S(2)}) copy-start(bf16[1,8192,256]{2,1,0:T(8,128)(2,1)} %param.5) | copy-start | bytes 12582916
  51.2 9.8 %collective-permute-start.10 = (bf16[2,144,512]{2,1,0:T(8,128)(2,1)S(1)}, bf16[2,144,512]{2,1,0:T(8,128)(2,1)S(1)}, u32[]{:S(2)}, u32[]{:S(2)}) collective-permute-start(bf16[2,144,512]{2,1,0:T(8,128)(2,1)S(1)} %get-tuple-element.40), channel_id=1, source_target_pairs={{0,96},{8,104},{16,112},{24,120},{32,0},{40,8},{48,16},{56,24},{64... | collective-permute-start | bytes 884744 | tf_op jit(solution)/shard_map/ppermute | solution.py:275
  53.6 8.1 %collective-permute-start.11 = (bf16[2,144,512]{2,1,0:T(8,128)(2,1)S(1)}, bf16[2,144,512]{2,1,0:T(8,128)(2,1)S(1)}, u32[]{:S(2)}, u32[]{:S(2)}) collective-permute-start(bf16[2,144,512]{2,1,0:T(8,128)(2,1)S(1)} %get-tuple-element.41), channel_id=1, source_target_pairs={{0,32},{8,40},{16,48},{24,56},{32,64},{40,72},{48,80},{56,88},{64,... | collective-permute-start | bytes 884744 | tf_op jit(solution)/shard_map/ppermute | solution.py:275
  53.6 8.1 %collective-permute-start.12 = (bf16[2,144,512]{2,1,0:T(8,128)(2,1)S(1)}, bf16[2,144,512]{2,1,0:T(8,128)(2,1)S(1)}, u32[]{:S(2)}, u32[]{:S(2)}) collective-permute-start(bf16[2,144,512]{2,1,0:T(8,128)(2,1)S(1)} %get-tuple-element.44), channel_id=1, source_target_pairs={{0,24},{8,0},{16,8},{24,16},{32,56},{40,32},{48,40},{56,48},{64,88... | collective-permute-start | bytes 884744 | tf_op jit(solution)/shard_map/ppermute | solution.py:275
  54.1 7.9 %collective-permute-start.13 = (bf16[2,144,512]{2,1,0:T(8,128)(2,1)S(1)}, bf16[2,144,512]{2,1,0:T(8,128)(2,1)S(1)}, u32[]{:S(2)}, u32[]{:S(2)}) collective-permute-start(bf16[2,144,512]{2,1,0:T(8,128)(2,1)S(1)} %get-tuple-element.45), channel_id=1, source_target_pairs={{0,8},{8,16},{16,24},{24,0},{32,40},{40,48},{48,56},{56,32},{64,72... | collective-permute-start | bytes 884744 | tf_op jit(solution)/shard_map/ppermute | solution.py:275
  55.7 41.5 %slice-start = ((s8[16777216]{0:T(1024)(128)(4,1)}), s8[4194304]{0:T(1024)(128)(4,1)S(1)}, s32[]{:S(2)}) async-start(s8[16777216]{0:T(1024)(128)(4,1)} %bitcast.10), calls=%async_computation | async-start | bytes 8388608
  55.7 41.5 %slice-start.1 = ((s8[16777216]{0:T(1024)(128)(4,1)}), s8[4194304]{0:T(1024)(128)(4,1)S(1)}, s32[]{:S(2)}) async-start(s8[16777216]{0:T(1024)(128)(4,1)} %bitcast.10), calls=%async_computation.1 | async-start | bytes 8388608
  62.1 7.2 %copy-start.1 = (bf16[4,64,1024]{2,1,0:T(8,128)(2,1)S(1)}, bf16[4,64,1024]{2,1,0:T(8,128)(2,1)}, u32[]{:S(2)}) copy-start(bf16[4,64,1024]{2,1,0:T(8,128)(2,1)} %copy-done) | copy-start | bytes 1572868
  62.7 11.5 %collective-permute-start.14 = (bf16[4,144,512]{2,1,0:T(8,128)(2,1)S(1)}, bf16[4,144,512]{2,1,0:T(8,128)(2,1)S(1)}, u32[]{:S(2)}, u32[]{:S(2)}) collective-permute-start(bf16[4,144,512]{2,1,0:T(8,128)(2,1)S(1)} %get-tuple-element.46), channel_id=1, source_target_pairs={{0,32},{8,40},{16,48},{24,56},{32,64},{40,72},{48,80},{56,88},{64,... | collective-permute-start | bytes 1769480 | tf_op jit(solution)/shard_map/ppermute | solution.py:275
  63.8 10.4 %collective-permute-start.15 = (bf16[4,144,512]{2,1,0:T(8,128)(2,1)S(1)}, bf16[4,144,512]{2,1,0:T(8,128)(2,1)S(1)}, u32[]{:S(2)}, u32[]{:S(2)}) collective-permute-start(bf16[4,144,512]{2,1,0:T(8,128)(2,1)S(1)} %get-tuple-element.47), channel_id=1, source_target_pairs={{0,96},{8,104},{16,112},{24,120},{32,0},{40,8},{48,16},{56,24},{64... | collective-permute-start | bytes 1769480 | tf_op jit(solution)/shard_map/ppermute | solution.py:275
  66.0 14.3 %collective-permute-start.16 = (bf16[4,144,512]{2,1,0:T(8,128)(2,1)S(1)}, bf16[4,144,512]{2,1,0:T(8,128)(2,1)S(1)}, u32[]{:S(2)}, u32[]{:S(2)}) collective-permute-start(bf16[4,144,512]{2,1,0:T(8,128)(2,1)S(1)} %get-tuple-element.49), channel_id=1, source_target_pairs={{0,8},{8,16},{16,24},{24,0},{32,40},{40,48},{48,56},{56,32},{64,72... | collective-permute-start | bytes 1769480 | tf_op jit(solution)/shard_map/ppermute | solution.py:275
  67.1 30.1 %slice-start.2 = ((s8[16777216]{0:T(1024)(128)(4,1)}), s8[4194304]{0:T(1024)(128)(4,1)S(1)}, s32[]{:S(2)}) async-start(s8[16777216]{0:T(1024)(128)(4,1)} %bitcast.10), calls=%async_computation.2 | async-start | bytes 8388608
  67.1 30.1 %slice-start.3 = ((s8[16777216]{0:T(1024)(128)(4,1)}), s8[4194304]{0:T(1024)(128)(4,1)S(1)}, s32[]{:S(2)}) async-start(s8[16777216]{0:T(1024)(128)(4,1)} %bitcast.10), calls=%async_computation.3 | async-start | bytes 8388608
  67.1 13.1 %collective-permute-start.17 = (bf16[4,144,512]{2,1,0:T(8,128)(2,1)S(1)}, bf16[4,144,512]{2,1,0:T(8,128)(2,1)S(1)}, u32[]{:S(2)}, u32[]{:S(2)}) collective-permute-start(bf16[4,144,512]{2,1,0:T(8,128)(2,1)S(1)} %get-tuple-element.50), channel_id=1, source_target_pairs={{0,24},{8,0},{16,8},{24,16},{32,56},{40,32},{48,40},{56,48},{64,88... | collective-permute-start | bytes 1769480 | tf_op jit(solution)/shard_map/ppermute | solution.py:275
  80.9 5.2 %collective-permute-start.18 = (bf16[1,144,512]{2,1,0:T(8,128)(2,1)S(1)}, bf16[1,144,512]{2,1,0:T(8,128)(2,1)S(1)}, u32[]{:S(2)}, u32[]{:S(2)}) collective-permute-start(bf16[1,144,512]{2,1,0:T(8,128)(2,1)S(1)} %get-tuple-element.52), channel_id=1, source_target_pairs={{0,8},{8,0},{16,24},{24,16},{32,40},{40,32},{48,56},{56,48},{64,72... | collective-permute-start | bytes 442376 | tf_op jit(solution)/shard_map/ppermute | solution.py:278
  81.0 7.6 %collective-permute-start.19 = (bf16[1,144,512]{2,1,0:T(8,128)(2,1)S(1)}, bf16[1,144,512]{2,1,0:T(8,128)(2,1)S(1)}, u32[]{:S(2)}, u32[]{:S(2)}) collective-permute-start(bf16[1,144,512]{2,1,0:T(8,128)(2,1)S(1)} %get-tuple-element.53), channel_id=1, source_target_pairs={{0,24},{8,16},{16,8},{24,0},{32,56},{40,48},{48,40},{56,32},{64,88... | collective-permute-start | bytes 442376 | tf_op jit(solution)/shard_map/ppermute | solution.py:278
  84.4 6.6 %collective-permute-start.20 = (bf16[1,144,512]{2,1,0:T(8,128)(2,1)S(1)}, bf16[1,144,512]{2,1,0:T(8,128)(2,1)S(1)}, u32[]{:S(2)}, u32[]{:S(2)}) collective-permute-start(bf16[1,144,512]{2,1,0:T(8,128)(2,1)S(1)} %get-tuple-element.54), channel_id=1, source_target_pairs={{0,16},{8,24},{16,0},{24,8},{32,48},{40,56},{48,32},{56,40},{64,80... | collective-permute-start | bytes 442376 | tf_op jit(solution)/shard_map/ppermute | solution.py:278
  85.7 5.3 %collective-permute-start.21 = (bf16[1,144,512]{2,1,0:T(8,128)(2,1)S(1)}, bf16[1,144,512]{2,1,0:T(8,128)(2,1)S(1)}, u32[]{:S(2)}, u32[]{:S(2)}) collective-permute-start(bf16[1,144,512]{2,1,0:T(8,128)(2,1)S(1)} %get-tuple-element.56), channel_id=1, source_target_pairs={{0,32},{8,40},{16,48},{24,56},{32,0},{40,8},{48,16},{56,24},{64,96... | collective-permute-start | bytes 442376 | tf_op jit(solution)/shard_map/ppermute | solution.py:278
  86.2 6.4 %collective-permute-start.22 = (bf16[1,144,512]{2,1,0:T(8,128)(2,1)S(1)}, bf16[1,144,512]{2,1,0:T(8,128)(2,1)S(1)}, u32[]{:S(2)}, u32[]{:S(2)}) collective-permute-start(bf16[1,144,512]{2,1,0:T(8,128)(2,1)S(1)} %get-tuple-element.57), channel_id=1, source_target_pairs={{0,96},{8,104},{16,112},{24,120},{32,64},{40,72},{48,80},{56,88},{... | collective-permute-start | bytes 442376 | tf_op jit(solution)/shard_map/ppermute | solution.py:278
  88.6 6.6 %collective-permute-start.23 = (bf16[1,144,512]{2,1,0:T(8,128)(2,1)S(1)}, bf16[1,144,512]{2,1,0:T(8,128)(2,1)S(1)}, u32[]{:S(2)}, u32[]{:S(2)}) collective-permute-start(bf16[1,144,512]{2,1,0:T(8,128)(2,1)S(1)} %get-tuple-element.58), channel_id=1, source_target_pairs={{0,64},{8,72},{16,80},{24,88},{32,96},{40,104},{48,112},{56,120},{... | collective-permute-start | bytes 442376 | tf_op jit(solution)/shard_map/ppermute | solution.py:278
  95.6 1.6 %collective-permute-start.24 = (bf16[128,1024]{1,0:T(8,128)(2,1)S(1)}, bf16[128,1024]{1,0:T(8,128)(2,1)S(1)}, u32[]{:S(2)}, u32[]{:S(2)}) collective-permute-start(bf16[128,1024]{1,0:T(8,128)(2,1)S(1)} %final.1.att_ref), channel_id=1, source_target_pairs={{0,1},{1,0},{2,3},{3,2},{4,5},{5,4},{6,7},{7,6},{8,9},{9,8},{10,11... | collective-permute-start | bytes 786440 | tf_op jit(solution)/shard_map/ppermute | solution.py:281
  100.1 13.5 %collective-permute-start.27 = (bf16[128,1024]{1,0:T(8,128)(2,1)S(1)}, bf16[128,1024]{1,0:T(8,128)(2,1)S(1)}, u32[]{:S(2)}, u32[]{:S(2)}) collective-permute-start(bf16[128,1024]{1,0:T(8,128)(2,1)S(1)} %project.5), channel_id=1, source_target_pairs={{0,4},{1,5},{2,6},{3,7},{4,0},{5,1},{6,2},{7,3},{8,12},{9,13},{10,... | collective-permute-start | bytes 786440 | tf_op jit(solution)/shard_map/ppermute | solution.py:281
  107.4 9.3 %collective-permute-start.26 = (bf16[128,1024]{1,0:T(8,128)(2,1)S(1)}, bf16[128,1024]{1,0:T(8,128)(2,1)S(1)}, u32[]{:S(2)}, u32[]{:S(2)}) collective-permute-start(bf16[128,1024]{1,0:T(8,128)(2,1)S(1)} %get-tuple-element.59), channel_id=1, source_target_pairs={{0,2},{1,3},{2,4},{3,5},{4,6},{5,7},{6,0},{7,1},{8,10},{9,11},{10,... | collective-permute-start | bytes 786440 | tf_op jit(solution)/shard_map/ppermute | solution.py:281
  108.2 8.6 %collective-permute-start.28 = (bf16[128,1024]{1,0:T(8,128)(2,1)S(1)}, bf16[128,1024]{1,0:T(8,128)(2,1)S(1)}, u32[]{:S(2)}, u32[]{:S(2)}) collective-permute-start(bf16[128,1024]{1,0:T(8,128)(2,1)S(1)} %get-tuple-element.60), channel_id=1, source_target_pairs={{0,6},{1,7},{2,0},{3,1},{4,2},{5,3},{6,4},{7,5},{8,14},{9,15},{10,... | collective-permute-start | bytes 786440 | tf_op jit(solution)/shard_map/ppermute | solution.py:281

commit v6 on v5

--- a/solution.py
+++ b/solution.py
@@ -230,17 +230,36 @@
     )(*args)
 
 
+PIECES = 2
+
+
 def project_kernel(place_ref, att_ref, other_ref, w_ref, wo_ref, *refs, fars):
     out_refs, (wo_scr, sems) = refs[: len(fars)], refs[len(fars) :]
     k = place_ref[1]
     cols = [pl.ds(pl.multiple_of((2 * ((k // 2 + far) % 4) + k % 2) * WIDE, WIDE), WIDE) for far in fars]
-    copies = [pltpu.make_async_copy(wo_ref.at[:, c], wo_scr.at[n], sems.at[n]) for n, c in enumerate(cols)]
-    for copy in copies:
+    rows = wo_ref.shape[0] // PIECES
+    copies = [
+        [
+            pltpu.make_async_copy(
+                wo_ref.at[r * rows : (r + 1) * rows, c],
+                wo_scr.at[n, r * rows : (r + 1) * rows],
+                sems.at[n, r],
+            )
+            for r in range(PIECES)
+        ]
+        for n, c in enumerate(cols)
+    ]
+    for copy in sum(copies, []):
         copy.start()
     for c, copy, wo, out_ref in zip(cols, copies, range(len(fars)), out_refs):
         value = jnp.dot(att_ref[...], w_ref[:, c], preferred_element_type=F32)
-        copy.wait()
-        value = value + jnp.dot(other_ref[...], wo_scr[wo], preferred_element_type=F32)
+        for r in range(PIECES):
+            copy[r].wait()
+            value = value + jnp.dot(
+                other_ref[:, r * rows : (r + 1) * rows],
+                wo_scr[wo, r * rows : (r + 1) * rows],
+                preferred_element_type=F32,
+            )
         out_ref[...] = value.astype(out_ref.dtype)
 
 
@@ -253,7 +272,7 @@
         out_specs=[VM] * len(fars),
         scratch_shapes=[
             pltpu.VMEM((len(fars), depth, WIDE), BF),
-            pltpu.SemaphoreType.DMA((len(fars),)),
+            pltpu.SemaphoreType.DMA((len(fars), PIECES)),
         ],
         compiler_params=pltpu.CompilerParams(vmem_limit_bytes=30 * 2**20),
         cost_estimate=pl.CostEstimate(flops=3 * 10**9 * len(fars), bytes_accessed=2**20, transcendentals=0),

time: 120 us -> 120 us (level); the launches traced: 118 us -> 119 us
  waiting for transfers between devices: 39.2 us -> 44.2 us
  starting transfers between devices: 42.1 us -> 39.3 us
    ppermute x10, starting transfers between devices: 17.3 us -> 14.9 us  [flip(): return lax.ppermute(v, 'seq', seq_flip(fz, fx))]
    ppermute x10, waiting for transfers between devices: 14.9 us -> 17.3 us  [flip(): return lax.ppermute(v, 'seq', seq_flip(fz, fx))]
    ppermute x14, waiting for transfers between devices: 19.6 us -> 22 us  [zx(): return lax.ppermute(v, 'seq', seq_shift(dz % 4, dx % 4))]
  transfers between devices with their start and end apart: 29 -> 29, of which waited for: 17 -> 17; matrix products, arithmetic and copies ran while one was open for 3% -> 3% of each run, Pallas kernels for 23% -> 22%
where the time goes in v6:
time: 120 us; the launch traced here: 119 us
  waiting for transfers between devices  44.2 us (37%)
  starting transfers between devices  39.3 us (33%)
  Pallas kernels  28.9 us (24%)
  local copies, waits for them, and re-layouts  3.28 us (3%)
  other arithmetic  3 us (2%)
    ppermute x14, waiting for transfers between devices, zx(): return lax.ppermute(v, 'seq', seq_shift(dz % 4, dx % 4))  22 us
    pallas_call x4, Pallas kernels, attend(): pl.pallas_call(functools.partial(attend_kernel, far=far, cut=cut), out_sh...  18.5 us
    ppermute x14, starting transfers between devices, zx(): return lax.ppermute(v, 'seq', seq_shift(dz % 4, dx % 4))  17.5 us
    ppermute x10, waiting for transfers between devices, flip(): return lax.ppermute(v, 'seq', seq_flip(fz, fx))  17.3 us
    ppermute x10, starting transfers between devices, flip(): return lax.ppermute(v, 'seq', seq_flip(fz, fx))  14.9 us
    pallas_call x3, Pallas kernels, project(): pl.pallas_call(functools.partial(project_kernel, fars=fars), out_shape=[j...  8.79 us
    ppermute x5, starting transfers between devices, yc(): return lax.ppermute(v, 'kvh', kvh_shift(dy % 4, dc))  6.89 us
    ppermute x5, waiting for transfers between devices, yc(): return lax.ppermute(v, 'kvh', kvh_shift(dy % 4, dc))  4.94 us
  transfers between devices with their start and end apart: 29, of which 17 were waited for; matrix products, arithmetic and copies ran while one was open for 3% of the time, Pallas kernels for 22%

profile of v6, /device:TPU:0, one launch (start us, length us, event | category | flops | bytes accessed | tf_op | source)
XLA Modules:
  0.0 118.9 jit_solution(3313603868373185253)
XLA Ops:
  0.0 1.0 slice_bitcast_fusion
  1.0 2.1 %collective-permute-start.1 = (bf16[1,64,1024]{2,1,0:T(8,128)(2,1)S(1)}, bf16[1,64,1024]{2,1,0:T(8,128)(2,1)S(1)}, u32[]{:S(2)}, u32[]{:S(2)}) collective-permute-start(bf16[1,64,1024]{2,1,0:T(8,128)(2,1)S(1)} %get-tuple-element.63), channel_id=1, source_target_pairs={{0,32},{8,40},{16,48},{24,56},{32,0},{40,8},{48,16},{56,24},{64,96... | collective-permute-start | bytes 393224 | tf_op jit(solution)/shard_map/ppermute | solution.py:297
  3.1 1.5 %collective-permute-start = (bf16[1,64,1024]{2,1,0:T(8,128)(2,1)S(1)}, bf16[1,64,1024]{2,1,0:T(8,128)(2,1)S(1)}, u32[]{:S(2)}, u32[]{:S(2)}) collective-permute-start(bf16[1,64,1024]{2,1,0:T(8,128)(2,1)S(1)} %get-tuple-element.64), channel_id=1, source_target_pairs={{0,8},{8,0},{16,24},{24,16},{32,40},{40,32},{48,56},{56,48},{64,72... | collective-permute-start | bytes 393224 | tf_op jit(solution)/shard_map/ppermute | solution.py:297
  4.6 0.8 fusion.5
  5.4 1.9 %collective-permute-done.1 = bf16[1,64,1024]{2,1,0:T(8,128)(2,1)S(1)} collective-permute-done((bf16[1,64,1024]{2,1,0:T(8,128)(2,1)S(1)}, bf16[1,64,1024]{2,1,0:T(8,128)(2,1)S(1)}, u32[]{:S(2)}, u32[]{:S(2)}) %collective-permute-start.1) | collective-permute-done | bytes 131104 | tf_op jit(solution)/shard_map/ppermute | solution.py:297
  7.3 1.4 %collective-permute-done = bf16[1,64,1024]{2,1,0:T(8,128)(2,1)S(1)} collective-permute-done((bf16[1,64,1024]{2,1,0:T(8,128)(2,1)S(1)}, bf16[1,64,1024]{2,1,0:T(8,128)(2,1)S(1)}, u32[]{:S(2)}, u32[]{:S(2)}) %collective-permute-start) | collective-permute-done | bytes 131104 | tf_op jit(solution)/shard_map/ppermute | solution.py:297
  8.7 2.8 %collective-permute-start.2 = (bf16[2,64,1024]{2,1,0:T(8,128)(2,1)S(1)}, bf16[2,64,1024]{2,1,0:T(8,128)(2,1)S(1)}, u32[]{:S(2)}, u32[]{:S(2)}) collective-permute-start(bf16[2,64,1024]{2,1,0:T(8,128)(2,1)S(1)} %pad_maximum_fusion.2), channel_id=1, source_target_pairs={{0,24},{8,16},{16,8},{24,0},{32,56},{40,48},{48,40},{56,32},{64,88... | collective-permute-start | bytes 786440 | tf_op jit(solution)/shard_map/ppermute | solution.py:297
  11.6 2.5 %collective-permute-start.3 = (bf16[2,64,1024]{2,1,0:T(8,128)(2,1)S(1)}, bf16[2,64,1024]{2,1,0:T(8,128)(2,1)S(1)}, u32[]{:S(2)}, u32[]{:S(2)}) collective-permute-start(bf16[2,64,1024]{2,1,0:T(8,128)(2,1)S(1)} %pad_maximum_fusion.3), channel_id=1, source_target_pairs={{0,96},{8,104},{16,112},{24,120},{32,64},{40,72},{48,80},{56,88},{... | collective-permute-start | bytes 786440 | tf_op jit(solution)/shard_map/ppermute | solution.py:297
  14.4 3.2 %collective-permute-done.2 = bf16[2,64,1024]{2,1,0:T(8,128)(2,1)S(1)} collective-permute-done((bf16[2,64,1024]{2,1,0:T(8,128)(2,1)S(1)}, bf16[2,64,1024]{2,1,0:T(8,128)(2,1)S(1)}, u32[]{:S(2)}, u32[]{:S(2)}) %collective-permute-start.2) | collective-permute-done | bytes 262176 | tf_op jit(solution)/shard_map/ppermute | solution.py:297
  17.7 2.4 %collective-permute-done.3 = bf16[2,64,1024]{2,1,0:T(8,128)(2,1)S(1)} collective-permute-done((bf16[2,64,1024]{2,1,0:T(8,128)(2,1)S(1)}, bf16[2,64,1024]{2,1,0:T(8,128)(2,1)S(1)}, u32[]{:S(2)}, u32[]{:S(2)}) %collective-permute-start.3) | collective-permute-done | bytes 262176 | tf_op jit(solution)/shard_map/ppermute | solution.py:297
  20.2 0.7 collective-permute-start.4
  21.1 0.6 select_reduce_fusion
  21.8 11.8 %collective-permute-done.4.refs_0_ = bf16[4,64,1024]{2,1,0:T(8,128)(2,1)S(1)} collective-permute-done((bf16[4,64,1024]{2,1,0:T(8,128)(2,1)S(1)}, bf16[4,64,1024]{2,1,0:T(8,128)(2,1)S(1)}, u32[]{:S(2)}, u32[]{:S(2)}) %collective-permute-start.4) | collective-permute-done | bytes 524320 | tf_op jit(solution)/shard_map/ppermute | solution.py:294
  33.6 0.5 collective-permute-done.5.refs_1_
  34.3 2.9 %collective-permute-start.6 = (bf16[4,64,1024]{2,1,0:T(8,128)(2,1)S(1)}, bf16[4,64,1024]{2,1,0:T(8,128)(2,1)S(1)}, u32[]{:S(2)}, u32[]{:S(2)}) collective-permute-start(bf16[4,64,1024]{2,1,0:T(8,128)(2,1)S(1)} %pad_maximum_fusion.refs_0_), channel_id=1, source_target_pairs={{0,96},{8,104},{16,112},{24,120},{32,0},{40,8},{48,16},{56,24},{64... | collective-permute-start | bytes 1572872 | tf_op jit(solution)/shard_map/ppermute | solution.py:294
  37.2 3.0 %collective-permute-start.7 = (bf16[4,64,1024]{2,1,0:T(8,128)(2,1)S(1)}, bf16[4,64,1024]{2,1,0:T(8,128)(2,1)S(1)}, u32[]{:S(2)}, u32[]{:S(2)}) collective-permute-start(bf16[4,64,1024]{2,1,0:T(8,128)(2,1)S(1)} %pad_maximum_fusion.1.refs_1_), channel_id=1, source_target_pairs={{0,24},{8,0},{16,8},{24,16},{32,56},{40,32},{48,40},{56,48},{64,88... | collective-permute-start | bytes 1572872 | tf_op jit(solution)/shard_map/ppermute | solution.py:294
  40.2 2.2 %copy-done.2 = bf16[1,8192,256]{2,1,0:T(8,128)(2,1)S(1)} copy-done((bf16[1,8192,256]{2,1,0:T(8,128)(2,1)S(1)}, bf16[1,8192,256]{2,1,0:T(8,128)(2,1)}, u32[]{:S(2)}) %copy-start.2) | copy-done | bytes 4194328
  42.4 4.5 %attend.5 = (f32[4,144,512]{2,1,0:T(8,128)S(1)}, f32[4,144,512]{2,1,0:T(8,128)S(1)}) custom-call(s32[3]{0:T(128)S(1)} %pad_add_fusion.place_ref, s32[32]{0:T(128)S(1)} %broadcast_add_fusion.count_ref, s32[512]{0:T(512)S(1)} %select_n.44.ids_ref, bf16[8192,256]{1,0:T(8,128)(2,1)S(1)} %bitcast.15, bf16[4,64,1024]{2,1,0:T(8,128)(2,1)S(1)} %collective-permute-done.4.refs_0_, ...), custom_call_target="tpu_custom_call" | custom-call | flops 4000000000 | bytes 1048576 | tf_op jit(solution)/shard_map/attend/pallas_call | solution.py:160
  46.9 4.9 %attend.7 = (bf16[2,144,512]{2,1,0:T(8,128)(2,1)S(1)}, bf16[2,144,512]{2,1,0:T(8,128)(2,1)S(1)}, bf16[2,144,512]{2,1,0:T(8,128)(2,1)S(1)}, bf16[2,144,512]{2,1,0:T(8,128)(2,1)S(1)}) custom-call(s32[3]{0:T(128)S(1)} %pad_add_fusion.place_ref, s32[32]{0:T(128)S(1)} %broadcast_add_fusion.count_ref, s32[512]{0:T(512)S(1)} %select_n.44.ids_ref, ...), custom_call_target="tpu_custom_call" | custom-call | flops 4000000000 | bytes 1048576 | tf_op jit(solution)/shard_map/attend/pallas_call | solution.py:160
  51.8 1.2 %collective-permute-start.10 = (bf16[2,144,512]{2,1,0:T(8,128)(2,1)S(1)}, bf16[2,144,512]{2,1,0:T(8,128)(2,1)S(1)}, u32[]{:S(2)}, u32[]{:S(2)}) collective-permute-start(bf16[2,144,512]{2,1,0:T(8,128)(2,1)S(1)} %get-tuple-element.40), channel_id=1, source_target_pairs={{0,96},{8,104},{16,112},{24,120},{32,0},{40,8},{48,16},{56,24},{64... | collective-permute-start | bytes 884744 | tf_op jit(solution)/shard_map/ppermute | solution.py:294
  53.0 0.9 collective-permute-start.11
  53.9 1.9 %collective-permute-start.12 = (bf16[2,144,512]{2,1,0:T(8,128)(2,1)S(1)}, bf16[2,144,512]{2,1,0:T(8,128)(2,1)S(1)}, u32[]{:S(2)}, u32[]{:S(2)}) collective-permute-start(bf16[2,144,512]{2,1,0:T(8,128)(2,1)S(1)} %get-tuple-element.44), channel_id=1, source_target_pairs={{0,24},{8,0},{16,8},{24,16},{32,56},{40,32},{48,40},{56,48},{64,88... | collective-permute-start | bytes 884744 | tf_op jit(solution)/shard_map/ppermute | solution.py:294
  55.9 4.4 %attend.6 = (f32[4,144,512]{2,1,0:T(8,128)S(1)}, f32[4,144,512]{2,1,0:T(8,128)S(1)}) custom-call(s32[3]{0:T(128)S(1)} %pad_add_fusion.place_ref, s32[32]{0:T(128)S(1)} %broadcast_add_fusion.count_ref, s32[512]{0:T(512)S(1)} %select_n.44.ids_ref, bf16[8192,256]{1,0:T(8,128)(2,1)S(1)} %bitcast.17, bf16[4,64,1024]{2,1,0:T(8,128)(2,1)S(1)} %collective-permute-done.6.refs_0_, ...), custom_call_target="tpu_custom_call" | custom-call | flops 4000000000 | bytes 1048576 | tf_op jit(solution)/shard_map/attend/pallas_call | solution.py:160
  60.4 0.6 collective-permute-done.11.refs_3_
  61.0 2.8 %collective-permute-done.13.refs_7_ = bf16[2,144,512]{2,1,0:T(8,128)(2,1)S(1)} collective-permute-done((bf16[2,144,512]{2,1,0:T(8,128)(2,1)S(1)}, bf16[2,144,512]{2,1,0:T(8,128)(2,1)S(1)}, u32[]{:S(2)}, u32[]{:S(2)}) %collective-permute-start.13) | collective-permute-done | bytes 294944 | tf_op jit(solution)/shard_map/ppermute | solution.py:294
  63.8 0.6 join.1
  64.5 3.2 %collective-permute-start.15 = (bf16[4,144,512]{2,1,0:T(8,128)(2,1)S(1)}, bf16[4,144,512]{2,1,0:T(8,128)(2,1)S(1)}, u32[]{:S(2)}, u32[]{:S(2)}) collective-permute-start(bf16[4,144,512]{2,1,0:T(8,128)(2,1)S(1)} %get-tuple-element.47), channel_id=1, source_target_pairs={{0,96},{8,104},{16,112},{24,120},{32,0},{40,8},{48,16},{56,24},{64... | collective-permute-start | bytes 1769480 | tf_op jit(solution)/shard_map/ppermute | solution.py:294
  67.7 3.2 %collective-permute-start.17 = (bf16[4,144,512]{2,1,0:T(8,128)(2,1)S(1)}, bf16[4,144,512]{2,1,0:T(8,128)(2,1)S(1)}, u32[]{:S(2)}, u32[]{:S(2)}) collective-permute-start(bf16[4,144,512]{2,1,0:T(8,128)(2,1)S(1)} %get-tuple-element.50), channel_id=1, source_target_pairs={{0,24},{8,0},{16,8},{24,16},{32,56},{40,32},{48,40},{56,48},{64,88... | collective-permute-start | bytes 1769480 | tf_op jit(solution)/shard_map/ppermute | solution.py:294
  70.9 4.7 %attend.4 = (f32[4,144,512]{2,1,0:T(8,128)S(1)}, f32[4,144,512]{2,1,0:T(8,128)S(1)}) custom-call(s32[3]{0:T(128)S(1)} %pad_add_fusion.place_ref, s32[32]{0:T(128)S(1)} %broadcast_add_fusion.count_ref, s32[512]{0:T(512)S(1)} %select_n.44.ids_ref, bf16[8192,256]{1,0:T(8,128)(2,1)S(1)} %bitcast.18, bf16[4,64,1024]{2,1,0:T(8,128)(2,1)S(1)} %pad_maximum_fusion.refs_0_, ...), custom_call_target="tpu_custom_call" | custom-call | flops 4000000000 | bytes 1048576 | tf_op jit(solution)/shard_map/attend/pallas_call | solution.py:160
  75.8 6.2 %collective-permute-done.16.refs_4_ = bf16[4,144,512]{2,1,0:T(8,128)(2,1)S(1)} collective-permute-done((bf16[4,144,512]{2,1,0:T(8,128)(2,1)S(1)}, bf16[4,144,512]{2,1,0:T(8,128)(2,1)S(1)}, u32[]{:S(2)}, u32[]{:S(2)}) %collective-permute-start.16) | collective-permute-done | bytes 589856 | tf_op jit(solution)/shard_map/ppermute | solution.py:294
  82.0 0.7 stage.1
  82.7 3.3 %collective-permute-start.19 = (bf16[1,144,512]{2,1,0:T(8,128)(2,1)S(1)}, bf16[1,144,512]{2,1,0:T(8,128)(2,1)S(1)}, u32[]{:S(2)}, u32[]{:S(2)}) collective-permute-start(bf16[1,144,512]{2,1,0:T(8,128)(2,1)S(1)} %get-tuple-element.53), channel_id=1, source_target_pairs={{0,24},{8,16},{16,8},{24,0},{32,56},{40,48},{48,40},{56,32},{64,88... | collective-permute-start | bytes 442376 | tf_op jit(solution)/shard_map/ppermute | solution.py:297
  86.1 1.4 %collective-permute-start.20 = (bf16[1,144,512]{2,1,0:T(8,128)(2,1)S(1)}, bf16[1,144,512]{2,1,0:T(8,128)(2,1)S(1)}, u32[]{:S(2)}, u32[]{:S(2)}) collective-permute-start(bf16[1,144,512]{2,1,0:T(8,128)(2,1)S(1)} %get-tuple-element.54), channel_id=1, source_target_pairs={{0,16},{8,24},{16,0},{24,8},{32,48},{40,56},{48,32},{56,40},{64,80... | collective-permute-start | bytes 442376 | tf_op jit(solution)/shard_map/ppermute | solution.py:297
  87.4 0.4 collective-permute-done.18.refs_1_
  87.9 2.5 %collective-permute-done.19.refs_2_ = bf16[1,144,512]{2,1,0:T(8,128)(2,1)S(1)} collective-permute-done((bf16[1,144,512]{2,1,0:T(8,128)(2,1)S(1)}, bf16[1,144,512]{2,1,0:T(8,128)(2,1)S(1)}, u32[]{:S(2)}, u32[]{:S(2)}) %collective-permute-start.19) | collective-permute-done | bytes 147488 | tf_op jit(solution)/shard_map/ppermute | solution.py:297
  90.3 1.2 %collective-permute-start.23 = (bf16[1,144,512]{2,1,0:T(8,128)(2,1)S(1)}, bf16[1,144,512]{2,1,0:T(8,128)(2,1)S(1)}, u32[]{:S(2)}, u32[]{:S(2)}) collective-permute-start(bf16[1,144,512]{2,1,0:T(8,128)(2,1)S(1)} %get-tuple-element.58), channel_id=1, source_target_pairs={{0,64},{8,72},{16,80},{24,88},{32,96},{40,104},{48,112},{56,120},{... | collective-permute-start | bytes 442376 | tf_op jit(solution)/shard_map/ppermute | solution.py:297
  91.5 1.2 collective-permute-done.20.refs_3_
  92.7 1.5 %collective-permute-done.22.refs_6_ = bf16[1,144,512]{2,1,0:T(8,128)(2,1)S(1)} collective-permute-done((bf16[1,144,512]{2,1,0:T(8,128)(2,1)S(1)}, bf16[1,144,512]{2,1,0:T(8,128)(2,1)S(1)}, u32[]{:S(2)}, u32[]{:S(2)}) %collective-permute-start.22) | collective-permute-done | bytes 147488 | tf_op jit(solution)/shard_map/ppermute | solution.py:297
  94.2 2.8 %collective-permute-done.23.refs_7_ = bf16[1,144,512]{2,1,0:T(8,128)(2,1)S(1)} collective-permute-done((bf16[1,144,512]{2,1,0:T(8,128)(2,1)S(1)}, bf16[1,144,512]{2,1,0:T(8,128)(2,1)S(1)}, u32[]{:S(2)}, u32[]{:S(2)}) %collective-permute-start.23) | collective-permute-done | bytes 147488 | tf_op jit(solution)/shard_map/ppermute | solution.py:297
  97.4 1.5 %collective-permute-done.24.other_ref = bf16[128,1024]{1,0:T(8,128)(2,1)S(1)} collective-permute-done((bf16[128,1024]{1,0:T(8,128)(2,1)S(1)}, bf16[128,1024]{1,0:T(8,128)(2,1)S(1)}, u32[]{:S(2)}, u32[]{:S(2)}) %collective-permute-start.24) | collective-permute-done | bytes 262176 | tf_op jit(solution)/shard_map/ppermute | solution.py:300
  99.0 2.6 %project.5 = bf16[128,1024]{1,0:T(8,128)(2,1)S(1)} custom-call(s32[3]{0:T(128)S(1)} %pad_add_fusion.place_ref, bf16[128,1024]{1,0:T(8,128)(2,1)S(1)} %final.1.att_ref, bf16[128,1024]{1,0:T(8,128)(2,1)S(1)} %collective-permute-done.24.other_ref, bf16[1024,8192]{1,0:T(8,128)(2,1)S(1)} %bitcast.12, bf16[1024,8192]{1,0:T(8,128)(2,1)} %collective-permute-done.25.wo_ref), custom_call_target="tpu_custom_call" | custom-call | flops 3000000000 | bytes 1048576 | tf_op jit(solution)/shard_map/project/pallas_call | solution.py:268
  101.6 3.5 %collective-permute-start.27 = (bf16[128,1024]{1,0:T(8,128)(2,1)S(1)}, bf16[128,1024]{1,0:T(8,128)(2,1)S(1)}, u32[]{:S(2)}, u32[]{:S(2)}) collective-permute-start(bf16[128,1024]{1,0:T(8,128)(2,1)S(1)} %project.5), channel_id=1, source_target_pairs={{0,4},{1,5},{2,6},{3,7},{4,0},{5,1},{6,2},{7,3},{8,12},{9,13},{10,... | collective-permute-start | bytes 786440 | tf_op jit(solution)/shard_map/ppermute | solution.py:300
  105.1 3.6 %project.4 = (bf16[128,1024]{1,0:T(8,128)(2,1)S(1)}, bf16[128,1024]{1,0:T(8,128)(2,1)S(1)}) custom-call(s32[3]{0:T(128)S(1)} %pad_add_fusion.place_ref, bf16[128,1024]{1,0:T(8,128)(2,1)S(1)} %final.1.att_ref, bf16[128,1024]{1,0:T(8,128)(2,1)S(1)} %collective-permute-done.24.other_ref, bf16[1024,8192]{1,0:T(8,128)(2,1)S(1)} %bitcast.13, ...), custom_call_target="tpu_custom_call" | custom-call | flops 6000000000 | bytes 1048576 | tf_op jit(solution)/shard_map/project/pallas_call | solution.py:268
  108.6 0.8 collective-permute-start.26
  109.4 2.5 %collective-permute-start.28 = (bf16[128,1024]{1,0:T(8,128)(2,1)S(1)}, bf16[128,1024]{1,0:T(8,128)(2,1)S(1)}, u32[]{:S(2)}, u32[]{:S(2)}) collective-permute-start(bf16[128,1024]{1,0:T(8,128)(2,1)S(1)} %get-tuple-element.60), channel_id=1, source_target_pairs={{0,6},{1,7},{2,0},{3,1},{4,2},{5,3},{6,4},{7,5},{8,14},{9,15},{10,... | collective-permute-start | bytes 786440 | tf_op jit(solution)/shard_map/ppermute | solution.py:300
  112.0 2.6 %project.3 = f32[128,1024]{1,0:T(8,128)S(1)} custom-call(s32[3]{0:T(128)S(1)} %pad_add_fusion.place_ref, bf16[128,1024]{1,0:T(8,128)(2,1)S(1)} %final.1.att_ref, bf16[128,1024]{1,0:T(8,128)(2,1)S(1)} %collective-permute-done.24.other_ref, bf16[1024,8192]{1,0:T(8,128)(2,1)S(1)} %bitcast.14, bf16[1024,8192]{1,0:T(8,128)(2,1)} %collective-permute-done.25.wo_ref), custom_call_target="tpu_custom_call" | custom-call | flops 3000000000 | bytes 1048576 | tf_op jit(solution)/shard_map/project/pallas_call | solution.py:268
  114.6 3.4 %collective-permute-done.26 = bf16[128,1024]{1,0:T(8,128)(2,1)S(1)} collective-permute-done((bf16[128,1024]{1,0:T(8,128)(2,1)S(1)}, bf16[128,1024]{1,0:T(8,128)(2,1)S(1)}, u32[]{:S(2)}, u32[]{:S(2)}) %collective-permute-start.26) | collective-permute-done | bytes 262176 | tf_op jit(solution)/shard_map/ppermute | solution.py:300
  118.0 0.9 convert_add_fusion
  (55 shorter events, 1.8 us)
Async XLA Ops:
  0.0 98.9 %collective-permute-start.25 = (bf16[1024,8192]{1,0:T(8,128)(2,1)}, bf16[1024,8192]{1,0:T(8,128)(2,1)}, u32[]{:S(2)}, u32[]{:S(2)}) collective-permute-start(bf16[1024,8192]{1,0:T(8,128)(2,1)} %bitcast.9), channel_id=1, source_target_pairs={{0,1},{1,0},{2,3},{3,2},{4,5},{5,4},{6,7},{7,6},{8,9},{9,8},{10,11... | collective-permute-start | bytes 50331656 | tf_op jit(solution)/shard_map/ppermute | solution.py:300
  1.0 6.2 %collective-permute-start.1 = (bf16[1,64,1024]{2,1,0:T(8,128)(2,1)S(1)}, bf16[1,64,1024]{2,1,0:T(8,128)(2,1)S(1)}, u32[]{:S(2)}, u32[]{:S(2)}) collective-permute-start(bf16[1,64,1024]{2,1,0:T(8,128)(2,1)S(1)} %get-tuple-element.63), channel_id=1, source_target_pairs={{0,32},{8,40},{16,48},{24,56},{32,0},{40,8},{48,16},{56,24},{64,96... | collective-permute-start | bytes 393224 | tf_op jit(solution)/shard_map/ppermute | solution.py:297
  3.1 5.6 %collective-permute-start = (bf16[1,64,1024]{2,1,0:T(8,128)(2,1)S(1)}, bf16[1,64,1024]{2,1,0:T(8,128)(2,1)S(1)}, u32[]{:S(2)}, u32[]{:S(2)}) collective-permute-start(bf16[1,64,1024]{2,1,0:T(8,128)(2,1)S(1)} %get-tuple-element.64), channel_id=1, source_target_pairs={{0,8},{8,0},{16,24},{24,16},{32,40},{40,32},{48,56},{56,48},{64,72... | collective-permute-start | bytes 393224 | tf_op jit(solution)/shard_map/ppermute | solution.py:297
  8.7 12.4 %copy-start.3 = (s32[32,64]{1,0:T(8,128)S(1)}, s32[32,64]{1,0:T(8,128)}, u32[]{:S(2)}) copy-start(s32[32,64]{1,0:T(8,128)} %param.6) | copy-start | bytes 24580
  8.7 8.9 %collective-permute-start.2 = (bf16[2,64,1024]{2,1,0:T(8,128)(2,1)S(1)}, bf16[2,64,1024]{2,1,0:T(8,128)(2,1)S(1)}, u32[]{:S(2)}, u32[]{:S(2)}) collective-permute-start(bf16[2,64,1024]{2,1,0:T(8,128)(2,1)S(1)} %pad_maximum_fusion.2), channel_id=1, source_target_pairs={{0,24},{8,16},{16,8},{24,0},{32,56},{40,48},{48,40},{56,32},{64,88... | collective-permute-start | bytes 786440 | tf_op jit(solution)/shard_map/ppermute | solution.py:297
  11.6 8.5 %collective-permute-start.3 = (bf16[2,64,1024]{2,1,0:T(8,128)(2,1)S(1)}, bf16[2,64,1024]{2,1,0:T(8,128)(2,1)S(1)}, u32[]{:S(2)}, u32[]{:S(2)}) collective-permute-start(bf16[2,64,1024]{2,1,0:T(8,128)(2,1)S(1)} %pad_maximum_fusion.3), channel_id=1, source_target_pairs={{0,96},{8,104},{16,112},{24,120},{32,64},{40,72},{48,80},{56,88},{... | collective-permute-start | bytes 786440 | tf_op jit(solution)/shard_map/ppermute | solution.py:297
  20.2 26.7 %copy-start = (bf16[4,64,1024]{2,1,0:T(8,128)(2,1)}, bf16[4,64,1024]{2,1,0:T(8,128)(2,1)S(1)}, u32[]{:S(2)}) copy-start(bf16[4,64,1024]{2,1,0:T(8,128)(2,1)S(1)} %pad_maximum_fusion.1.refs_1_) | copy-start | bytes 1572868
  20.2 13.4 %collective-permute-start.4 = (bf16[4,64,1024]{2,1,0:T(8,128)(2,1)S(1)}, bf16[4,64,1024]{2,1,0:T(8,128)(2,1)S(1)}, u32[]{:S(2)}, u32[]{:S(2)}) collective-permute-start(bf16[4,64,1024]{2,1,0:T(8,128)(2,1)S(1)} %pad_maximum_fusion.refs_0_), channel_id=1, source_target_pairs={{0,32},{8,40},{16,48},{24,56},{32,64},{40,72},{48,80},{56,88},{64,... | collective-permute-start | bytes 1572872 | tf_op jit(solution)/shard_map/ppermute | solution.py:294
  20.9 13.2 %collective-permute-start.5 = (bf16[4,64,1024]{2,1,0:T(8,128)(2,1)S(1)}, bf16[4,64,1024]{2,1,0:T(8,128)(2,1)S(1)}, u32[]{:S(2)}, u32[]{:S(2)}) collective-permute-start(bf16[4,64,1024]{2,1,0:T(8,128)(2,1)S(1)} %pad_maximum_fusion.1.refs_1_), channel_id=1, source_target_pairs={{0,8},{8,16},{16,24},{24,0},{32,40},{40,48},{48,56},{56,32},{64,72... | collective-permute-start | bytes 1572872 | tf_op jit(solution)/shard_map/ppermute | solution.py:294
  33.6 13.3 %collective-permute-start.8 = (bf16[4,64,1024]{2,1,0:T(8,128)(2,1)S(1)}, bf16[4,64,1024]{2,1,0:T(8,128)(2,1)S(1)}, u32[]{:S(2)}, u32[]{:S(2)}) collective-permute-start(bf16[4,64,1024]{2,1,0:T(8,128)(2,1)S(1)} %collective-permute-done.4.refs_0_), channel_id=1, source_target_pairs={{0,32},{8,40},{16,48},{24,56},{32,64},{40,72},{48,80},{56,88},{64,... | collective-permute-start | bytes 1572872 | tf_op jit(solution)/shard_map/ppermute | solution.py:294
  34.1 12.8 %collective-permute-start.9 = (bf16[4,64,1024]{2,1,0:T(8,128)(2,1)S(1)}, bf16[4,64,1024]{2,1,0:T(8,128)(2,1)}, u32[]{:S(2)}, u32[]{:S(2)}) collective-permute-start(bf16[4,64,1024]{2,1,0:T(8,128)(2,1)S(1)} %collective-permute-done.5.refs_1_), channel_id=1, source_target_pairs={{0,8},{8,16},{16,24},{24,0},{32,40},{40,48},{48,56},{56,32},{64,72... | collective-permute-start | bytes 1572872 | tf_op jit(solution)/shard_map/ppermute | solution.py:294
  34.3 19.6 %collective-permute-start.6 = (bf16[4,64,1024]{2,1,0:T(8,128)(2,1)S(1)}, bf16[4,64,1024]{2,1,0:T(8,128)(2,1)S(1)}, u32[]{:S(2)}, u32[]{:S(2)}) collective-permute-start(bf16[4,64,1024]{2,1,0:T(8,128)(2,1)S(1)} %pad_maximum_fusion.refs_0_), channel_id=1, source_target_pairs={{0,96},{8,104},{16,112},{24,120},{32,0},{40,8},{48,16},{56,24},{64... | collective-permute-start | bytes 1572872 | tf_op jit(solution)/shard_map/ppermute | solution.py:294
  37.2 18.6 %collective-permute-start.7 = (bf16[4,64,1024]{2,1,0:T(8,128)(2,1)S(1)}, bf16[4,64,1024]{2,1,0:T(8,128)(2,1)S(1)}, u32[]{:S(2)}, u32[]{:S(2)}) collective-permute-start(bf16[4,64,1024]{2,1,0:T(8,128)(2,1)S(1)} %pad_maximum_fusion.1.refs_1_), channel_id=1, source_target_pairs={{0,24},{8,0},{16,8},{24,16},{32,56},{40,32},{48,40},{56,48},{64,88... | collective-permute-start | bytes 1572872 | tf_op jit(solution)/shard_map/ppermute | solution.py:294
  40.2 2.2 %copy-start.2 = (bf16[1,8192,256]{2,1,0:T(8,128)(2,1)S(1)}, bf16[1,8192,256]{2,1,0:T(8,128)(2,1)}, u32[]{:S(2)}) copy-start(bf16[1,8192,256]{2,1,0:T(8,128)(2,1)} %param.5) | copy-start | bytes 12582916
  51.8 8.6 %collective-permute-start.10 = (bf16[2,144,512]{2,1,0:T(8,128)(2,1)S(1)}, bf16[2,144,512]{2,1,0:T(8,128)(2,1)S(1)}, u32[]{:S(2)}, u32[]{:S(2)}) collective-permute-start(bf16[2,144,512]{2,1,0:T(8,128)(2,1)S(1)} %get-tuple-element.40), channel_id=1, source_target_pairs={{0,96},{8,104},{16,112},{24,120},{32,0},{40,8},{48,16},{56,24},{64... | collective-permute-start | bytes 884744 | tf_op jit(solution)/shard_map/ppermute | solution.py:294
  53.0 7.9 %collective-permute-start.11 = (bf16[2,144,512]{2,1,0:T(8,128)(2,1)S(1)}, bf16[2,144,512]{2,1,0:T(8,128)(2,1)S(1)}, u32[]{:S(2)}, u32[]{:S(2)}) collective-permute-start(bf16[2,144,512]{2,1,0:T(8,128)(2,1)S(1)} %get-tuple-element.41), channel_id=1, source_target_pairs={{0,32},{8,40},{16,48},{24,56},{32,64},{40,72},{48,80},{56,88},{64,... | collective-permute-start | bytes 884744 | tf_op jit(solution)/shard_map/ppermute | solution.py:294
  53.9 7.1 %collective-permute-start.12 = (bf16[2,144,512]{2,1,0:T(8,128)(2,1)S(1)}, bf16[2,144,512]{2,1,0:T(8,128)(2,1)S(1)}, u32[]{:S(2)}, u32[]{:S(2)}) collective-permute-start(bf16[2,144,512]{2,1,0:T(8,128)(2,1)S(1)} %get-tuple-element.44), channel_id=1, source_target_pairs={{0,24},{8,0},{16,8},{24,16},{32,56},{40,32},{48,40},{56,48},{64,88... | collective-permute-start | bytes 884744 | tf_op jit(solution)/shard_map/ppermute | solution.py:294
  55.8 7.9 %collective-permute-start.13 = (bf16[2,144,512]{2,1,0:T(8,128)(2,1)S(1)}, bf16[2,144,512]{2,1,0:T(8,128)(2,1)S(1)}, u32[]{:S(2)}, u32[]{:S(2)}) collective-permute-start(bf16[2,144,512]{2,1,0:T(8,128)(2,1)S(1)} %get-tuple-element.45), channel_id=1, source_target_pairs={{0,8},{8,16},{16,24},{24,0},{32,40},{40,48},{48,56},{56,32},{64,72... | collective-permute-start | bytes 884744 | tf_op jit(solution)/shard_map/ppermute | solution.py:294
  55.9 43.0 %slice-start = ((s8[16777216]{0:T(1024)(128)(4,1)}), s8[4194304]{0:T(1024)(128)(4,1)S(1)}, s32[]{:S(2)}) async-start(s8[16777216]{0:T(1024)(128)(4,1)} %bitcast.10), calls=%async_computation | async-start | bytes 8388608
  55.9 43.0 %slice-start.1 = ((s8[16777216]{0:T(1024)(128)(4,1)}), s8[4194304]{0:T(1024)(128)(4,1)S(1)}, s32[]{:S(2)}) async-start(s8[16777216]{0:T(1024)(128)(4,1)} %bitcast.10), calls=%async_computation.1 | async-start | bytes 8388608
  63.8 7.2 %copy-start.1 = (bf16[4,64,1024]{2,1,0:T(8,128)(2,1)S(1)}, bf16[4,64,1024]{2,1,0:T(8,128)(2,1)}, u32[]{:S(2)}) copy-start(bf16[4,64,1024]{2,1,0:T(8,128)(2,1)} %copy-done) | copy-start | bytes 1572868
  64.4 11.4 %collective-permute-start.14 = (bf16[4,144,512]{2,1,0:T(8,128)(2,1)S(1)}, bf16[4,144,512]{2,1,0:T(8,128)(2,1)S(1)}, u32[]{:S(2)}, u32[]{:S(2)}) collective-permute-start(bf16[4,144,512]{2,1,0:T(8,128)(2,1)S(1)} %get-tuple-element.46), channel_id=1, source_target_pairs={{0,32},{8,40},{16,48},{24,56},{32,64},{40,72},{48,80},{56,88},{64,... | collective-permute-start | bytes 1769480 | tf_op jit(solution)/shard_map/ppermute | solution.py:294
  64.5 11.3 %collective-permute-start.15 = (bf16[4,144,512]{2,1,0:T(8,128)(2,1)S(1)}, bf16[4,144,512]{2,1,0:T(8,128)(2,1)S(1)}, u32[]{:S(2)}, u32[]{:S(2)}) collective-permute-start(bf16[4,144,512]{2,1,0:T(8,128)(2,1)S(1)} %get-tuple-element.47), channel_id=1, source_target_pairs={{0,96},{8,104},{16,112},{24,120},{32,0},{40,8},{48,16},{56,24},{64... | collective-permute-start | bytes 1769480 | tf_op jit(solution)/shard_map/ppermute | solution.py:294
  67.7 14.3 %collective-permute-start.16 = (bf16[4,144,512]{2,1,0:T(8,128)(2,1)S(1)}, bf16[4,144,512]{2,1,0:T(8,128)(2,1)S(1)}, u32[]{:S(2)}, u32[]{:S(2)}) collective-permute-start(bf16[4,144,512]{2,1,0:T(8,128)(2,1)S(1)} %get-tuple-element.49), channel_id=1, source_target_pairs={{0,8},{8,16},{16,24},{24,0},{32,40},{40,48},{48,56},{56,32},{64,72... | collective-permute-start | bytes 1769480 | tf_op jit(solution)/shard_map/ppermute | solution.py:294
  67.7 31.2 %slice-start.2 = ((s8[16777216]{0:T(1024)(128)(4,1)}), s8[4194304]{0:T(1024)(128)(4,1)S(1)}, s32[]{:S(2)}) async-start(s8[16777216]{0:T(1024)(128)(4,1)} %bitcast.10), calls=%async_computation.2 | async-start | bytes 8388608
  67.7 31.2 %slice-start.3 = ((s8[16777216]{0:T(1024)(128)(4,1)}), s8[4194304]{0:T(1024)(128)(4,1)S(1)}, s32[]{:S(2)}) async-start(s8[16777216]{0:T(1024)(128)(4,1)} %bitcast.10), calls=%async_computation.3 | async-start | bytes 8388608
  67.7 14.2 %collective-permute-start.17 = (bf16[4,144,512]{2,1,0:T(8,128)(2,1)S(1)}, bf16[4,144,512]{2,1,0:T(8,128)(2,1)S(1)}, u32[]{:S(2)}, u32[]{:S(2)}) collective-permute-start(bf16[4,144,512]{2,1,0:T(8,128)(2,1)S(1)} %get-tuple-element.50), channel_id=1, source_target_pairs={{0,24},{8,0},{16,8},{24,16},{32,56},{40,32},{48,40},{56,48},{64,88... | collective-permute-start | bytes 1769480 | tf_op jit(solution)/shard_map/ppermute | solution.py:294
  82.7 5.2 %collective-permute-start.18 = (bf16[1,144,512]{2,1,0:T(8,128)(2,1)S(1)}, bf16[1,144,512]{2,1,0:T(8,128)(2,1)S(1)}, u32[]{:S(2)}, u32[]{:S(2)}) collective-permute-start(bf16[1,144,512]{2,1,0:T(8,128)(2,1)S(1)} %get-tuple-element.52), channel_id=1, source_target_pairs={{0,8},{8,0},{16,24},{24,16},{32,40},{40,32},{48,56},{56,48},{64,72... | collective-permute-start | bytes 442376 | tf_op jit(solution)/shard_map/ppermute | solution.py:297
  82.7 7.6 %collective-permute-start.19 = (bf16[1,144,512]{2,1,0:T(8,128)(2,1)S(1)}, bf16[1,144,512]{2,1,0:T(8,128)(2,1)S(1)}, u32[]{:S(2)}, u32[]{:S(2)}) collective-permute-start(bf16[1,144,512]{2,1,0:T(8,128)(2,1)S(1)} %get-tuple-element.53), channel_id=1, source_target_pairs={{0,24},{8,16},{16,8},{24,0},{32,56},{40,48},{48,40},{56,32},{64,88... | collective-permute-start | bytes 442376 | tf_op jit(solution)/shard_map/ppermute | solution.py:297
  86.1 6.6 %collective-permute-start.20 = (bf16[1,144,512]{2,1,0:T(8,128)(2,1)S(1)}, bf16[1,144,512]{2,1,0:T(8,128)(2,1)S(1)}, u32[]{:S(2)}, u32[]{:S(2)}) collective-permute-start(bf16[1,144,512]{2,1,0:T(8,128)(2,1)S(1)} %get-tuple-element.54), channel_id=1, source_target_pairs={{0,16},{8,24},{16,0},{24,8},{32,48},{40,56},{48,32},{56,40},{64,80... | collective-permute-start | bytes 442376 | tf_op jit(solution)/shard_map/ppermute | solution.py:297
  87.4 5.3 %collective-permute-start.21 = (bf16[1,144,512]{2,1,0:T(8,128)(2,1)S(1)}, bf16[1,144,512]{2,1,0:T(8,128)(2,1)S(1)}, u32[]{:S(2)}, u32[]{:S(2)}) collective-permute-start(bf16[1,144,512]{2,1,0:T(8,128)(2,1)S(1)} %get-tuple-element.56), channel_id=1, source_target_pairs={{0,32},{8,40},{16,48},{24,56},{32,0},{40,8},{48,16},{56,24},{64,96... | collective-permute-start | bytes 442376 | tf_op jit(solution)/shard_map/ppermute | solution.py:297
  87.9 6.4 %collective-permute-start.22 = (bf16[1,144,512]{2,1,0:T(8,128)(2,1)S(1)}, bf16[1,144,512]{2,1,0:T(8,128)(2,1)S(1)}, u32[]{:S(2)}, u32[]{:S(2)}) collective-permute-start(bf16[1,144,512]{2,1,0:T(8,128)(2,1)S(1)} %get-tuple-element.57), channel_id=1, source_target_pairs={{0,96},{8,104},{16,112},{24,120},{32,64},{40,72},{48,80},{56,88},{... | collective-permute-start | bytes 442376 | tf_op jit(solution)/shard_map/ppermute | solution.py:297
  90.3 6.6 %collective-permute-start.23 = (bf16[1,144,512]{2,1,0:T(8,128)(2,1)S(1)}, bf16[1,144,512]{2,1,0:T(8,128)(2,1)S(1)}, u32[]{:S(2)}, u32[]{:S(2)}) collective-permute-start(bf16[1,144,512]{2,1,0:T(8,128)(2,1)S(1)} %get-tuple-element.58), channel_id=1, source_target_pairs={{0,64},{8,72},{16,80},{24,88},{32,96},{40,104},{48,112},{56,120},{... | collective-permute-start | bytes 442376 | tf_op jit(solution)/shard_map/ppermute | solution.py:297
  97.3 1.6 %collective-permute-start.24 = (bf16[128,1024]{1,0:T(8,128)(2,1)S(1)}, bf16[128,1024]{1,0:T(8,128)(2,1)S(1)}, u32[]{:S(2)}, u32[]{:S(2)}) collective-permute-start(bf16[128,1024]{1,0:T(8,128)(2,1)S(1)} %final.1.att_ref), channel_id=1, source_target_pairs={{0,1},{1,0},{2,3},{3,2},{4,5},{5,4},{6,7},{7,6},{8,9},{9,8},{10,11... | collective-permute-start | bytes 786440 | tf_op jit(solution)/shard_map/ppermute | solution.py:300
  101.6 13.0 %collective-permute-start.27 = (bf16[128,1024]{1,0:T(8,128)(2,1)S(1)}, bf16[128,1024]{1,0:T(8,128)(2,1)S(1)}, u32[]{:S(2)}, u32[]{:S(2)}) collective-permute-start(bf16[128,1024]{1,0:T(8,128)(2,1)S(1)} %project.5), channel_id=1, source_target_pairs={{0,4},{1,5},{2,6},{3,7},{4,0},{5,1},{6,2},{7,3},{8,12},{9,13},{10,... | collective-permute-start | bytes 786440 | tf_op jit(solution)/shard_map/ppermute | solution.py:300
  108.6 9.3 %collective-permute-start.26 = (bf16[128,1024]{1,0:T(8,128)(2,1)S(1)}, bf16[128,1024]{1,0:T(8,128)(2,1)S(1)}, u32[]{:S(2)}, u32[]{:S(2)}) collective-permute-start(bf16[128,1024]{1,0:T(8,128)(2,1)S(1)} %get-tuple-element.59), channel_id=1, source_target_pairs={{0,2},{1,3},{2,4},{3,5},{4,6},{5,7},{6,0},{7,1},{8,10},{9,11},{10,... | collective-permute-start | bytes 786440 | tf_op jit(solution)/shard_map/ppermute | solution.py:300
  109.4 8.6 %collective-permute-start.28 = (bf16[128,1024]{1,0:T(8,128)(2,1)S(1)}, bf16[128,1024]{1,0:T(8,128)(2,1)S(1)}, u32[]{:S(2)}, u32[]{:S(2)}) collective-permute-start(bf16[128,1024]{1,0:T(8,128)(2,1)S(1)} %get-tuple-element.60), channel_id=1, source_target_pairs={{0,6},{1,7},{2,0},{3,1},{4,2},{5,3},{6,4},{7,5},{8,14},{9,15},{10,... | collective-permute-start | bytes 786440 | tf_op jit(solution)/shard_map/ppermute | solution.py:300
